TPU v7x, 512 devices: a whole 4x4x16 slice. The times are simulated.
512 devices in a mesh: shard: 128 (over z, x, core), rep: 4 (over y).
Axes of the slice: x: 4, y: 4, z: 16, core: 2. Of those that a mesh axis runs over, the one named last changes fastest.
Arguments:
- embeddings: bfloat16 [32768, 4096], P('shard')
- cluster_of: int32 [32768], P('shard'), may hold values from 0 to 127, as said below
Outputs:
- max_similarity: float32 [32768], P('shard')
Inputs may be any that keep to these rules, and one draw needn't show every extreme that they name: `cluster_of`: cluster c is owned by index c // 1 of shard. Of the 256 documents of one index of shard at most 4 lie in clusters of one owner, and one owner takes exactly 4 from every index of shard.
All inputs are finite; a program needn't handle non-finite values.
Results may differ from a plain program's by a relative error of at most 0.0003.
Values may be sent and summed in bfloat16 or wider, within the bound.
No kernel may reach another device: no remote copies, remote signals or barrier semaphores. Data moves between devices by JAX's collectives and lax.ppermute only.
A program may use at most 64 MiB of HBM per device.

v0:
```python
import jax
import jax.numpy as jnp
from jax import lax
from jax.sharding import PartitionSpec as P

CL_OWN = 1


epsilon = 1e-06


def on_device(embeddings, cluster_of):
    shards = lax.axis_size("shard")
    replicas = lax.axis_size("rep")
    doc_count = embeddings.shape[0]
    width = embeddings.shape[1]
    capacity = replicas * max(1, 2 * doc_count // (shards * replicas))
    slot_count = shards * capacity
    owner_doc = cluster_of // CL_OWN
    label_doc = (cluster_of % CL_OWN + 1).astype(jnp.bfloat16)
    doc_index = jnp.arange(doc_count, dtype=jnp.int32)
    earlier = (owner_doc[:, None] == owner_doc[None, :]) & (doc_index[None, :] < doc_index[:, None])
    slot_rank = jnp.sum(earlier.astype(jnp.int32), axis=1)
    slot_id = owner_doc * capacity + slot_rank
    outgoing = (
        jnp.zeros((slot_count, width), jnp.bfloat16)
        .at[slot_id]
        .set(embeddings)
        .reshape(shards, capacity, width)
    )
    slot_tags = (
        jnp.zeros((slot_count,), jnp.bfloat16).at[slot_id].set(label_doc).reshape(shards, capacity)
    )
    rep_index = lax.axis_index("rep")
    row_data, row_tags = (
        lax.all_to_all(outgoing, "shard", split_axis=0, concat_axis=0, tiled=True),
        lax.all_to_all(slot_tags, "shard", split_axis=0, concat_axis=0, tiled=True),
    )
    row_data = row_data.reshape(slot_count, width)
    row_tags = row_tags.reshape(slot_count).astype(jnp.float32)
    inverse = lax.rsqrt(jnp.sum(jnp.square(row_data.astype(jnp.float32)), axis=1) + epsilon)
    block_rows = slot_count // replicas
    best_so_far = jnp.full((slot_count,), -1.0, jnp.float32)
    row_start = rep_index * block_rows
    queries = lax.dynamic_slice_in_dim(row_data, row_start, block_rows, 0)
    products = lax.dot_general(
        queries, row_data, (((1,), (1,)), ((), ())), preferred_element_type=jnp.float32
    )
    query_inv = lax.dynamic_slice_in_dim(inverse, row_start, block_rows, 0)
    query_tags = lax.dynamic_slice_in_dim(row_tags, row_start, block_rows, 0)
    cosine = products * query_inv[:, None] * inverse[None, :]
    query_ids = row_start + jnp.arange(block_rows, dtype=jnp.int32)
    column_ids = jnp.arange(slot_count, dtype=jnp.int32)
    mate_mask = (
        (query_tags[:, None] == row_tags[None, :])
        & (query_tags[:, None] > 0.0)
        & (query_ids[:, None] != column_ids[None, :])
    )
    scored = jnp.where(mate_mask, cosine, jnp.float32(-1.0))
    row_max = jnp.max(scored, axis=1)
    start = rep_index * block_rows
    current = lax.dynamic_slice_in_dim(best_so_far, start, row_max.shape[0], 0)
    best_so_far = lax.dynamic_update_slice_in_dim(
        best_so_far, jnp.maximum(current, row_max), start, 0
    )
    maxima = lax.pmax(best_so_far, "rep")
    returned = lax.all_to_all(
        maxima.reshape(shards, capacity), "shard", split_axis=0, concat_axis=0, tiled=True
    )
    return returned.reshape(-1)[slot_id]


def solution(mesh):
    in_specs = (P("shard", None), P("shard"))
    out_specs = P("shard")
    return jax.shard_map(
        on_device, mesh=mesh, in_specs=in_specs, out_specs=out_specs, check_vma=False
    )
```

profile of v0, /device:TPU:1, one launch (start us, length us, event | category | flops | bytes accessed | tf_op | source)
XLA Modules:
  0.0 305.5 jit_solution(1048247977242377695)
XLA Ops:
  0.0 0.9 convert_reduce_fusion
  0.9 0.7 compare_select_fusion
  1.6 2.2 scatter_custom_fusion
  3.8 0.8 all_to_all.20
  4.6 20.4 %all-to-all-start = ((bf16[128,1,4]{2,1,0:T(2,128)(2,1)}), bf16[128,1,4]{2,1,0:T(2,128)(2,1)S(1)}, u32[]{:S(2)}, u32[]{:S(2)}) async-start(bf16[128,1,4]{2,1,0:T(2,128)(2,1)} %all_to_all.20), calls=%async_computation | async-start | bytes 131072 | tf_op jit(solution)/shard_map/all_to_all | solution.py:37
  25.0 7.1 %scatter_custom_fusion.1 = bf16[512,4096]{1,0:T(8,128)(2,1)} fusion(s32[256]{0:T(256)S(1)} %compare_select_fusion, bf16[256,4096]{1,0:T(8,128)(2,1)} %param.2, bf16[]{:T(256)} %constant.19.clone.1), kind=kCustom, calls=%fused_computation.4 | custom fusion | bytes 4194816 | tf_op jit(solution)/shard_map/scatter | solution.py:28
  32.0 7.2 %reshape.49 = bf16[128,4,4096]{2,1,0:T(4,128)(2,1)} reshape(bf16[512,4096]{1,0:T(8,128)(2,1)} %scatter_custom_fusion.1) | data formatting | bytes 8388608 | tf_op jit(solution)/shard_map/reshape | solution.py:29
  39.2 0.7 all-to-all-done
  39.9 15.9 %all-to-all-start.1 = ((bf16[128,4,4096]{2,1,0:T(4,128)(2,1)}), bf16[128,4,4096]{2,1,0:T(4,128)(2,1)}, u32[]{:S(2)}, u32[]{:S(2)}) async-start(bf16[128,4,4096]{2,1,0:T(4,128)(2,1)} %reshape.49), calls=%async_computation.1 | async-start | bytes 8388608 | tf_op jit(solution)/shard_map/all_to_all | solution.py:36
  55.8 0.2 convert_reduce_fusion.1
  56.0 0.1 reshape.52
  56.1 0.1 broadcast_compare_fusion
  56.2 183.1 %all-to-all-done.1 = bf16[128,4,4096]{2,1,0:T(4,128)(2,1)} async-done(((bf16[128,4,4096]{2,1,0:T(4,128)(2,1)}), bf16[128,4,4096]{2,1,0:T(4,128)(2,1)}, u32[]{:S(2)}, u32[]{:S(2)}) %all-to-all-start.1) | async-done | bytes 4194336 | tf_op jit(solution)/shard_map/all_to_all | solution.py:36
  239.3 4.4 %multiply_reduce_fusion = f32[128,4]{1,0:T(8,128)S(1)} fusion(bf16[128,4,4096]{2,1,0:T(4,128)(2,1)} %all-to-all-done.1), kind=kLoop, calls=%fused_computation.3 | loop fusion | flops 6290944 | bytes 4196352 | tf_op jit(solution)/shard_map/reduce_sum | solution.py:41
  243.8 0.1 rsqrt.11
  243.9 0.1 dynamic_slice.14
  244.0 6.9 %reshape.50 = bf16[512,4096]{1,0:T(8,128)(2,1)} reshape(bf16[128,4,4096]{2,1,0:T(4,128)(2,1)} %all-to-all-done.1) | data formatting | bytes 8388608 | tf_op jit(solution)/shard_map/reshape | solution.py:39
  250.9 4.1 %fusion.4 = f32[128]{0:T(128)S(1)} fusion(bf16[512,4096]{1,0:T(8,128)(2,1)} %reshape.50, s32[]{:T(128)S(6)} %select_n.25, f32[512]{0:T(512)S(1)} %rsqrt.11, f32[128]{0:T(128)S(1)} %dynamic_slice.14, s32[128]{0:T(128)S(1)} %iota_add_fusion, f32[512]{0:T(512)S(1)} %reshape.52, f32[128]{0:T(128)S(1)} %get-tuple-element.6, pred[128]{0:T(512)(128)(4,1)S(1)} %get-tuple-element.5), kind=kOutput, calls=%fused_computation.9 | convolution fusion | flops 537395072 | bytes 5249156 | tf_op jit(solution)/shard_map/dot_general | solution.py:46
  255.0 0.1 maximum_dynamic-update-slice_fusion
  255.1 0.1 all_to_all.18
  255.2 14.6 %pmax.7 = f32[128,1,4]{2,0,1:T(8,128)} all-reduce(f32[128,1,4]{2,0,1:T(8,128)S(1)} %all_to_all.18), channel_id=1, replica_groups=mesh['shard'=128,'rep'=4] {'rep'}, use_global_device_ids=true, to_apply=%region_5.6 | all-reduce | flops 512 | bytes 4096 | tf_op jit(solution)/shard_map/pmax | solution.py:66
  269.9 16.8 %all-to-all-start.2 = ((f32[128,1,4]{2,1,0:T(1,128)}), f32[128,1,4]{2,1,0:T(1,128)S(1)}, u32[]{:S(2)}, u32[]{:S(2)}) async-start(f32[128,1,4]{2,1,0:T(1,128)} %bitcast), calls=%async_computation.2 | async-start | bytes 131072 | tf_op jit(solution)/shard_map/all_to_all | solution.py:67
  286.7 14.8 %all-to-all-done.2 = f32[128,1,4]{2,1,0:T(1,128)S(1)} async-done(((f32[128,1,4]{2,1,0:T(1,128)}), f32[128,1,4]{2,1,0:T(1,128)S(1)}, u32[]{:S(2)}, u32[]{:S(2)}) %all-to-all-start.2) | async-done | bytes 2080 | tf_op jit(solution)/shard_map/all_to_all | solution.py:67
  301.6 0.5 broadcast.58
  302.1 0.8 reduce.8
  302.9 0.1 reshape.51
  303.0 2.5 gather_fusion
  (5 shorter events, 0.0 us)
Async XLA Ops:
  4.6 35.3 %all-to-all-start = ((bf16[128,1,4]{2,1,0:T(2,128)(2,1)}), bf16[128,1,4]{2,1,0:T(2,128)(2,1)S(1)}, u32[]{:S(2)}, u32[]{:S(2)}) async-start(bf16[128,1,4]{2,1,0:T(2,128)(2,1)} %all_to_all.20), calls=%async_computation | async-start | bytes 131072 | tf_op jit(solution)/shard_map/all_to_all | solution.py:37
  39.9 199.4 %all-to-all-start.1 = ((bf16[128,4,4096]{2,1,0:T(4,128)(2,1)}), bf16[128,4,4096]{2,1,0:T(4,128)(2,1)}, u32[]{:S(2)}, u32[]{:S(2)}) async-start(bf16[128,4,4096]{2,1,0:T(4,128)(2,1)} %reshape.49), calls=%async_computation.1 | async-start | bytes 8388608 | tf_op jit(solution)/shard_map/all_to_all | solution.py:36
  269.9 31.7 %all-to-all-start.2 = ((f32[128,1,4]{2,1,0:T(1,128)}), f32[128,1,4]{2,1,0:T(1,128)S(1)}, u32[]{:S(2)}, u32[]{:S(2)}) async-start(f32[128,1,4]{2,1,0:T(1,128)} %bitcast), calls=%async_computation.2 | async-start | bytes 131072 | tf_op jit(solution)/shard_map/all_to_all | solution.py:67
where the time goes:
time: 306 us; the launch traced here: 305 us
  waiting for transfers between devices  199 us (65%)
  starting transfers between devices  53.2 us (17%)
  local copies, waits for them, and re-layouts  27.7 us (9%)
  blocking collectives  14.6 us (5%)
  other arithmetic  7.25 us (2%)
  matrix products  4.13 us (1%)
    all_to_all x1, waiting for transfers between devices, on_device(): lax.all_to_all(outgoing, 'shard', split_axis=0, concat_axis=0, tiled=True)  183 us
    all_to_all x1, starting transfers between devices, on_device(): lax.all_to_all(slot_tags, 'shard', split_axis=0, concat_axis=0, tiled=True)  20.4 us
    all_to_all x1, starting transfers between devices, on_device(): lax.all_to_all(maxima.reshape(shards, capacity), 'shard', split_axis=0, c...  16.8 us
    all_to_all x1, starting transfers between devices, on_device(): lax.all_to_all(outgoing, 'shard', split_axis=0, concat_axis=0, tiled=True)  15.9 us
    all_to_all x1, waiting for transfers between devices, on_device(): lax.all_to_all(maxima.reshape(shards, capacity), 'shard', split_axis=0, c...  14.8 us
    pmax x1, blocking collectives, on_device(): maxima = lax.pmax(best_so_far, 'rep')  14.6 us
    reshape x1, local copies, waits for them, and re-layouts, on_device(): outgoing = jnp.zeros((slot_count, width), jnp.bfloat16).at[slot_id].set(e...  7.2 us
    scatter x1, local copies, waits for them, and re-layouts, on_device(): outgoing = jnp.zeros((slot_count, width), jnp.bfloat16).at[slot_id].set(e...  7.08 us
  transfers between devices with their start and end apart: 3, of which 3 were waited for; matrix products, arithmetic and copies ran while one was open for 5% of the time, Pallas kernels for 0%

commit v1 on v0

v1 whole, which is shorter than its diff:
```python
import jax
import jax.numpy as jnp
import numpy as np
from jax import lax
from jax.experimental import pallas as pl
from jax.experimental.pallas import tpu as pltpu
from jax.sharding import Mesh
from jax.sharding import PartitionSpec as P

SHARDS = 128
PLANES = 16
LANES = 8
REPS = 4
RANKS = 4
DOCS = 256
WIDTH = 1024
HALF = WIDTH // 2
ROWS = SHARDS * RANKS * 2
SLOTS = SHARDS * RANKS
PAIR_ROWS = 168

epsilon = 1e-06
f32 = jnp.float32
bf16 = jnp.bfloat16


def iota(shape, dim):
    return lax.broadcasted_iota(jnp.int32, shape, dim)


def as_column(row, neutral):
    n = row.shape[1]
    eye = iota((n, n), 0) == iota((n, n), 1)
    return jnp.max(jnp.where(eye, jnp.broadcast_to(row, (n, n)), neutral), axis=1, keepdims=True)


def as_row(column, neutral):
    n = column.shape[0]
    eye = iota((n, n), 0) == iota((n, n), 1)
    return jnp.max(jnp.where(eye, jnp.broadcast_to(column, (n, n)), neutral), axis=0, keepdims=True)


def dispatch_kernel(rep_ref, cluster_ref, docs_ref, out_ref, slot_ref):
    cluster = cluster_ref[...].astype(f32)
    column = as_column(cluster, f32(-1.0))
    earlier = (column == cluster) & (iota((DOCS, DOCS), 0) < iota((DOCS, DOCS), 1))
    rank = jnp.sum(jnp.where(earlier, f32(1.0), f32(0.0)), axis=0, keepdims=True)
    slot = cluster_ref[...] * RANKS + rank.astype(jnp.int32)
    slot_ref[...] = slot
    step = 256
    docs = [docs_ref[:, h * HALF : (h + 1) * HALF] for h in range(2)]
    ones = jnp.ones((DOCS, 128), bf16)
    for start in range(0, ROWS, step):
        row = iota((step, DOCS), 0) + start
        chosen = jnp.where((row >> 1) == slot, f32(1.0), f32(0.0)).astype(bf16)
        values = [jnp.dot(chosen, d, preferred_element_type=f32) for d in docs]
        live = jnp.dot(chosen, ones, preferred_element_type=f32) > 0.5
        odd = (iota((step, 128), 0) & 1) == 1
        for part in range(HALF // 128):
            lanes = slice(part * 128, (part + 1) * 128)
            merged = jnp.where(odd, values[1][:, lanes], values[0][:, lanes])
            out_ref[start : start + step, lanes] = jnp.where(live, merged, jnp.nan).astype(bf16)


def gram_kernel(pick_ref, rows_ref, out_ref, gram_ref):
    rows = rows_ref[...].astype(f32)
    empty = rows != rows
    clean = jnp.where(empty, f32(0.0), rows).astype(bf16)
    flags = jnp.where(empty[:, :128], f32(1.0), f32(0.0)).astype(bf16)
    slots = jnp.concatenate(
        [
            jnp.dot(pick_ref[h], clean, preferred_element_type=f32).astype(bf16)
            for h in range(2)
        ],
        axis=1,
    )
    vacant = jnp.dot(pick_ref[0], flags, preferred_element_type=f32)
    gram_ref[...] = lax.dot_general(
        slots, slots, (((1,), (1,)), ((), ())), preferred_element_type=f32
    )

    def block(a, b):
        return gram_ref[a * 128 : (a + 1) * 128, b * 128 : (b + 1) * 128]

    eye = iota((128, 128), 0) == iota((128, 128), 1)
    squares = []
    for k in range(RANKS):
        diagonal = jnp.where(vacant[k * 128 : (k + 1) * 128] > 0.5, jnp.nan, block(k, k))
        squares.append(jnp.sum(jnp.where(eye, diagonal, f32(0.0)), axis=0, keepdims=True))
    for r in range(REPS):
        following = (r + 1) % RANKS
        a, b, half = r % 2, r % 2 + 2, r // 2
        out_ref[r, 0:128, 0:128] = block(r, r)
        out_ref[r, 0:128, 128:256] = block(r, following)
        top = a * 128 + half * 64
        out_ref[r, 128:160, 0:128] = gram_ref[top : top + 32, b * 128 : (b + 1) * 128]
        out_ref[r, 128:160, 128:256] = gram_ref[top + 32 : top + 64, b * 128 : (b + 1) * 128]
        norms = [
            jnp.concatenate([squares[r], squares[following]], axis=1),
            jnp.concatenate([squares[a], squares[b]], axis=1),
            jnp.zeros((6, 256), f32),
        ]
        out_ref[r, 160:168, :] = jnp.concatenate(norms, axis=0)


def best_kernel(rep_ref, parts_ref, out_ref):
    rep = rep_ref[0]
    total = parts_ref[0] + parts_ref[1] + parts_ref[2] + parts_ref[3]
    eye = iota((128, 128), 0) == iota((128, 128), 1)

    def scales(squares):
        live = squares == squares
        return jnp.where(live, lax.rsqrt(squares + epsilon), f32(-1.0))

    def scored(products, column, row):
        cosine = products * column * row
        return jnp.where((column >= 0.0) & (row >= 0.0), cosine, f32(-1.0))

    main = scales(total[160:161, :])
    other = scales(total[161:162, :])
    own, nxt = main[:, 0:128], main[:, 128:256]
    own_column = as_column(own, f32(-2.0))
    same = jnp.where(eye, f32(-1.0), scored(total[0:128, 0:128], own_column, own))
    near = scored(total[0:128, 128:256], own_column, nxt)
    best_own = as_row(
        jnp.maximum(jnp.max(same, axis=1, keepdims=True), jnp.max(near, axis=1, keepdims=True)),
        f32(-1.0),
    )
    best_next = jnp.max(near, axis=0, keepdims=True)
    a_column = as_column(other[:, 0:128], f32(-2.0))
    upper = rep >= 2
    a_column = jnp.where(upper, a_column[64:128], a_column[0:64])
    extra = jnp.concatenate([total[128:160, 0:128], total[128:160, 128:256]], axis=0)
    far = scored(extra, a_column, other[:, 128:256])
    best_b = jnp.max(far, axis=0, keepdims=True)
    rows = jnp.max(far, axis=1, keepdims=True)
    rows = jnp.concatenate([rows, rows], axis=0)
    in_half = (iota((1, 128), 1) >= 64) == upper
    best_a = jnp.where(in_half, as_row(rows, f32(-1.0)), f32(-1.0))
    rank = iota((RANKS, 128), 0)
    low = jnp.full((RANKS, 128), -1.0, f32)
    best = jnp.where(rank == rep, best_own, low)
    best = jnp.maximum(best, jnp.where(rank == (rep + 1) % RANKS, best_next, low))
    best = jnp.maximum(best, jnp.where(rank == rep % 2, best_a, low))
    best = jnp.maximum(best, jnp.where(rank == rep % 2 + 2, best_b, low))
    for target in range(LANES * REPS):
        out_ref[target] = best


def turn_kernel(lane_ref, best_ref, out_ref, turned_ref):
    joined = []
    for lane in range(LANES):
        base = lane * REPS
        joined.append(
            jnp.maximum(
                jnp.maximum(best_ref[base], best_ref[base + 1]),
                jnp.maximum(best_ref[base + 2], best_ref[base + 3]),
            )
        )
    joined.append(jnp.zeros((128 - LANES * RANKS, 128), f32))
    turned_ref[...] = jnp.transpose(jnp.concatenate(joined, axis=0))
    start = pl.multiple_of(lane_ref[0] * PLANES, PLANES)
    out_ref[...] = turned_ref[pl.ds(start, PLANES), :].reshape(PLANES, 1, 128)


def collect_kernel(slot_ref, best_ref, out_ref):
    slot = slot_ref[...]
    best = best_ref[...].reshape(PLANES, 128)
    chosen = jnp.where(iota((128, DOCS), 0) == slot % (LANES * RANKS), f32(1.0), f32(0.0))
    values = jnp.dot(best, chosen, precision=lax.Precision.HIGHEST, preferred_element_type=f32)
    plane = iota((PLANES, DOCS), 0) == slot // (LANES * RANKS)
    out_ref[...] = jnp.sum(jnp.where(plane, values, f32(0.0)), axis=0, keepdims=True)


VMEM = pl.BlockSpec(memory_space=pltpu.VMEM)
SMEM = pl.BlockSpec(memory_space=pltpu.SMEM)
PARAMS = pltpu.CompilerParams(vmem_limit_bytes=40 * 1024 * 1024)


def picks():
    slot = np.arange(SLOTS)
    rank, place = slot // SHARDS, slot % SHARDS
    source = (place % PLANES) * LANES + place // PLANES
    row = source * (2 * RANKS) + rank * 2
    out = [jnp.arange(ROWS)[None, :] == jnp.asarray(row + h, jnp.int32)[:, None] for h in range(2)]
    return jnp.stack(out).astype(bf16)


def on_device(embeddings, cluster_of):
    rep = lax.axis_index("rep").reshape(1)
    lane = (lax.axis_index("x") * 2 + lax.axis_index("core")).reshape(1)
    outgoing, slot = pl.pallas_call(
        dispatch_kernel,
        grid_spec=pltpu.PrefetchScalarGridSpec(
            num_scalar_prefetch=1,
            grid=(1,),
            in_specs=[
                pl.BlockSpec((1, DOCS), lambda i, r: (0, 0)),
                pl.BlockSpec((DOCS, WIDTH), lambda i, r: (0, r[0])),
            ],
            out_specs=[
                pl.BlockSpec((ROWS, HALF), lambda i, r: (0, 0)),
                pl.BlockSpec((1, DOCS), lambda i, r: (0, 0)),
            ],
        ),
        out_shape=[
            jax.ShapeDtypeStruct((ROWS, HALF), bf16),
            jax.ShapeDtypeStruct((1, DOCS), jnp.int32),
        ],
        compiler_params=PARAMS,
        name="dispatch",
    )(rep, cluster_of.reshape(1, DOCS), embeddings)
    rows = lax.all_to_all(
        outgoing.reshape(SHARDS, 2 * RANKS, HALF), ("z", "x", "core"), 0, 0, tiled=True
    ).reshape(ROWS, HALF)
    grams = pl.pallas_call(
        gram_kernel,
        in_specs=[VMEM, VMEM],
        out_specs=VMEM,
        out_shape=jax.ShapeDtypeStruct((REPS, PAIR_ROWS, 256), f32),
        scratch_shapes=[pltpu.VMEM((SLOTS, SLOTS), f32)],
        compiler_params=PARAMS,
        name="gram",
    )(picks(), rows)
    parts = lax.all_to_all(grams, "rep", 0, 0, tiled=True)
    best = pl.pallas_call(
        best_kernel,
        in_specs=[SMEM, VMEM],
        out_specs=VMEM,
        out_shape=jax.ShapeDtypeStruct((LANES * REPS, RANKS, 128), f32),
        compiler_params=PARAMS,
        name="best",
    )(rep, parts)
    best = lax.all_to_all(best, ("x", "core", "rep"), 0, 0, tiled=True)
    turned = pl.pallas_call(
        turn_kernel,
        in_specs=[SMEM, VMEM],
        out_specs=VMEM,
        out_shape=jax.ShapeDtypeStruct((PLANES, 1, 128), f32),
        scratch_shapes=[pltpu.VMEM((128, 128), f32)],
        compiler_params=PARAMS,
        name="turn",
    )(lane, best)
    returned = lax.all_to_all(turned, "z", 0, 0, tiled=True)
    out = pl.pallas_call(
        collect_kernel,
        in_specs=[VMEM, VMEM],
        out_specs=VMEM,
        out_shape=jax.ShapeDtypeStruct((1, DOCS), f32),
        compiler_params=PARAMS,
        name="collect",
    )(slot, returned)
    return out.reshape(DOCS)


def solution(mesh):
    fine = Mesh(mesh.devices.reshape(PLANES, LANES // 2, 2, REPS), ("z", "x", "core", "rep"))
    shard = ("z", "x", "core")
    return jax.shard_map(
        on_device,
        mesh=fine,
        in_specs=(P(shard, None), P(shard)),
        out_specs=P(shard),
        check_vma=False,
    )
```

time: 306 us -> 126 us (0.41)
  waiting for transfers between devices: 199 us -> 57.9 us
  local copies, waits for them, and re-layouts: 27.7 us -> 2.28 us
  starting transfers between devices: 53.2 us -> 31.7 us
  blocking collectives: 14.6 us -> 27.1 us
  other arithmetic: 7.25 us -> 1.14 us
  Pallas kernels: 0 us -> 5.9 us
  matrix products: 4.13 us -> 0 us
    all_to_all x3 -> x2, waiting for transfers between devices: 199 us -> 57.9 us  [the longest x1 50.7 us: on_device(): lax.all_to_all(outgoing.reshape(SHARDS, 2 * RANKS, HALF), ('z', 'x', 'cor...]
    all_to_all x0 -> x2, blocking collectives: none -> 27.1 us  [the longest x1 14.6 us: on_device(): returned = lax.all_to_all(turned, 'z', 0, 0, tiled=True)]
    all_to_all x3 -> x2, starting transfers between devices: 53.2 us -> 31.7 us  [the longest x1 20.4 us: on_device(): lax.all_to_all(outgoing.reshape(SHARDS, 2 * RANKS, HALF), ('z', 'x', 'cor...]
    pmax x1 -> x0, blocking collectives: 14.6 us -> none  [on_device(): maxima = lax.pmax(best_so_far, 'rep')]
    reshape x3 -> x0, local copies, waits for them, and re-layouts: 14.2 us -> none  [the longest x1 7.2 us: on_device(): outgoing = jnp.zeros((slot_count, width), jnp.bfloat16).at[slot_id].set(e...]
    scatter x2 -> x0, local copies, waits for them, and re-layouts: 9.24 us -> none  [the longest x1 7.08 us: on_device(): outgoing = jnp.zeros((slot_count, width), jnp.bfloat16).at[slot_id].set(e...]
    pallas_call x0 -> x5, Pallas kernels: none -> 5.9 us  [the longest x1 2.16 us: on_device(): pl.pallas_call(gram_kernel, in_specs=[VMEM, VMEM], out_specs=VMEM, out_sh...]
    reduce_sum x2 -> x0, other arithmetic: 5.36 us -> none  [the longest x1 4.43 us: on_device(): jnp.sum(jnp.square(row_data.astype(jnp.float32)), axis=1) + epsilon]
  transfers between devices with their start and end apart: 3 -> 2, of which waited for: 3 -> 2; matrix products, arithmetic and copies ran while one was open for 5% -> 1% of each run, Pallas kernels for 0% -> 0%
where the time goes in v1:
time: 126 us
  waiting for transfers between devices  57.9 us (46%)
  starting transfers between devices  31.7 us (25%)
  blocking collectives  27.1 us (22%)
  Pallas kernels  5.9 us (5%)
  local copies, waits for them, and re-layouts  2.28 us (2%)
    all_to_all x1, waiting for transfers between devices, on_device(): lax.all_to_all(outgoing.reshape(SHARDS, 2 * RANKS, HALF), ('z', 'x', 'cor...  50.7 us
    all_to_all x1, starting transfers between devices, on_device(): lax.all_to_all(outgoing.reshape(SHARDS, 2 * RANKS, HALF), ('z', 'x', 'cor...  20.4 us
    all_to_all x1, blocking collectives, on_device(): returned = lax.all_to_all(turned, 'z', 0, 0, tiled=True)  14.6 us
    all_to_all x1, blocking collectives, on_device(): parts = lax.all_to_all(grams, 'rep', 0, 0, tiled=True)  12.5 us
    all_to_all x1, starting transfers between devices, on_device(): best = lax.all_to_all(best, ('x', 'core', 'rep'), 0, 0, tiled=True)  11.3 us
    all_to_all x1, waiting for transfers between devices, on_device(): best = lax.all_to_all(best, ('x', 'core', 'rep'), 0, 0, tiled=True)  7.26 us
  transfers between devices with their start and end apart: 2, of which 2 were waited for; matrix products, arithmetic and copies ran while one was open for 1% of the time, Pallas kernels for 0%

profile of v1, /device:TPU:1, one launch (start us, length us, event | category | flops | bytes accessed | tf_op | source)
XLA Modules:
  0.0 126.1 jit_solution(9176602066774081794)
XLA Ops:
  0.0 0.0 copy-start
  0.0 1.6 %copy-done = bf16[256,4096]{1,0:T(8,128)(2,1)S(1)} copy-done((bf16[256,4096]{1,0:T(8,128)(2,1)S(1)}, bf16[256,4096]{1,0:T(8,128)(2,1)}, u32[]{:S(2)}) %copy-start) | copy-done | bytes 2097176
  1.6 0.0 copy-start.1
  1.6 0.7 copy-done.1
  2.3 0.0 copy-start.2
  2.3 0.0 copy-start.3
  2.3 1.9 %dispatch.1 = (bf16[1024,512]{1,0:T(8,128)(2,1)}, s32[1,256]{1,0:T(1,128)S(1)}) custom-call(s32[1]{0:T(128)} %bitcast.rep_ref, s32[1,256]{1,0:T(1,128)S(1)} %bitcast.7, bf16[256,4096]{1,0:T(8,128)(2,1)S(1)} %copy-done), custom_call_target="tpu_custom_call" | custom-call | tf_op jit(solution)/shard_map/dispatch/pallas_call | solution.py:192
  4.2 20.4 %all-to-all-start = ((bf16[128,8,512]{2,1,0:T(8,128)(2,1)}), bf16[128,8,512]{2,1,0:T(8,128)(2,1)S(1)}, u32[]{:S(2)}, u32[]{:S(2)}) async-start(bf16[128,8,512]{2,1,0:T(8,128)(2,1)} %bitcast.3), calls=%async_computation | async-start | bytes 2097152 | tf_op jit(solution)/shard_map/all_to_all | solution.py:213
  24.6 0.0 copy-done.2
  24.6 0.0 copy-done.3
  24.6 0.7 iota_compare_fusion
  25.3 0.5 add_convert_fusion.pick_ref
  25.8 50.7 %all-to-all-done = bf16[128,8,512]{2,1,0:T(8,128)(2,1)S(1)} async-done(((bf16[128,8,512]{2,1,0:T(8,128)(2,1)}), bf16[128,8,512]{2,1,0:T(8,128)(2,1)S(1)}, u32[]{:S(2)}, u32[]{:S(2)}) %all-to-all-start) | async-done | bytes 1048608 | tf_op jit(solution)/shard_map/all_to_all | solution.py:213
  76.5 2.2 %gram.1 = f32[4,168,256]{2,1,0:T(8,128)S(1)} custom-call(bf16[2,512,1024]{2,1,0:T(8,128)(2,1)S(1)} %add_convert_fusion.pick_ref, bf16[1024,512]{1,0:T(8,128)(2,1)S(1)} %bitcast.6), custom_call_target="tpu_custom_call" | custom-call | tf_op jit(solution)/shard_map/gram/pallas_call | solution.py:216
  78.6 12.5 %all_to_all.20.parts_ref = f32[4,168,256]{2,1,0:T(8,128)S(1)} all-to-all(f32[4,168,256]{2,1,0:T(8,128)S(1)} %gram.1), channel_id=1, replica_groups=mesh['z'=16,'x'=4,'core'=2,'rep'=4] {'rep'}, dimensions={0} | all-to-all | bytes 1376256 | tf_op jit(solution)/shard_map/all_to_all | solution.py:225
  91.1 0.9 best.1
  92.1 11.3 %all-to-all-start.2 = ((f32[32,4,128]{2,1,0:T(4,128)}), f32[32,4,128]{2,1,0:T(4,128)S(1)}, u32[]{:S(2)}, u32[]{:S(2)}) async-start(f32[32,4,128]{2,1,0:T(4,128)} %best.1), calls=%async_computation.2 | async-start | bytes 131072 | tf_op jit(solution)/shard_map/all_to_all | solution.py:234
  103.4 7.3 %all-to-all-done.2.best_ref = f32[32,4,128]{2,1,0:T(4,128)S(1)} async-done(((f32[32,4,128]{2,1,0:T(4,128)}), f32[32,4,128]{2,1,0:T(4,128)S(1)}, u32[]{:S(2)}, u32[]{:S(2)}) %all-to-all-start.2) | async-done | bytes 65568 | tf_op jit(solution)/shard_map/all_to_all | solution.py:234
  110.7 0.1 turn.1
  110.8 14.6 %all_to_all.21.best_ref = f32[16,1,128]{2,1,0:T(1,128)S(1)} all-to-all(f32[16,1,128]{2,1,0:T(1,128)S(1)} %turn.1), channel_id=1, replica_groups=mesh['z'=16,'x'=4,'core'=2,'rep'=4] {'z'}, dimensions={0} | all-to-all | bytes 16384 | tf_op jit(solution)/shard_map/all_to_all | solution.py:244
  125.4 0.8 collect.1
Async XLA Ops:
  0.0 1.6 %copy-start = (bf16[256,4096]{1,0:T(8,128)(2,1)S(1)}, bf16[256,4096]{1,0:T(8,128)(2,1)}, u32[]{:S(2)}) copy-start(bf16[256,4096]{1,0:T(8,128)(2,1)} %docs_ref.1) | copy-start | bytes 6291460
  1.6 0.7 copy-start.1
  2.3 22.4 %copy-start.2 = (s32[512]{0:T(512)S(1)}, s32[512]{0:T(512)}, u32[]{:S(2)}) copy-start(s32[512]{0:T(512)} %constant.18.clone) | copy-start | bytes 6148
  2.3 22.4 %copy-start.3 = (s32[512]{0:T(512)S(1)}, s32[512]{0:T(512)}, u32[]{:S(2)}) copy-start(s32[512]{0:T(512)} %constant.19.clone) | copy-start | bytes 6148
  4.2 72.3 %all-to-all-start = ((bf16[128,8,512]{2,1,0:T(8,128)(2,1)}), bf16[128,8,512]{2,1,0:T(8,128)(2,1)S(1)}, u32[]{:S(2)}, u32[]{:S(2)}) async-start(bf16[128,8,512]{2,1,0:T(8,128)(2,1)} %bitcast.3), calls=%async_computation | async-start | bytes 2097152 | tf_op jit(solution)/shard_map/all_to_all | solution.py:213
  92.1 18.6 %all-to-all-start.2 = ((f32[32,4,128]{2,1,0:T(4,128)}), f32[32,4,128]{2,1,0:T(4,128)S(1)}, u32[]{:S(2)}, u32[]{:S(2)}) async-start(f32[32,4,128]{2,1,0:T(4,128)} %best.1), calls=%async_computation.2 | async-start | bytes 131072 | tf_op jit(solution)/shard_map/all_to_all | solution.py:234

commit v2 on v0

v2 whole, which is shorter than its diff:
```python
import jax
import jax.numpy as jnp
from jax import lax
from jax.experimental import pallas as pl
from jax.experimental.pallas import tpu as pltpu
from jax.sharding import Mesh
from jax.sharding import PartitionSpec as P

SHARDS = 128
PLANES = 16
LANES = 8
PARTS = 4
PAIR = 2
REPS = 4
RANKS = 4
DOCS = 256
WIDTH = 4096
QUARTER = WIDTH // PARTS
HALF = QUARTER // 2
ROWS = SHARDS * RANKS * 2
SLOTS = SHARDS * RANKS
LOCAL = SLOTS // LANES
CHUNK = 256
BLOCK = LOCAL + 8

epsilon = 1e-06
f32 = jnp.float32
bf16 = jnp.bfloat16


def iota(shape, dim):
    return lax.broadcasted_iota(jnp.int32, shape, dim)


def dispatch_kernel(
    rep_ref, cluster_ref, docs_ref, out_ref, slot_ref, labels, docs, staged, label_sem, sems, out_sems
):
    fetch_labels = pltpu.make_async_copy(cluster_ref, labels, label_sem)
    fetch_labels.start()
    fetches = []
    for part in range(PARTS):
        columns = slice(part * QUARTER, (part + 1) * QUARTER)
        fetch = pltpu.make_async_copy(docs_ref.at[:, columns], docs.at[part], sems.at[part])
        fetch.start()
        fetches.append(fetch)
    fetch_labels.wait()
    cluster = labels[...]
    row = jnp.broadcast_to(cluster.astype(f32), (DOCS, DOCS))
    first, second = iota((DOCS, DOCS), 0), iota((DOCS, DOCS), 1)
    column = jnp.max(jnp.where(first == second, row, f32(-1.0)), axis=1, keepdims=True)
    earlier = (column == row) & (first < second)
    rank = jnp.sum(jnp.where(earlier, f32(1.0), f32(0.0)), axis=0, keepdims=True)
    slot = cluster * RANKS + rank.astype(jnp.int32)
    slot_ref[...] = slot
    local = slot - rep_ref[0] * SHARDS
    chosen = jnp.where((first >> 1) == local, f32(1.0), f32(0.0)).astype(bf16)
    live = jnp.dot(chosen, jnp.ones((DOCS, 128), bf16), preferred_element_type=f32) > 0.5
    odd = (iota((DOCS, 128), 0) & 1) == 1
    stores = []
    for part in range(PARTS):
        fetches[part].wait()
        even_rows = jnp.dot(chosen, docs[part, :, :HALF], preferred_element_type=f32)
        odd_rows = jnp.dot(chosen, docs[part, :, HALF:], preferred_element_type=f32)
        for start in range(0, HALF, 128):
            lanes = slice(start, start + 128)
            merged = jnp.where(odd, odd_rows[:, lanes], even_rows[:, lanes])
            if start == 0:
                merged = jnp.where(live, merged, jnp.nan)
            staged[part, :, :, lanes] = merged.astype(bf16).reshape(PLANES, 16, 128)
        store = pltpu.make_async_copy(staged.at[part], out_ref.at[:, part], out_sems.at[part])
        store.start()
        stores.append(store)
    for store in stores:
        store.wait()


def gram_kernel(rows_ref, out_ref, slots_ref, vacant_ref):
    row = iota((CHUNK, CHUNK), 0)
    half, lane, rank, plane = row >> 7, (row >> 4) & 7, (row >> 2) & 3, row & 3
    source = (plane * LANES + lane) * (2 * RANKS) + rank * 2 + half
    pick = jnp.where(iota((CHUNK, CHUNK), 1) == source, f32(1.0), f32(0.0)).astype(bf16)
    for chunk in range(ROWS // CHUNK):
        span = slice(chunk * CHUNK, (chunk + 1) * CHUNK)
        marked = rows_ref[span, :128].astype(f32)
        empty = marked != marked
        clean = jnp.where(empty, f32(0.0), marked).astype(bf16)
        flags = jnp.where(empty, f32(1.0), f32(0.0)).astype(bf16)
        rows = jnp.concatenate([clean, rows_ref[span, 128:]], axis=1)
        picked = jnp.dot(pick, rows, preferred_element_type=f32).astype(bf16)
        vacant = jnp.dot(pick[: CHUNK // 2], flags, preferred_element_type=f32)
        for lane in range(LANES):
            at = slice(lane * LOCAL + chunk * 16, lane * LOCAL + (chunk + 1) * 16)
            slots_ref[at, :HALF] = picked[lane * 16 : (lane + 1) * 16]
            slots_ref[at, HALF:] = picked[128 + lane * 16 : 128 + (lane + 1) * 16]
            vacant_ref[at, :] = vacant[lane * 16 : (lane + 1) * 16]
    slots = slots_ref[...]
    eye = iota((128, 128), 0) == iota((128, 128), 1)
    squares = []
    for b in range(SLOTS // 128):
        span = slice(b * 128, (b + 1) * 128)
        products = lax.dot_general(
            slots[span], slots, (((1,), (1,)), ((), ())), preferred_element_type=f32
        )
        diagonal = jnp.where(eye & (vacant_ref[span, :] > 0.5), jnp.nan, products[:, span])
        squares.append(jnp.sum(jnp.where(eye, diagonal, f32(0.0)), axis=0, keepdims=True))
        for half in range(2):
            rows = slice(half * LOCAL, (half + 1) * LOCAL)
            out_ref[2 * b + half, :LOCAL, :] = products[rows]
            out_ref[2 * b + half, :LOCAL, span] = diagonal[rows]
    norms = jnp.broadcast_to(jnp.concatenate(squares, axis=1), (8, SLOTS))
    for lane in range(LANES):
        out_ref[lane, LOCAL:, :] = norms


def best_kernel(lane_ref, parts_ref, out_ref):
    row, column = iota((LOCAL, SLOTS), 0), iota((LOCAL, SLOTS), 1)
    same = column == row + lane_ref[0] * LOCAL
    spot = iota((LOCAL, 128), 1)
    rank = (iota((LOCAL, 128), 0) >> 2) & 3
    spread = jnp.zeros((LOCAL, 128), f32)

    def scale(squares):
        return jnp.where(squares == squares, lax.rsqrt(squares + epsilon), f32(-1.0))

    for cluster in range(PAIR):
        total = parts_ref[cluster]
        for part in range(1, PARTS):
            total = total + parts_ref[part * PAIR + cluster]
        products = total[:LOCAL]
        own = scale(jnp.sum(jnp.where(same, products, f32(0.0)), axis=1, keepdims=True))
        mate = scale(total[LOCAL : LOCAL + 1])
        cosine = products * own * mate
        mates = (own >= 0.0) & (mate >= 0.0) & jnp.logical_not(same)
        best = jnp.max(jnp.where(mates, cosine, f32(-1.0)), axis=1, keepdims=True)
        spread = jnp.where(spot == cluster * RANKS + rank, best, spread)
    planes = []
    for chunk in range(4):
        both = spread[chunk * 16 : chunk * 16 + 8] + spread[chunk * 16 + 8 : chunk * 16 + 16]
        planes.append(both[0:4] + both[4:8])
    turned = jnp.concatenate(planes, axis=0).reshape(PLANES, 1, 128)
    for rep in range(REPS):
        out_ref[rep * PLANES : (rep + 1) * PLANES] = turned


def collect_kernel(slot_ref, best_ref, out_ref):
    slot = slot_ref[...]
    best = best_ref[...].reshape(REPS * PLANES, 128)
    chosen = jnp.where(iota((128, DOCS), 0) == slot % (PAIR * RANKS), f32(1.0), f32(0.0))
    values = jnp.dot(best, chosen, precision=lax.Precision.HIGHEST, preferred_element_type=f32)
    line = iota((REPS * PLANES, DOCS), 0) == slot // (PAIR * RANKS)
    out_ref[...] = jnp.sum(jnp.where(line, values, f32(0.0)), axis=0, keepdims=True)


VMEM = pl.BlockSpec(memory_space=pltpu.VMEM)
SMEM = pl.BlockSpec(memory_space=pltpu.SMEM)
HBM = pl.BlockSpec(memory_space=pltpu.HBM)
WIDE = pltpu.CompilerParams(vmem_limit_bytes=60 * 1024 * 1024)
PARAMS = pltpu.CompilerParams(vmem_limit_bytes=32 * 1024 * 1024)


def on_device(embeddings, cluster_of):
    rep = lax.axis_index("rep").reshape(1)
    lane = (lax.axis_index("x") * 2 + lax.axis_index("core")).reshape(1)
    outgoing, slot = pl.pallas_call(
        dispatch_kernel,
        in_specs=[SMEM, HBM, HBM],
        out_specs=[HBM, VMEM],
        out_shape=[
            jax.ShapeDtypeStruct((PLANES, PARTS, 16, HALF), bf16),
            jax.ShapeDtypeStruct((1, DOCS), jnp.int32),
        ],
        scratch_shapes=[
            pltpu.VMEM((1, DOCS), jnp.int32),
            pltpu.VMEM((PARTS, DOCS, QUARTER), bf16),
            pltpu.VMEM((PARTS, PLANES, 16, HALF), bf16),
            pltpu.SemaphoreType.DMA,
            pltpu.SemaphoreType.DMA((PARTS,)),
            pltpu.SemaphoreType.DMA((PARTS,)),
        ],
        compiler_params=WIDE,
        name="dispatch",
    )(rep, cluster_of.reshape(1, DOCS), embeddings)
    rows = lax.all_to_all(
        outgoing.reshape(SHARDS, 2 * RANKS, HALF), ("z", "x", "core"), 0, 0, tiled=True
    ).reshape(ROWS, HALF)
    products = pl.pallas_call(
        gram_kernel,
        in_specs=[VMEM],
        out_specs=VMEM,
        out_shape=jax.ShapeDtypeStruct((LANES, BLOCK, SLOTS), f32),
        scratch_shapes=[pltpu.VMEM((SLOTS, QUARTER), bf16), pltpu.VMEM((SLOTS, 128), f32)],
        compiler_params=PARAMS,
        name="gram",
    )(rows)
    products = lax.all_to_all(products, ("x", "core"), 0, 0, tiled=True)
    best = pl.pallas_call(
        best_kernel,
        in_specs=[SMEM, VMEM],
        out_specs=VMEM,
        out_shape=jax.ShapeDtypeStruct((REPS * PLANES, 1, 128), f32),
        compiler_params=PARAMS,
        name="best",
    )(lane, products)
    returned = lax.all_to_all(best, ("rep", "z"), 0, 0, tiled=True)
    out = pl.pallas_call(
        collect_kernel,
        in_specs=[VMEM, VMEM],
        out_specs=VMEM,
        out_shape=jax.ShapeDtypeStruct((1, DOCS), f32),
        compiler_params=PARAMS,
        name="collect",
    )(slot, returned)
    return out.reshape(DOCS)


def solution(mesh):
    fine = Mesh(mesh.devices.reshape(PLANES, PARTS, PAIR, REPS), ("z", "x", "core", "rep"))
    shard = ("z", "x", "core")
    return jax.shard_map(
        on_device,
        mesh=fine,
        in_specs=(P(shard, None), P(shard)),
        out_specs=P(shard),
        check_vma=False,
    )
```

time: 306 us -> 125 us (0.41)
  waiting for transfers between devices: 199 us -> 16.5 us
  blocking collectives: 14.6 us -> 93.4 us
  starting transfers between devices: 53.2 us -> 7.29 us
  local copies, waits for them, and re-layouts: 27.7 us -> 0.01 us
  Pallas kernels: 0 us -> 7.86 us
  other arithmetic: 7.25 us -> 0 us
  matrix products: 4.13 us -> 0 us
    all_to_all x3 -> x1, waiting for transfers between devices: 199 us -> 16.5 us  [on_device(): products = lax.all_to_all(products, ('x', 'core'), 0, 0, tiled=True)]
    all_to_all x0 -> x2, blocking collectives: none -> 93.4 us  [the longest x1 72.3 us: on_device(): lax.all_to_all(outgoing.reshape(SHARDS, 2 * RANKS, HALF), ('z', 'x', 'cor...]
    all_to_all x3 -> x1, starting transfers between devices: 53.2 us -> 7.29 us  [on_device(): products = lax.all_to_all(products, ('x', 'core'), 0, 0, tiled=True)]
    pmax x1 -> x0, blocking collectives: 14.6 us -> none  [on_device(): maxima = lax.pmax(best_so_far, 'rep')]
    reshape x3 -> x0, local copies, waits for them, and re-layouts: 14.2 us -> none  [the longest x1 7.2 us: on_device(): outgoing = jnp.zeros((slot_count, width), jnp.bfloat16).at[slot_id].set(e...]
    scatter x2 -> x0, local copies, waits for them, and re-layouts: 9.24 us -> none  [the longest x1 7.08 us: on_device(): outgoing = jnp.zeros((slot_count, width), jnp.bfloat16).at[slot_id].set(e...]
    pallas_call x0 -> x4, Pallas kernels: none -> 7.86 us  [the longest x1 4.02 us: on_device(): pl.pallas_call(dispatch_kernel, in_specs=[SMEM, HBM, HBM], out_specs=[HBM...]
    reduce_sum x2 -> x0, other arithmetic: 5.36 us -> none  [the longest x1 4.43 us: on_device(): jnp.sum(jnp.square(row_data.astype(jnp.float32)), axis=1) + epsilon]
  transfers between devices with their start and end apart: 3 -> 1, of which waited for: 3 -> 1; matrix products, arithmetic and copies ran while one was open for 5% -> 0% of each run, Pallas kernels for 0% -> 0%
where the time goes in v2:
time: 125 us
  blocking collectives  93.4 us (75%)
  waiting for transfers between devices  16.5 us (13%)
  Pallas kernels  7.86 us (6%)
  starting transfers between devices  7.29 us (6%)
    all_to_all x1, blocking collectives, on_device(): lax.all_to_all(outgoing.reshape(SHARDS, 2 * RANKS, HALF), ('z', 'x', 'cor...  72.3 us
    all_to_all x1, blocking collectives, on_device(): returned = lax.all_to_all(best, ('rep', 'z'), 0, 0, tiled=True)  21.2 us
    all_to_all x1, waiting for transfers between devices, on_device(): products = lax.all_to_all(products, ('x', 'core'), 0, 0, tiled=True)  16.5 us
    all_to_all x1, starting transfers between devices, on_device(): products = lax.all_to_all(products, ('x', 'core'), 0, 0, tiled=True)  7.29 us
    pallas_call x1, Pallas kernels, on_device(): pl.pallas_call(dispatch_kernel, in_specs=[SMEM, HBM, HBM], out_specs=[HBM...  4.02 us
    pallas_call x1, Pallas kernels, on_device(): pl.pallas_call(gram_kernel, in_specs=[VMEM], out_specs=VMEM, out_shape=ja...  2.79 us
  transfers between devices with their start and end apart: 1, of which 1 were waited for; matrix products, arithmetic and copies ran while one was open for 0% of the time, Pallas kernels for 0%

profile of v2, /device:TPU:1, one launch (start us, length us, event | category | flops | bytes accessed | tf_op | source)
XLA Modules:
  0.0 125.1 jit_solution(12569084146913465531)
XLA Ops:
  0.0 4.0 %dispatch.1 = (bf16[16,4,16,512]{3,2,1,0:T(8,128)(2,1)}, s32[1,256]{1,0:T(1,128)}) custom-call(s32[1]{0:T(128)} %bitcast.rep_ref, s32[1,256]{1,0:T(1,128)} %bitcast.8, bf16[256,4096]{1,0:T(8,128)(2,1)} %docs_ref.1), custom_call_target="tpu_custom_call" | custom-call | tf_op jit(solution)/shard_map/dispatch/pallas_call | solution.py:164
  4.0 72.3 %all_to_all.15 = bf16[128,8,512]{2,1,0:T(8,128)(2,1)S(1)} all-to-all(bf16[128,8,512]{2,1,0:T(8,128)(2,1)} %bitcast.7), channel_id=1, replica_groups=mesh['z'=16,'x'=4,'core'=2,'rep'=4] {'z','x','core'}, dimensions={0} | all-to-all | bytes 2097152 | tf_op jit(solution)/shard_map/all_to_all | solution.py:183
  76.3 2.8 %gram.1 = f32[8,72,512]{2,1,0:T(8,128)} custom-call(bf16[1024,512]{1,0:T(8,128)(2,1)S(1)} %bitcast.6), custom_call_target="tpu_custom_call" | custom-call | tf_op jit(solution)/shard_map/gram/pallas_call | solution.py:186
  79.1 7.3 %all-to-all-start.1 = ((f32[8,72,512]{2,1,0:T(8,128)}), f32[8,72,512]{2,1,0:T(8,128)S(1)}, u32[]{:S(2)}, u32[]{:S(2)}) async-start(f32[8,72,512]{2,1,0:T(8,128)} %gram.1), calls=%async_computation.1 | async-start | bytes 2359296 | tf_op jit(solution)/shard_map/all_to_all | solution.py:195
  86.4 0.0 copy-start
  86.4 16.5 %all-to-all-done.1.parts_ref = f32[8,72,512]{2,1,0:T(8,128)S(1)} async-done(((f32[8,72,512]{2,1,0:T(8,128)}), f32[8,72,512]{2,1,0:T(8,128)S(1)}, u32[]{:S(2)}, u32[]{:S(2)}) %all-to-all-start.1) | async-done | bytes 1179680 | tf_op jit(solution)/shard_map/all_to_all | solution.py:195
  102.9 0.3 best.1
  103.1 21.2 %all_to_all.16.best_ref = f32[64,1,128]{2,1,0:T(1,128)S(1)} all-to-all(f32[64,1,128]{2,1,0:T(1,128)S(1)} %best.1), channel_id=1, replica_groups=mesh['z'=16,'x'=4,'core'=2,'rep'=4] {'rep','z'}, dimensions={0} | all-to-all | bytes 65536 | tf_op jit(solution)/shard_map/all_to_all | solution.py:204
  124.3 0.0 copy-done
  124.3 0.8 collect.1
Async XLA Ops:
  79.1 23.8 %all-to-all-start.1 = ((f32[8,72,512]{2,1,0:T(8,128)}), f32[8,72,512]{2,1,0:T(8,128)S(1)}, u32[]{:S(2)}, u32[]{:S(2)}) async-start(f32[8,72,512]{2,1,0:T(8,128)} %gram.1), calls=%async_computation.1 | async-start | bytes 2359296 | tf_op jit(solution)/shard_map/all_to_all | solution.py:195
  86.4 37.9 %copy-start = (s32[1,256]{1,0:T(1,128)S(1)}, s32[1,256]{1,0:T(1,128)}, u32[]{:S(2)}) copy-start(s32[1,256]{1,0:T(1,128)} %get-tuple-element.7.slot_ref) | copy-start | bytes 3076

commit v3 on v2

v3 whole, which is shorter than its diff:
```python
import jax
import jax.numpy as jnp
from jax import lax
from jax.experimental import pallas as pl
from jax.experimental.pallas import tpu as pltpu
from jax.sharding import Mesh
from jax.sharding import PartitionSpec as P

PLANES = 16
LANES = 4
PARTS = 2
PAIR = 2
REPS = 4
RANKS = 4
DOCS = 256
WIDTH = 4096
SHARE = WIDTH // PARTS
HALF = SHARE // 2
SOURCES = PLANES * LANES
SLOTS = SOURCES * RANKS
ROWS = SLOTS * 2
CHUNK = 256
LOCAL = SLOTS // LANES
BLOCK = LOCAL + 8

epsilon = 1e-06
f32 = jnp.float32
bf16 = jnp.bfloat16


def iota(shape, dim):
    return lax.broadcasted_iota(jnp.int32, shape, dim)


def dispatch_kernel(rep_ref, cluster_ref, docs_ref, out_ref, slot_ref, docs, sems):
    fetches = []
    for part in range(PARTS):
        columns = slice(part * SHARE, (part + 1) * SHARE)
        fetch = pltpu.make_async_copy(docs_ref.at[:, columns], docs.at[part], sems.at[part])
        fetch.start()
        fetches.append(fetch)
    cluster = cluster_ref[...]
    row = jnp.broadcast_to(cluster.astype(f32), (DOCS, DOCS))
    first, second = iota((DOCS, DOCS), 0), iota((DOCS, DOCS), 1)
    column = jnp.max(jnp.where(first == second, row, f32(-1.0)), axis=1, keepdims=True)
    earlier = (column == row) & (first < second)
    rank = jnp.sum(jnp.where(earlier, f32(1.0), f32(0.0)), axis=0, keepdims=True)
    slot = cluster * RANKS + rank.astype(jnp.int32)
    slot_ref[...] = slot
    local = slot - rep_ref[0] * (PLANES * PAIR * RANKS)
    chosen = jnp.where((first >> 1) == local, f32(1.0), f32(0.0)).astype(bf16)
    live = jnp.dot(chosen, jnp.ones((DOCS, 128), bf16), preferred_element_type=f32) > 0.5
    odd = (iota((DOCS, 128), 0) & 1) == 1
    for part in range(PARTS):
        fetches[part].wait()
        for start in range(0, HALF, 256):
            here = slice(start, start + 256)
            there = slice(HALF + start, HALF + start + 256)
            even_rows = jnp.dot(chosen, docs[part, :, here], preferred_element_type=f32)
            odd_rows = jnp.dot(chosen, docs[part, :, there], preferred_element_type=f32)
            for step in range(0, 256, 128):
                lanes = slice(step, step + 128)
                merged = jnp.where(odd, odd_rows[:, lanes], even_rows[:, lanes])
                if start + step == 0:
                    merged = jnp.where(live, merged, jnp.nan)
                target = slice(start + step, start + step + 128)
                out_ref[:, part, :, target] = merged.astype(bf16).reshape(PLANES, 16, 128)


def gram_kernel(own_ref, other_ref, out_ref, slots_ref, vacant_ref):
    row = iota((CHUNK, CHUNK), 0)
    half, lane, rank, plane = row >> 7, (row >> 5) & 3, (row >> 3) & 3, row & 7
    source = (plane * LANES + lane) * (2 * RANKS) + rank * 2 + half
    pick = jnp.where(iota((CHUNK, CHUNK), 1) == source, f32(1.0), f32(0.0)).astype(bf16)
    for side, rows_ref in enumerate((own_ref, other_ref)):
        for chunk in range(ROWS // CHUNK):
            span = slice(chunk * CHUNK, (chunk + 1) * CHUNK)
            marked = rows_ref[span, :128].astype(f32)
            empty = marked != marked
            clean = jnp.where(empty, f32(0.0), marked).astype(bf16)
            flags = jnp.where(empty, f32(1.0), f32(0.0)).astype(bf16)
            rows = jnp.concatenate([clean, rows_ref[span, 128:]], axis=1)
            picked = jnp.dot(pick, rows, preferred_element_type=f32).astype(bf16)
            vacant = jnp.dot(pick[: CHUNK // 2], flags, preferred_element_type=f32)
            for lane in range(LANES):
                top = side * SLOTS + lane * LOCAL + chunk * 32
                slots_ref[top : top + 32, :HALF] = picked[lane * 32 : (lane + 1) * 32]
                slots_ref[top : top + 32, HALF:] = picked[128 + lane * 32 : 128 + (lane + 1) * 32]
                vacant_ref[top : top + 32, :] = vacant[lane * 32 : (lane + 1) * 32]

    def multiply(left, right):
        return lax.dot_general(left, right, (((1,), (1,)), ((), ())), preferred_element_type=f32)

    def flagged(block, span):
        return jnp.where(eye & (vacant_ref[span, :] > 0.5), jnp.nan, block)

    def diagonal(block):
        return jnp.sum(jnp.where(eye, block, f32(0.0)), axis=0, keepdims=True)

    eye = iota((128, 128), 0) == iota((128, 128), 1)
    squares = []
    for b in range(SLOTS // 128):
        span = slice(b * 128, (b + 1) * 128)
        products = multiply(slots_ref[span, :], slots_ref[...])
        block = flagged(products[:, span], span)
        squares.append(diagonal(block))
        for half in range(2):
            rows = slice(half * LOCAL, (half + 1) * LOCAL)
            out_ref[2 * b + half, :LOCAL, :] = products[rows]
            out_ref[2 * b + half, :LOCAL, span] = block[rows]
    for b in range(SLOTS // 128, 2 * SLOTS // 128):
        span = slice(b * 128, (b + 1) * 128)
        others = slots_ref[span, :]
        squares.append(diagonal(flagged(multiply(others, others), span)))
    norms = jnp.broadcast_to(jnp.concatenate(squares, axis=1), (8, 2 * SLOTS))
    for lane in range(LANES):
        out_ref[lane, LOCAL:, :] = norms


def best_kernel(lane_ref, parts_ref, out_ref):
    row, column = iota((LOCAL, 2 * SLOTS), 0), iota((LOCAL, 2 * SLOTS), 1)
    same = column == row + lane_ref[0] * LOCAL
    spot = iota((LOCAL, 128), 1)
    rank = (iota((LOCAL, 128), 0) >> 3) & 3
    spread = jnp.zeros((LOCAL, 128), f32)

    def scale(squares):
        return jnp.where(squares == squares, lax.rsqrt(squares + epsilon), f32(-1.0))

    for cluster in range(PAIR):
        total = parts_ref[cluster] + parts_ref[PAIR + cluster]
        products = total[:LOCAL]
        own = scale(jnp.sum(jnp.where(same, products, f32(0.0)), axis=1, keepdims=True))
        mate = scale(total[LOCAL : LOCAL + 1])
        cosine = products * own * mate
        mates = (own >= 0.0) & (mate >= 0.0) & jnp.logical_not(same)
        best = jnp.max(jnp.where(mates, cosine, f32(-1.0)), axis=1, keepdims=True)
        spread = jnp.where(spot == cluster * RANKS + rank, best, spread)
    planes = []
    for top in range(0, LOCAL, 32):
        tiles = [spread[top + k * 8 : top + (k + 1) * 8] for k in range(RANKS)]
        planes.append((tiles[0] + tiles[1]) + (tiles[2] + tiles[3]))
    turned = jnp.concatenate(planes, axis=0).reshape(PLANES, 1, 128)
    for rep in range(REPS):
        out_ref[rep * PLANES : (rep + 1) * PLANES] = turned


def collect_kernel(slot_ref, best_ref, out_ref):
    slot = slot_ref[...]
    best = best_ref[...].reshape(REPS * PLANES, 128)
    chosen = jnp.where(iota((128, DOCS), 0) == slot % (PAIR * RANKS), f32(1.0), f32(0.0))
    values = jnp.dot(best, chosen, precision=lax.Precision.HIGHEST, preferred_element_type=f32)
    line = iota((REPS * PLANES, DOCS), 0) == slot // (PAIR * RANKS)
    out_ref[...] = jnp.sum(jnp.where(line, values, f32(0.0)), axis=0, keepdims=True)


VMEM = pl.BlockSpec(memory_space=pltpu.VMEM)
SMEM = pl.BlockSpec(memory_space=pltpu.SMEM)
HBM = pl.BlockSpec(memory_space=pltpu.HBM)
WIDE = pltpu.CompilerParams(vmem_limit_bytes=52 * 1024 * 1024)
PARAMS = pltpu.CompilerParams(vmem_limit_bytes=32 * 1024 * 1024)


def on_device(embeddings, cluster_of):
    rep = lax.axis_index("rep").reshape(1)
    lane = lax.axis_index("x").reshape(1)
    outgoing, slot = pl.pallas_call(
        dispatch_kernel,
        in_specs=[SMEM, VMEM, HBM],
        out_specs=[VMEM, VMEM],
        out_shape=[
            jax.ShapeDtypeStruct((PLANES, PARTS, 16, HALF), bf16),
            jax.ShapeDtypeStruct((1, DOCS), jnp.int32),
        ],
        scratch_shapes=[
            pltpu.VMEM((PARTS, DOCS, SHARE), bf16),
            pltpu.SemaphoreType.DMA((PARTS,)),
        ],
        compiler_params=WIDE,
        name="dispatch",
    )(rep, cluster_of.reshape(1, DOCS), embeddings)
    own = lax.all_to_all(
        outgoing.reshape(SOURCES, 2 * RANKS, HALF), ("z", "x"), 0, 0, tiled=True
    ).reshape(ROWS, HALF)
    other = lax.ppermute(own, "core", [(0, 1), (1, 0)])
    products = pl.pallas_call(
        gram_kernel,
        in_specs=[VMEM, VMEM],
        out_specs=VMEM,
        out_shape=jax.ShapeDtypeStruct((LANES, BLOCK, 2 * SLOTS), f32),
        scratch_shapes=[pltpu.VMEM((2 * SLOTS, SHARE), bf16), pltpu.VMEM((2 * SLOTS, 128), f32)],
        compiler_params=PARAMS,
        name="gram",
    )(own, other)
    products = lax.all_to_all(products, "x", 0, 0, tiled=True)
    best = pl.pallas_call(
        best_kernel,
        in_specs=[SMEM, VMEM],
        out_specs=VMEM,
        out_shape=jax.ShapeDtypeStruct((REPS * PLANES, 1, 128), f32),
        compiler_params=PARAMS,
        name="best",
    )(lane, products)
    returned = lax.all_to_all(best, ("rep", "z"), 0, 0, tiled=True)
    out = pl.pallas_call(
        collect_kernel,
        in_specs=[VMEM, VMEM],
        out_specs=VMEM,
        out_shape=jax.ShapeDtypeStruct((1, DOCS), f32),
        compiler_params=PARAMS,
        name="collect",
    )(slot, returned)
    return out.reshape(DOCS)


def solution(mesh):
    fine = Mesh(mesh.devices.reshape(PLANES, LANES, 2, REPS), ("z", "x", "core", "rep"))
    shard = ("z", "x", "core")
    return jax.shard_map(
        on_device,
        mesh=fine,
        in_specs=(P(shard, None), P(shard)),
        out_specs=P(shard),
        check_vma=False,
    )
```

time: 125 us -> 120 us (0.960)
  waiting for transfers between devices: 16.5 us -> 11.9 us
  starting transfers between devices: 7.29 us -> 10.7 us
  blocking collectives: 93.4 us -> 90.1 us
  Pallas kernels: 7.86 us -> 6.54 us
    all_to_all x1, waiting for transfers between devices: 16.5 us -> 9.62 us  [on_device(): products = lax.all_to_all(products, 'x', 0, 0, tiled=True)]
    ppermute x0 -> x1, starting transfers between devices: none -> 6.7 us  [on_device(): other = lax.ppermute(own, 'core', [(0, 1), (1, 0)])]
    all_to_all x1, starting transfers between devices: 7.29 us -> 3.97 us  [on_device(): products = lax.all_to_all(products, 'x', 0, 0, tiled=True)]
    ppermute x0 -> x1, waiting for transfers between devices: none -> 2.26 us  [on_device(): other = lax.ppermute(own, 'core', [(0, 1), (1, 0)])]
    all_to_all x1, blocking collectives: 72.3 us -> 70.4 us  [on_device(): lax.all_to_all(outgoing.reshape(SOURCES, 2 * RANKS, HALF), ('z', 'x'), 0,...]
    all_to_all x1, blocking collectives: 21.2 us -> 19.8 us  [on_device(): returned = lax.all_to_all(best, ('rep', 'z'), 0, 0, tiled=True)]
    pallas_call x2, Pallas kernels: 6.81 us -> 5.5 us  [the longest x1 3.24 us: on_device(): pl.pallas_call(gram_kernel, in_specs=[VMEM, VMEM], out_specs=VMEM, out_sh...]
  transfers between devices with their start and end apart: 1 -> 2, of which waited for: 1 -> 2; matrix products, arithmetic and copies ran while one was open for 0% -> 0% of each run, Pallas kernels for 0% -> 0%
where the time goes in v3:
time: 120 us
  blocking collectives  90.1 us (75%)
  waiting for transfers between devices  11.9 us (10%)
  starting transfers between devices  10.7 us (9%)
  Pallas kernels  6.54 us (5%)
    all_to_all x1, blocking collectives, on_device(): lax.all_to_all(outgoing.reshape(SOURCES, 2 * RANKS, HALF), ('z', 'x'), 0,...  70.4 us
    all_to_all x1, blocking collectives, on_device(): returned = lax.all_to_all(best, ('rep', 'z'), 0, 0, tiled=True)  19.8 us
    all_to_all x1, waiting for transfers between devices, on_device(): products = lax.all_to_all(products, 'x', 0, 0, tiled=True)  9.62 us
    ppermute x1, starting transfers between devices, on_device(): other = lax.ppermute(own, 'core', [(0, 1), (1, 0)])  6.7 us
    all_to_all x1, starting transfers between devices, on_device(): products = lax.all_to_all(products, 'x', 0, 0, tiled=True)  3.97 us
    pallas_call x1, Pallas kernels, on_device(): pl.pallas_call(gram_kernel, in_specs=[VMEM, VMEM], out_specs=VMEM, out_sh...  3.24 us
  transfers between devices with their start and end apart: 2, of which 2 were waited for; matrix products, arithmetic and copies ran while one was open for 0% of the time, Pallas kernels for 0%

profile of v3, /device:TPU:1, one launch (start us, length us, event | category | flops | bytes accessed | tf_op | source)
XLA Modules:
  0.0 119.9 jit_solution(7001286293983948548)
XLA Ops:
  0.0 0.0 copy-start
  0.0 0.7 copy-done
  0.7 2.3 %dispatch.1 = (bf16[16,2,16,1024]{3,2,1,0:T(8,128)(2,1)S(1)}, s32[1,256]{1,0:T(1,128)S(1)}) custom-call(s32[1]{0:T(128)} %bitcast.rep_ref, s32[1,256]{1,0:T(1,128)S(1)} %bitcast.9, bf16[256,4096]{1,0:T(8,128)(2,1)} %docs_ref.1), custom_call_target="tpu_custom_call" | custom-call | tf_op jit(solution)/shard_map/dispatch/pallas_call | solution.py:167
  2.9 70.4 %all_to_all.15 = bf16[64,8,1024]{2,1,0:T(8,128)(2,1)S(1)} all-to-all(bf16[64,8,1024]{2,1,0:T(8,128)(2,1)S(1)} %bitcast.8), channel_id=1, replica_groups=mesh['z'=16,'x'=4,'core'=2,'rep'=4] {'z','x'}, dimensions={0} | all-to-all | bytes 2097152 | tf_op jit(solution)/shard_map/all_to_all | solution.py:182
  73.3 6.7 %collective-permute-start = (bf16[512,1024]{1,0:T(8,128)(2,1)S(1)}, bf16[512,1024]{1,0:T(8,128)(2,1)S(1)}, u32[]{:S(2)}, u32[]{:S(2)}) collective-permute-start(bf16[512,1024]{1,0:T(8,128)(2,1)S(1)} %bitcast.6), channel_id=1, source_target_pairs={{0,4},{4,0},{1,5},{5,1},{2,6},{6,2},{3,7},{7,3},{8,12},{12,8},{9,1... | collective-permute-start | bytes 3145736 | tf_op jit(solution)/shard_map/ppermute | solution.py:185
  80.0 2.3 %collective-permute-done.other_ref = bf16[512,1024]{1,0:T(8,128)(2,1)S(1)} collective-permute-done((bf16[512,1024]{1,0:T(8,128)(2,1)S(1)}, bf16[512,1024]{1,0:T(8,128)(2,1)S(1)}, u32[]{:S(2)}, u32[]{:S(2)}) %collective-permute-start) | collective-permute-done | bytes 1048608 | tf_op jit(solution)/shard_map/ppermute | solution.py:185
  82.3 3.2 %gram.1 = f32[4,72,512]{2,1,0:T(8,128)} custom-call(bf16[512,1024]{1,0:T(8,128)(2,1)S(1)} %bitcast.7, bf16[512,1024]{1,0:T(8,128)(2,1)S(1)} %collective-permute-done.other_ref), custom_call_target="tpu_custom_call" | custom-call | tf_op jit(solution)/shard_map/gram/pallas_call | solution.py:186
  85.5 4.0 %all-to-all-start.1 = ((f32[4,72,512]{2,1,0:T(8,128)}), f32[4,72,512]{2,1,0:T(8,128)S(1)}, u32[]{:S(2)}, u32[]{:S(2)}) async-start(f32[4,72,512]{2,1,0:T(8,128)} %gram.1), calls=%async_computation.1 | async-start | bytes 1179648 | tf_op jit(solution)/shard_map/all_to_all | solution.py:195
  89.5 9.6 %all-to-all-done.1.parts_ref = f32[4,72,512]{2,1,0:T(8,128)S(1)} async-done(((f32[4,72,512]{2,1,0:T(8,128)}), f32[4,72,512]{2,1,0:T(8,128)S(1)}, u32[]{:S(2)}, u32[]{:S(2)}) %all-to-all-start.1) | async-done | bytes 589856 | tf_op jit(solution)/shard_map/all_to_all | solution.py:195
  99.1 0.3 best.1
  99.4 19.8 %all_to_all.16.best_ref = f32[64,1,128]{2,1,0:T(1,128)S(1)} all-to-all(f32[64,1,128]{2,1,0:T(1,128)S(1)} %best.1), channel_id=1, replica_groups=mesh['z'=16,'x'=4,'core'=2,'rep'=4] {'rep','z'}, dimensions={0} | all-to-all | bytes 65536 | tf_op jit(solution)/shard_map/all_to_all | solution.py:204
  119.1 0.8 collect.1
Async XLA Ops:
  0.0 0.7 copy-start
  73.3 9.0 %collective-permute-start = (bf16[512,1024]{1,0:T(8,128)(2,1)S(1)}, bf16[512,1024]{1,0:T(8,128)(2,1)S(1)}, u32[]{:S(2)}, u32[]{:S(2)}) collective-permute-start(bf16[512,1024]{1,0:T(8,128)(2,1)S(1)} %bitcast.6), channel_id=1, source_target_pairs={{0,4},{4,0},{1,5},{5,1},{2,6},{6,2},{3,7},{7,3},{8,12},{12,8},{9,1... | collective-permute-start | bytes 3145736 | tf_op jit(solution)/shard_map/ppermute | solution.py:185
  85.5 13.6 %all-to-all-start.1 = ((f32[4,72,512]{2,1,0:T(8,128)}), f32[4,72,512]{2,1,0:T(8,128)S(1)}, u32[]{:S(2)}, u32[]{:S(2)}) async-start(f32[4,72,512]{2,1,0:T(8,128)} %gram.1), calls=%async_computation.1 | async-start | bytes 1179648 | tf_op jit(solution)/shard_map/all_to_all | solution.py:195

commit v4 on v3

v4 whole, which is shorter than its diff:
```python
import jax
import jax.numpy as jnp
from jax import lax
from jax.experimental import pallas as pl
from jax.experimental.pallas import tpu as pltpu
from jax.sharding import Mesh
from jax.sharding import PartitionSpec as P

PLANES = 16
LANES = 4
PARTS = 2
PAIR = 2
REPS = 4
RANKS = 4
DOCS = 256
WIDTH = 4096
SHARE = WIDTH // PARTS
HALF = SHARE // 2
SOURCES = PLANES * LANES
SLOTS = SOURCES * RANKS
ROWS = SLOTS * 2
CHUNK = 256
LOCAL = SLOTS // LANES
BLOCK = 4 * LOCAL + 8
STRIP = HALF // 2
STEPS = PARTS * 2

epsilon = 1e-06
f32 = jnp.float32
bf16 = jnp.bfloat16


def iota(shape, dim):
    return lax.broadcasted_iota(jnp.int32, shape, dim)


def dispatch_kernel(
    rep_ref, cluster_ref, docs_ref, out_ref, slot_ref, labels, docs, label_sem, sems
):
    fetch_labels = pltpu.make_async_copy(cluster_ref, labels, label_sem)
    fetch_labels.start()
    fetches = []
    for step in range(STEPS):
        fetches.append([])
        for half in range(2):
            at = (step // 2) * SHARE + half * HALF + (step % 2) * STRIP
            fetch = pltpu.make_async_copy(
                docs_ref.at[:, at : at + STRIP],
                docs.at[step, half * DOCS : (half + 1) * DOCS, :],
                sems.at[step, half],
            )
            fetch.start()
            fetches[step].append(fetch)
    fetch_labels.wait()
    cluster = labels[...]
    row = jnp.broadcast_to(cluster.astype(f32), (DOCS, DOCS))
    first, second = iota((DOCS, DOCS), 0), iota((DOCS, DOCS), 1)
    column = jnp.max(jnp.where(first == second, row, f32(-1.0)), axis=1, keepdims=True)
    earlier = (column == row) & (first < second)
    rank = jnp.sum(jnp.where(earlier, f32(1.0), f32(0.0)), axis=0, keepdims=True)
    slot = cluster * RANKS + rank.astype(jnp.int32)
    slot_ref[...] = slot
    local = slot - rep_ref[0] * (PLANES * PAIR * RANKS)
    hit = (first >> 1) == local
    odd = (first & 1) == 1
    zero, one = f32(0.0), f32(1.0)
    chosen = jnp.concatenate(
        [
            jnp.where(hit & jnp.logical_not(odd), one, zero).astype(bf16),
            jnp.where(hit & odd, one, zero).astype(bf16),
        ],
        axis=1,
    )
    live = jnp.dot(chosen, jnp.ones((2 * DOCS, 128), bf16), preferred_element_type=f32) > 0.5
    for step in range(STEPS):
        for fetch in fetches[step]:
            fetch.wait()
        merged = jnp.dot(chosen, docs[step], preferred_element_type=f32)
        at = (step % 2) * STRIP
        if at == 0:
            marked = jnp.where(live, merged[:, :128], jnp.nan)
            merged = jnp.concatenate([marked, merged[:, 128:]], axis=1)
        out_ref[:, step // 2, :, at : at + STRIP] = merged.astype(bf16).reshape(PLANES, 16, STRIP)


def multiply(left, right):
    return lax.dot_general(left, right, (((1,), (1,)), ((), ())), preferred_element_type=f32)


def gather_slots(rows_ref, slots_ref, vacant_ref):
    row = iota((CHUNK, CHUNK), 0)
    half, lane, rank, plane = row >> 7, (row >> 5) & 3, (row >> 3) & 3, row & 7
    source = (plane * LANES + lane) * (2 * RANKS) + rank * 2 + half
    pick = jnp.where(iota((CHUNK, CHUNK), 1) == source, f32(1.0), f32(0.0)).astype(bf16)
    for chunk in range(ROWS // CHUNK):
        span = slice(chunk * CHUNK, (chunk + 1) * CHUNK)
        marked = rows_ref[span, :128].astype(f32)
        empty = marked != marked
        clean = jnp.where(empty, f32(0.0), marked).astype(bf16)
        flags = jnp.where(empty, f32(1.0), f32(0.0)).astype(bf16)
        rows = jnp.concatenate([clean, rows_ref[span, 128:], flags], axis=1)
        picked = jnp.dot(pick, rows, preferred_element_type=f32)
        slots = picked[:, :HALF].astype(bf16)
        for lane in range(LANES):
            top = lane * LOCAL + chunk * 32
            slots_ref[top : top + 32, :HALF] = slots[lane * 32 : (lane + 1) * 32]
            slots_ref[top : top + 32, HALF:] = slots[128 + lane * 32 : 128 + (lane + 1) * 32]
            vacant_ref[top : top + 32, :] = picked[lane * 32 : (lane + 1) * 32, HALF:]


def flagged_block(block, vacant):
    eye = iota((128, 128), 0) == iota((128, 128), 1)
    flagged = jnp.where(eye & (vacant > 0.5), jnp.nan, block)
    return flagged, jnp.sum(jnp.where(eye, flagged, f32(0.0)), axis=0, keepdims=True)


def own_kernel(rows_ref, out_ref, slots_ref, vacant_ref):
    gather_slots(rows_ref, slots_ref, vacant_ref)
    slots = slots_ref[...]
    products = multiply(slots, slots)
    for b in range(2):
        span = slice(b * 128, (b + 1) * 128)
        block, squares = flagged_block(products[span, span], vacant_ref[span, :])
        for lane in range(LANES):
            rows = slice(lane * LOCAL, (lane + 1) * LOCAL)
            inside = slice((lane % 2) * LOCAL, (lane % 2 + 1) * LOCAL)
            tile = block[inside] if lane // 2 == b else products[rows, span]
            out_ref[lane, b * LOCAL : (b + 1) * LOCAL, :] = tile
            out_ref[lane, 4 * LOCAL + b : 4 * LOCAL + b + 1, :] = squares


def cross_kernel(part_ref, slots_ref, rows_ref, out_ref, other_ref, vacant_ref):
    gather_slots(rows_ref, other_ref, vacant_ref)
    products = multiply(slots_ref[...], other_ref[...])
    for lane in range(LANES):
        rows = slice(lane * LOCAL, (lane + 1) * LOCAL)
        out_ref[lane, : 2 * LOCAL, :] = part_ref[lane, : 2 * LOCAL, :]
        out_ref[lane, 2 * LOCAL : 3 * LOCAL, :] = products[rows, :128]
        out_ref[lane, 3 * LOCAL : 4 * LOCAL, :] = products[rows, 128:]
    for b in range(2):
        span = slice(b * 128, (b + 1) * 128)
        others = other_ref[span, :]
        squares = flagged_block(multiply(others, others), vacant_ref[span, :])[1]
        for lane in range(LANES):
            out_ref[lane, 4 * LOCAL + 2 + b : 4 * LOCAL + 3 + b, :] = squares
    for lane in range(LANES):
        own_norms = slice(4 * LOCAL, 4 * LOCAL + 2)
        out_ref[lane, own_norms, :] = part_ref[lane, own_norms, :]
        out_ref[lane, 4 * LOCAL + 4 :, :] = jnp.zeros((4, 128), f32)


def best_kernel(lane_ref, parts_ref, out_ref):
    row, column = iota((LOCAL, 128), 0), iota((LOCAL, 128), 1)
    spot = column & 7
    rank = (row >> 3) & 3
    spread = jnp.zeros((LOCAL, 128), f32)

    def scale(squares):
        return jnp.where(squares == squares, lax.rsqrt(squares + epsilon), f32(-1.0))

    for cluster in range(PAIR):
        total = parts_ref[cluster] + parts_ref[PAIR + cluster]
        tiles = [total[t * LOCAL : (t + 1) * LOCAL] for t in range(4)]
        mates = [scale(total[4 * LOCAL + t : 4 * LOCAL + t + 1]) for t in range(4)]
        same = [column + t * 128 == row + lane_ref[0] * LOCAL for t in range(2)]
        squares = jnp.where(same[0], tiles[0], f32(0.0)) + jnp.where(same[1], tiles[1], f32(0.0))
        own = scale(jnp.sum(squares, axis=1, keepdims=True))
        best = jnp.full((LOCAL, 128), -1.0, f32)
        for t in range(4):
            cosine = tiles[t] * own * mates[t]
            allowed = (own >= 0.0) & (mates[t] >= 0.0)
            if t < 2:
                allowed = allowed & jnp.logical_not(same[t])
            best = jnp.maximum(best, jnp.where(allowed, cosine, f32(-1.0)))
        best = jnp.max(best, axis=1, keepdims=True)
        spread = jnp.where(spot == cluster * RANKS + rank, best, spread)
    planes = []
    for top in range(0, LOCAL, 32):
        tiles = [spread[top + k * 8 : top + (k + 1) * 8] for k in range(RANKS)]
        planes.append((tiles[0] + tiles[1]) + (tiles[2] + tiles[3]))
    turned = jnp.concatenate(planes, axis=0)
    for rep in range(REPS):
        out_ref[rep * PLANES : (rep + 1) * PLANES, :] = turned


def collect_kernel(slot_ref, best_ref, out_ref):
    slot = slot_ref[...]
    best = best_ref[...]
    high = best.astype(bf16).astype(f32)
    middle = (best - high).astype(bf16).astype(f32)
    low = best - high - middle
    group = iota((REPS * PLANES, 128), 1) >> 3
    pieces = jnp.where(group == 0, high, jnp.where(group == 1, middle, low))
    pieces = jnp.where(group < 3, pieces, f32(0.0)).astype(bf16)
    chosen = (iota((128, DOCS), 0) & 7) == (slot & 7)
    chosen = jnp.where(chosen, f32(1.0), f32(0.0)).astype(bf16)
    values = jnp.dot(pieces, chosen, preferred_element_type=f32)
    line = iota((REPS * PLANES, DOCS), 0) == (slot >> 3)
    out_ref[...] = jnp.sum(jnp.where(line, values, f32(0.0)), axis=0, keepdims=True)


VMEM = pl.BlockSpec(memory_space=pltpu.VMEM)
SMEM = pl.BlockSpec(memory_space=pltpu.SMEM)
HBM = pl.BlockSpec(memory_space=pltpu.HBM)
WIDE = pltpu.CompilerParams(vmem_limit_bytes=52 * 1024 * 1024)
PARAMS = pltpu.CompilerParams(vmem_limit_bytes=32 * 1024 * 1024)


def on_device(embeddings, cluster_of):
    rep = lax.axis_index("rep").reshape(1)
    lane = lax.axis_index("x").reshape(1)
    outgoing, slot = pl.pallas_call(
        dispatch_kernel,
        in_specs=[SMEM, HBM, HBM],
        out_specs=[VMEM, VMEM],
        out_shape=[
            jax.ShapeDtypeStruct((PLANES, PARTS, 16, HALF), bf16),
            jax.ShapeDtypeStruct((1, DOCS), jnp.int32),
        ],
        scratch_shapes=[
            pltpu.VMEM((1, DOCS), jnp.int32),
            pltpu.VMEM((STEPS, 2 * DOCS, STRIP), bf16),
            pltpu.SemaphoreType.DMA,
            pltpu.SemaphoreType.DMA((STEPS, 2)),
        ],
        compiler_params=WIDE,
        name="dispatch",
    )(rep, cluster_of.reshape(1, DOCS), embeddings)
    own_rows = lax.all_to_all(
        outgoing.reshape(SOURCES, 2 * RANKS, HALF), ("z", "x"), 0, 0, tiled=True
    ).reshape(ROWS, HALF)
    other_rows = lax.ppermute(own_rows, "core", [(0, 1), (1, 0)])
    part, slots = pl.pallas_call(
        own_kernel,
        in_specs=[VMEM],
        out_specs=[VMEM, VMEM],
        out_shape=[
            jax.ShapeDtypeStruct((LANES, BLOCK, 128), f32),
            jax.ShapeDtypeStruct((SLOTS, SHARE), bf16),
        ],
        scratch_shapes=[pltpu.VMEM((SLOTS, 128), f32)],
        compiler_params=PARAMS,
        cost_estimate=pl.CostEstimate(
            flops=2 * SLOTS * SLOTS * SHARE * 2, bytes_accessed=2**22, transcendentals=0
        ),
        name="own",
    )(own_rows)
    products = pl.pallas_call(
        cross_kernel,
        in_specs=[VMEM, VMEM, VMEM],
        out_specs=VMEM,
        out_shape=jax.ShapeDtypeStruct((LANES, BLOCK, 128), f32),
        scratch_shapes=[pltpu.VMEM((SLOTS, SHARE), bf16), pltpu.VMEM((SLOTS, 128), f32)],
        compiler_params=PARAMS,
        name="cross",
    )(part, slots, other_rows)
    products = lax.all_to_all(products, "x", 0, 0, tiled=True)
    best = pl.pallas_call(
        best_kernel,
        in_specs=[SMEM, VMEM],
        out_specs=VMEM,
        out_shape=jax.ShapeDtypeStruct((REPS * PLANES, 128), f32),
        compiler_params=PARAMS,
        name="best",
    )(lane, products)
    returned = lax.all_to_all(
        best.reshape(REPS * PLANES, 1, 128), ("rep", "z"), 0, 0, tiled=True
    ).reshape(REPS * PLANES, 128)
    out = pl.pallas_call(
        collect_kernel,
        in_specs=[VMEM, VMEM],
        out_specs=VMEM,
        out_shape=jax.ShapeDtypeStruct((1, DOCS), f32),
        compiler_params=PARAMS,
        name="collect",
    )(slot, returned)
    return out.reshape(DOCS)


def solution(mesh):
    fine = Mesh(mesh.devices.reshape(PLANES, LANES, 2, REPS), ("z", "x", "core", "rep"))
    shard = ("z", "x", "core")
    return jax.shard_map(
        on_device,
        mesh=fine,
        in_specs=(P(shard, None), P(shard)),
        out_specs=P(shard),
        check_vma=False,
    )
```

time: 120 us -> 118 us (0.983)
  waiting for transfers between devices: 11.9 us -> 10.2 us
    pallas_call x2 -> x3, Pallas kernels: 5.5 us -> 5.33 us  [the longest x1 2.33 us: on_device(): pl.pallas_call(dispatch_kernel, in_specs=[SMEM, HBM, HBM], out_specs=[VME...]
  transfers between devices with their start and end apart: 2 -> 2, of which waited for: 2 -> 2; matrix products, arithmetic and copies ran while one was open for 0% -> 0% of each run, Pallas kernels for 0% -> 1%
where the time goes in v4:
time: 118 us
  blocking collectives  90.1 us (76%)
  starting transfers between devices  10.7 us (9%)
  waiting for transfers between devices  10.2 us (9%)
  Pallas kernels  6.29 us (5%)
    all_to_all x1, blocking collectives, on_device(): lax.all_to_all(outgoing.reshape(SOURCES, 2 * RANKS, HALF), ('z', 'x'), 0,...  70.3 us
    all_to_all x1, blocking collectives, on_device(): lax.all_to_all(best.reshape(REPS * PLANES, 1, 128), ('rep', 'z'), 0, 0, t...  19.7 us
    all_to_all x1, waiting for transfers between devices, on_device(): products = lax.all_to_all(products, 'x', 0, 0, tiled=True)  9.09 us
    ppermute x1, starting transfers between devices, on_device(): other_rows = lax.ppermute(own_rows, 'core', [(0, 1), (1, 0)])  6.7 us
    all_to_all x1, starting transfers between devices, on_device(): products = lax.all_to_all(products, 'x', 0, 0, tiled=True)  3.98 us
  transfers between devices with their start and end apart: 2, of which 2 were waited for; matrix products, arithmetic and copies ran while one was open for 0% of the time, Pallas kernels for 1%

profile of v4, /device:TPU:1, one launch (start us, length us, event | category | flops | bytes accessed | tf_op | source)
XLA Modules:
  0.0 118.0 jit_solution(471799546185056977)
XLA Ops:
  0.0 0.0 copy-start
  0.0 0.7 copy-done
  0.7 2.3 %dispatch.1 = (bf16[16,2,16,1024]{3,2,1,0:T(8,128)(2,1)S(1)}, s32[1,256]{1,0:T(1,128)S(1)}) custom-call(s32[1]{0:T(128)} %bitcast.rep_ref, s32[1,256]{1,0:T(1,128)S(1)} %bitcast.15, bf16[256,4096]{1,0:T(8,128)(2,1)} %docs_ref.1), custom_call_target="tpu_custom_call" | custom-call | tf_op jit(solution)/shard_map/dispatch/pallas_call | solution.py:212
  3.0 70.3 %all_to_all.15 = bf16[64,8,1024]{2,1,0:T(8,128)(2,1)S(1)} all-to-all(bf16[64,8,1024]{2,1,0:T(8,128)(2,1)S(1)} %bitcast.12), channel_id=1, replica_groups=mesh['z'=16,'x'=4,'core'=2,'rep'=4] {'z','x'}, dimensions={0} | all-to-all | bytes 2097152 | tf_op jit(solution)/shard_map/all_to_all | solution.py:229
  73.4 6.7 %collective-permute-start = (bf16[512,1024]{1,0:T(8,128)(2,1)S(1)}, bf16[512,1024]{1,0:T(8,128)(2,1)S(1)}, u32[]{:S(2)}, u32[]{:S(2)}) collective-permute-start(bf16[512,1024]{1,0:T(8,128)(2,1)S(1)} %bitcast.10), channel_id=1, source_target_pairs={{0,4},{4,0},{1,5},{5,1},{2,6},{6,2},{3,7},{7,3},{8,12},{12,8},{9,1... | collective-permute-start | bytes 3145736 | tf_op jit(solution)/shard_map/ppermute | solution.py:232
  80.1 1.1 own.1
  81.2 1.1 collective-permute-done.rows_ref
  82.3 1.9 %cross.1 = f32[4,264,128]{2,1,0:T(8,128)} custom-call(f32[4,264,128]{2,1,0:T(8,128)S(1)} %get-tuple-element.11.part_ref, bf16[256,2048]{1,0:T(8,128)(2,1)S(1)} %get-tuple-element.12.slots_ref, bf16[512,1024]{1,0:T(8,128)(2,1)S(1)} %collective-permute-done.rows_ref), custom_call_target="tpu_custom_call" | custom-call | tf_op jit(solution)/shard_map/cross/pallas_call | solution.py:248
  84.2 4.0 %all-to-all-start.1 = ((f32[4,264,128]{2,1,0:T(8,128)}), f32[4,264,128]{2,1,0:T(8,128)S(1)}, u32[]{:S(2)}, u32[]{:S(2)}) async-start(f32[4,264,128]{2,1,0:T(8,128)} %cross.1), calls=%async_computation.1 | async-start | bytes 1081344 | tf_op jit(solution)/shard_map/all_to_all | solution.py:257
  88.2 9.1 %all-to-all-done.1.parts_ref = f32[4,264,128]{2,1,0:T(8,128)S(1)} async-done(((f32[4,264,128]{2,1,0:T(8,128)}), f32[4,264,128]{2,1,0:T(8,128)S(1)}, u32[]{:S(2)}, u32[]{:S(2)}) %all-to-all-start.1) | async-done | bytes 540704 | tf_op jit(solution)/shard_map/all_to_all | solution.py:257
  97.3 0.2 best.1
  97.5 19.7 %all_to_all.16 = f32[64,1,128]{2,1,0:T(1,128)S(1)} all-to-all(f32[64,1,128]{2,1,0:T(1,128)S(1)} %bitcast.14), channel_id=1, replica_groups=mesh['z'=16,'x'=4,'core'=2,'rep'=4] {'rep','z'}, dimensions={0} | all-to-all | bytes 65536 | tf_op jit(solution)/shard_map/all_to_all | solution.py:266
  117.2 0.7 collect.1
Async XLA Ops:
  0.0 0.7 copy-start
  73.4 9.0 %collective-permute-start = (bf16[512,1024]{1,0:T(8,128)(2,1)S(1)}, bf16[512,1024]{1,0:T(8,128)(2,1)S(1)}, u32[]{:S(2)}, u32[]{:S(2)}) collective-permute-start(bf16[512,1024]{1,0:T(8,128)(2,1)S(1)} %bitcast.10), channel_id=1, source_target_pairs={{0,4},{4,0},{1,5},{5,1},{2,6},{6,2},{3,7},{7,3},{8,12},{12,8},{9,1... | collective-permute-start | bytes 3145736 | tf_op jit(solution)/shard_map/ppermute | solution.py:232
  84.2 13.1 %all-to-all-start.1 = ((f32[4,264,128]{2,1,0:T(8,128)}), f32[4,264,128]{2,1,0:T(8,128)S(1)}, u32[]{:S(2)}, u32[]{:S(2)}) async-start(f32[4,264,128]{2,1,0:T(8,128)} %cross.1), calls=%async_computation.1 | async-start | bytes 1081344 | tf_op jit(solution)/shard_map/all_to_all | solution.py:257

commit v5 on v4

--- a/solution.py
+++ b/solution.py
@@ -127,26 +127,27 @@
             tile = block[inside] if lane // 2 == b else products[rows, span]
             out_ref[lane, b * LOCAL : (b + 1) * LOCAL, :] = tile
             out_ref[lane, 4 * LOCAL + b : 4 * LOCAL + b + 1, :] = squares
-
-
-def cross_kernel(part_ref, slots_ref, rows_ref, out_ref, other_ref, vacant_ref):
+    for lane in range(LANES):
+        out_ref[lane, 4 * LOCAL + 4 :, :] = jnp.zeros((4, 128), f32)
+
+
+def cross_kernel(part_ref, own_ref, rows_ref, out_ref, other_ref, vacant_ref):
     gather_slots(rows_ref, other_ref, vacant_ref)
-    products = multiply(slots_ref[...], other_ref[...])
+    other = other_ref[...]
+    products = multiply(jnp.concatenate([own_ref[...], other], axis=0), other)
     for lane in range(LANES):
         rows = slice(lane * LOCAL, (lane + 1) * LOCAL)
-        out_ref[lane, : 2 * LOCAL, :] = part_ref[lane, : 2 * LOCAL, :]
+        own_rows = slice(0, 2 * LOCAL)
+        out_ref[lane, own_rows, :] = part_ref[lane, own_rows, :]
         out_ref[lane, 2 * LOCAL : 3 * LOCAL, :] = products[rows, :128]
         out_ref[lane, 3 * LOCAL : 4 * LOCAL, :] = products[rows, 128:]
+        out_ref[lane, 4 * LOCAL :, :] = part_ref[lane, 4 * LOCAL :, :]
     for b in range(2):
         span = slice(b * 128, (b + 1) * 128)
-        others = other_ref[span, :]
-        squares = flagged_block(multiply(others, others), vacant_ref[span, :])[1]
+        below = products[SLOTS + b * 128 : SLOTS + (b + 1) * 128, span]
+        squares = flagged_block(below, vacant_ref[span, :])[1]
         for lane in range(LANES):
             out_ref[lane, 4 * LOCAL + 2 + b : 4 * LOCAL + 3 + b, :] = squares
-    for lane in range(LANES):
-        own_norms = slice(4 * LOCAL, 4 * LOCAL + 2)
-        out_ref[lane, own_norms, :] = part_ref[lane, own_norms, :]
-        out_ref[lane, 4 * LOCAL + 4 :, :] = jnp.zeros((4, 128), f32)
 
 
 def best_kernel(lane_ref, parts_ref, out_ref):
@@ -202,13 +203,13 @@
 VMEM = pl.BlockSpec(memory_space=pltpu.VMEM)
 SMEM = pl.BlockSpec(memory_space=pltpu.SMEM)
 HBM = pl.BlockSpec(memory_space=pltpu.HBM)
-WIDE = pltpu.CompilerParams(vmem_limit_bytes=52 * 1024 * 1024)
 PARAMS = pltpu.CompilerParams(vmem_limit_bytes=32 * 1024 * 1024)
 
 
 def on_device(embeddings, cluster_of):
     rep = lax.axis_index("rep").reshape(1)
     lane = lax.axis_index("x").reshape(1)
+    labels = pltpu.with_memory_space_constraint(cluster_of.reshape(1, DOCS), pltpu.HBM)
     outgoing, slot = pl.pallas_call(
         dispatch_kernel,
         in_specs=[SMEM, HBM, HBM],
@@ -223,9 +224,9 @@
             pltpu.SemaphoreType.DMA,
             pltpu.SemaphoreType.DMA((STEPS, 2)),
         ],
-        compiler_params=WIDE,
+        compiler_params=PARAMS,
         name="dispatch",
-    )(rep, cluster_of.reshape(1, DOCS), embeddings)
+    )(rep, labels, pltpu.with_memory_space_constraint(embeddings, pltpu.HBM))
     own_rows = lax.all_to_all(
         outgoing.reshape(SOURCES, 2 * RANKS, HALF), ("z", "x"), 0, 0, tiled=True
     ).reshape(ROWS, HALF)

time: 118 us -> 118 us (level)
  no operation moved by 1% of the time
where the time goes in v5:
time: 118 us
  blocking collectives  90.1 us (76%)
  starting transfers between devices  10.7 us (9%)
  waiting for transfers between devices  10.2 us (9%)
  Pallas kernels  6.84 us (6%)
    all_to_all x1, blocking collectives, on_device(): lax.all_to_all(outgoing.reshape(SOURCES, 2 * RANKS, HALF), ('z', 'x'), 0,...  70.3 us
    all_to_all x1, blocking collectives, on_device(): lax.all_to_all(best.reshape(REPS * PLANES, 1, 128), ('rep', 'z'), 0, 0, t...  19.7 us
    all_to_all x1, waiting for transfers between devices, on_device(): products = lax.all_to_all(products, 'x', 0, 0, tiled=True)  9.09 us
    ppermute x1, starting transfers between devices, on_device(): other_rows = lax.ppermute(own_rows, 'core', [(0, 1), (1, 0)])  6.7 us
    all_to_all x1, starting transfers between devices, on_device(): products = lax.all_to_all(products, 'x', 0, 0, tiled=True)  3.97 us
    pallas_call x1, Pallas kernels, on_device(): pl.pallas_call(dispatch_kernel, in_specs=[SMEM, HBM, HBM], out_specs=[VME...  2.88 us
  transfers between devices with their start and end apart: 2, of which 2 were waited for; matrix products, arithmetic and copies ran while one was open for 0% of the time, Pallas kernels for 1%

profile of v5, /device:TPU:1, one launch (start us, length us, event | category | flops | bytes accessed | tf_op | source)
XLA Modules:
  0.0 117.8 jit_solution(17715641869728864182)
XLA Ops:
  0.0 2.9 %dispatch.1 = (bf16[16,2,16,1024]{3,2,1,0:T(8,128)(2,1)S(1)}, s32[1,256]{1,0:T(1,128)S(1)}) custom-call(s32[1]{0:T(128)} %bitcast.rep_ref, s32[1,256]{1,0:T(1,128)} %bitcast.15, bf16[256,4096]{1,0:T(8,128)(2,1)} %docs_ref.1), custom_call_target="tpu_custom_call" | custom-call | tf_op jit(solution)/shard_map/dispatch/pallas_call | solution.py:213
  2.9 70.3 %all_to_all.15 = bf16[64,8,1024]{2,1,0:T(8,128)(2,1)S(1)} all-to-all(bf16[64,8,1024]{2,1,0:T(8,128)(2,1)S(1)} %bitcast.12), channel_id=1, replica_groups=mesh['z'=16,'x'=4,'core'=2,'rep'=4] {'z','x'}, dimensions={0} | all-to-all | bytes 2097152 | tf_op jit(solution)/shard_map/all_to_all | solution.py:230
  73.2 6.7 %collective-permute-start = (bf16[512,1024]{1,0:T(8,128)(2,1)S(1)}, bf16[512,1024]{1,0:T(8,128)(2,1)S(1)}, u32[]{:S(2)}, u32[]{:S(2)}) collective-permute-start(bf16[512,1024]{1,0:T(8,128)(2,1)S(1)} %bitcast.10), channel_id=1, source_target_pairs={{0,4},{4,0},{1,5},{5,1},{2,6},{6,2},{3,7},{7,3},{8,12},{12,8},{9,1... | collective-permute-start | bytes 3145736 | tf_op jit(solution)/shard_map/ppermute | solution.py:233
  79.9 1.1 own.1
  81.1 1.1 collective-permute-done.rows_ref
  82.2 1.9 %cross.1 = f32[4,264,128]{2,1,0:T(8,128)} custom-call(f32[4,264,128]{2,1,0:T(8,128)S(1)} %get-tuple-element.11.part_ref, bf16[256,2048]{1,0:T(8,128)(2,1)S(1)} %get-tuple-element.12.own_ref, bf16[512,1024]{1,0:T(8,128)(2,1)S(1)} %collective-permute-done.rows_ref), custom_call_target="tpu_custom_call" | custom-call | tf_op jit(solution)/shard_map/cross/pallas_call | solution.py:249
  84.1 4.0 %all-to-all-start.1 = ((f32[4,264,128]{2,1,0:T(8,128)}), f32[4,264,128]{2,1,0:T(8,128)S(1)}, u32[]{:S(2)}, u32[]{:S(2)}) async-start(f32[4,264,128]{2,1,0:T(8,128)} %cross.1), calls=%async_computation.1 | async-start | bytes 1081344 | tf_op jit(solution)/shard_map/all_to_all | solution.py:258
  88.1 9.1 %all-to-all-done.1.parts_ref = f32[4,264,128]{2,1,0:T(8,128)S(1)} async-done(((f32[4,264,128]{2,1,0:T(8,128)}), f32[4,264,128]{2,1,0:T(8,128)S(1)}, u32[]{:S(2)}, u32[]{:S(2)}) %all-to-all-start.1) | async-done | bytes 540704 | tf_op jit(solution)/shard_map/all_to_all | solution.py:258
  97.2 0.2 best.1
  97.4 19.7 %all_to_all.16 = f32[64,1,128]{2,1,0:T(1,128)S(1)} all-to-all(f32[64,1,128]{2,1,0:T(1,128)S(1)} %bitcast.14), channel_id=1, replica_groups=mesh['z'=16,'x'=4,'core'=2,'rep'=4] {'rep','z'}, dimensions={0} | all-to-all | bytes 65536 | tf_op jit(solution)/shard_map/all_to_all | solution.py:267
  117.1 0.7 collect.1
Async XLA Ops:
  73.2 9.0 %collective-permute-start = (bf16[512,1024]{1,0:T(8,128)(2,1)S(1)}, bf16[512,1024]{1,0:T(8,128)(2,1)S(1)}, u32[]{:S(2)}, u32[]{:S(2)}) collective-permute-start(bf16[512,1024]{1,0:T(8,128)(2,1)S(1)} %bitcast.10), channel_id=1, source_target_pairs={{0,4},{4,0},{1,5},{5,1},{2,6},{6,2},{3,7},{7,3},{8,12},{12,8},{9,1... | collective-permute-start | bytes 3145736 | tf_op jit(solution)/shard_map/ppermute | solution.py:233
  84.1 13.1 %all-to-all-start.1 = ((f32[4,264,128]{2,1,0:T(8,128)}), f32[4,264,128]{2,1,0:T(8,128)S(1)}, u32[]{:S(2)}, u32[]{:S(2)}) async-start(f32[4,264,128]{2,1,0:T(8,128)} %cross.1), calls=%async_computation.1 | async-start | bytes 1081344 | tf_op jit(solution)/shard_map/all_to_all | solution.py:258

commit v6 on v5

--- a/solution.py
+++ b/solution.py
@@ -35,7 +35,7 @@
 
 
 def dispatch_kernel(
-    rep_ref, cluster_ref, docs_ref, out_ref, slot_ref, labels, docs, label_sem, sems
+    cluster_ref, docs_ref, out_ref, slot_ref, labels, docs, label_sem, sems
 ):
     fetch_labels = pltpu.make_async_copy(cluster_ref, labels, label_sem)
     fetch_labels.start()
@@ -60,7 +60,7 @@
     rank = jnp.sum(jnp.where(earlier, f32(1.0), f32(0.0)), axis=0, keepdims=True)
     slot = cluster * RANKS + rank.astype(jnp.int32)
     slot_ref[...] = slot
-    local = slot - rep_ref[0] * (PLANES * PAIR * RANKS)
+    local = slot - lax.axis_index("rep") * (PLANES * PAIR * RANKS)
     hit = (first >> 1) == local
     odd = (first & 1) == 1
     zero, one = f32(0.0), f32(1.0)
@@ -150,7 +150,7 @@
             out_ref[lane, 4 * LOCAL + 2 + b : 4 * LOCAL + 3 + b, :] = squares
 
 
-def best_kernel(lane_ref, parts_ref, out_ref):
+def best_kernel(parts_ref, out_ref):
     row, column = iota((LOCAL, 128), 0), iota((LOCAL, 128), 1)
     spot = column & 7
     rank = (row >> 3) & 3
@@ -163,7 +163,7 @@
         total = parts_ref[cluster] + parts_ref[PAIR + cluster]
         tiles = [total[t * LOCAL : (t + 1) * LOCAL] for t in range(4)]
         mates = [scale(total[4 * LOCAL + t : 4 * LOCAL + t + 1]) for t in range(4)]
-        same = [column + t * 128 == row + lane_ref[0] * LOCAL for t in range(2)]
+        same = [column + t * 128 == row + lax.axis_index("x") * LOCAL for t in range(2)]
         squares = jnp.where(same[0], tiles[0], f32(0.0)) + jnp.where(same[1], tiles[1], f32(0.0))
         own = scale(jnp.sum(squares, axis=1, keepdims=True))
         best = jnp.full((LOCAL, 128), -1.0, f32)
@@ -201,18 +201,15 @@
 
 
 VMEM = pl.BlockSpec(memory_space=pltpu.VMEM)
-SMEM = pl.BlockSpec(memory_space=pltpu.SMEM)
 HBM = pl.BlockSpec(memory_space=pltpu.HBM)
 PARAMS = pltpu.CompilerParams(vmem_limit_bytes=32 * 1024 * 1024)
 
 
 def on_device(embeddings, cluster_of):
-    rep = lax.axis_index("rep").reshape(1)
-    lane = lax.axis_index("x").reshape(1)
     labels = pltpu.with_memory_space_constraint(cluster_of.reshape(1, DOCS), pltpu.HBM)
     outgoing, slot = pl.pallas_call(
         dispatch_kernel,
-        in_specs=[SMEM, HBM, HBM],
+        in_specs=[HBM, HBM],
         out_specs=[VMEM, VMEM],
         out_shape=[
             jax.ShapeDtypeStruct((PLANES, PARTS, 16, HALF), bf16),
@@ -226,7 +223,7 @@
         ],
         compiler_params=PARAMS,
         name="dispatch",
-    )(rep, labels, pltpu.with_memory_space_constraint(embeddings, pltpu.HBM))
+    )(labels, pltpu.with_memory_space_constraint(embeddings, pltpu.HBM))
     own_rows = lax.all_to_all(
         outgoing.reshape(SOURCES, 2 * RANKS, HALF), ("z", "x"), 0, 0, tiled=True
     ).reshape(ROWS, HALF)
@@ -258,12 +255,12 @@
     products = lax.all_to_all(products, "x", 0, 0, tiled=True)
     best = pl.pallas_call(
         best_kernel,
-        in_specs=[SMEM, VMEM],
+        in_specs=[VMEM],
         out_specs=VMEM,
         out_shape=jax.ShapeDtypeStruct((REPS * PLANES, 128), f32),
         compiler_params=PARAMS,
         name="best",
-    )(lane, products)
+    )(products)
     returned = lax.all_to_all(
         best.reshape(REPS * PLANES, 1, 128), ("rep", "z"), 0, 0, tiled=True
     ).reshape(REPS * PLANES, 128)

time: 118 us -> 117 us (level)
  blocking collectives: 90.1 us -> 102 us
  waiting for transfers between devices: 10.2 us -> 1.13 us
  starting transfers between devices: 10.7 us -> 6.7 us
    all_to_all x0 -> x1, blocking collectives: none -> 12.9 us  [on_device(): products = lax.all_to_all(products, 'x', 0, 0, tiled=True)]
    all_to_all x1 -> x0, waiting for transfers between devices: 9.09 us -> none  [on_device(): products = lax.all_to_all(products, 'x', 0, 0, tiled=True)]
    all_to_all x1 -> x0, starting transfers between devices: 3.97 us -> none  [on_device(): products = lax.all_to_all(products, 'x', 0, 0, tiled=True)]
  transfers between devices with their start and end apart: 2 -> 1, of which waited for: 2 -> 1; matrix products, arithmetic and copies ran while one was open for 0% -> 0% of each run, Pallas kernels for 1% -> 1%
where the time goes in v6:
time: 117 us; the launch traced here: 116 us
  blocking collectives  102 us (87%)
  starting transfers between devices  6.7 us (6%)
  Pallas kernels  6.05 us (5%)
    all_to_all x1, blocking collectives, on_device(): lax.all_to_all(outgoing.reshape(SOURCES, 2 * RANKS, HALF), ('z', 'x'), 0,...  70.3 us
    all_to_all x1, blocking collectives, on_device(): lax.all_to_all(best.reshape(REPS * PLANES, 1, 128), ('rep', 'z'), 0, 0, t...  18.9 us
    all_to_all x1, blocking collectives, on_device(): products = lax.all_to_all(products, 'x', 0, 0, tiled=True)  12.9 us
    ppermute x1, starting transfers between devices, on_device(): other_rows = lax.ppermute(own_rows, 'core', [(0, 1), (1, 0)])  6.7 us
    pallas_call x1, Pallas kernels, on_device(): pl.pallas_call(dispatch_kernel, in_specs=[HBM, HBM], out_specs=[VMEM, VME...  2.88 us
  transfers between devices with their start and end apart: 1, of which 1 were waited for; matrix products, arithmetic and copies ran while one was open for 0% of the time, Pallas kernels for 1%

profile of v6, /device:TPU:1, one launch (start us, length us, event | category | flops | bytes accessed | tf_op | source)
XLA Modules:
  0.0 116.0 jit_solution(16935999517022286376)
XLA Ops:
  0.0 2.9 %dispatch.1 = (bf16[16,2,16,1024]{3,2,1,0:T(8,128)(2,1)S(1)}, s32[1,256]{1,0:T(1,128)S(1)}) custom-call(s32[1,256]{1,0:T(1,128)} %bitcast.13, bf16[256,4096]{1,0:T(8,128)(2,1)} %docs_ref.1), custom_call_target="tpu_custom_call" | custom-call | tf_op jit(solution)/shard_map/dispatch/pallas_call | solution.py:210
  2.9 70.3 %all_to_all.15 = bf16[64,8,1024]{2,1,0:T(8,128)(2,1)S(1)} all-to-all(bf16[64,8,1024]{2,1,0:T(8,128)(2,1)S(1)} %bitcast.10), channel_id=1, replica_groups=mesh['z'=16,'x'=4,'core'=2,'rep'=4] {'z','x'}, dimensions={0} | all-to-all | bytes 2097152 | tf_op jit(solution)/shard_map/all_to_all | solution.py:227
  73.2 6.7 %collective-permute-start = (bf16[512,1024]{1,0:T(8,128)(2,1)S(1)}, bf16[512,1024]{1,0:T(8,128)(2,1)S(1)}, u32[]{:S(2)}, u32[]{:S(2)}) collective-permute-start(bf16[512,1024]{1,0:T(8,128)(2,1)S(1)} %bitcast.8), channel_id=1, source_target_pairs={{0,4},{4,0},{1,5},{5,1},{2,6},{6,2},{3,7},{7,3},{8,12},{12,8},{9,1... | collective-permute-start | bytes 3145736 | tf_op jit(solution)/shard_map/ppermute | solution.py:230
  79.9 1.1 own.1
  81.1 1.1 collective-permute-done.rows_ref
  82.2 1.1 cross.1
  83.3 12.9 %all_to_all.16.parts_ref = f32[4,264,128]{2,1,0:T(8,128)S(1)} all-to-all(f32[4,264,128]{2,1,0:T(8,128)S(1)} %cross.1), channel_id=1, replica_groups=mesh['z'=16,'x'=4,'core'=2,'rep'=4] {'x'}, dimensions={0} | all-to-all | bytes 1081344 | tf_op jit(solution)/shard_map/all_to_all | solution.py:255
  96.2 0.2 best.1
  96.4 18.9 %all_to_all.17 = f32[64,1,128]{2,1,0:T(1,128)S(1)} all-to-all(f32[64,1,128]{2,1,0:T(1,128)S(1)} %bitcast.11), channel_id=1, replica_groups=mesh['z'=16,'x'=4,'core'=2,'rep'=4] {'rep','z'}, dimensions={0} | all-to-all | bytes 65536 | tf_op jit(solution)/shard_map/all_to_all | solution.py:264
  115.3 0.7 collect.1
Async XLA Ops:
  73.2 9.0 %collective-permute-start = (bf16[512,1024]{1,0:T(8,128)(2,1)S(1)}, bf16[512,1024]{1,0:T(8,128)(2,1)S(1)}, u32[]{:S(2)}, u32[]{:S(2)}) collective-permute-start(bf16[512,1024]{1,0:T(8,128)(2,1)S(1)} %bitcast.8), channel_id=1, source_target_pairs={{0,4},{4,0},{1,5},{5,1},{2,6},{6,2},{3,7},{7,3},{8,12},{12,8},{9,1... | collective-permute-start | bytes 3145736 | tf_op jit(solution)/shard_map/ppermute | solution.py:230

commit v7 on v6

--- a/solution.py
+++ b/solution.py
@@ -39,19 +39,23 @@
 ):
     fetch_labels = pltpu.make_async_copy(cluster_ref, labels, label_sem)
     fetch_labels.start()
-    fetches = []
-    for step in range(STEPS):
-        fetches.append([])
+
+    def fetch(step):
+        copies = []
         for half in range(2):
             at = (step // 2) * SHARE + half * HALF + (step % 2) * STRIP
-            fetch = pltpu.make_async_copy(
+            copy = pltpu.make_async_copy(
                 docs_ref.at[:, at : at + STRIP],
                 docs.at[step, half * DOCS : (half + 1) * DOCS, :],
                 sems.at[step, half],
             )
-            fetch.start()
-            fetches[step].append(fetch)
+            copy.start()
+            copies.append(copy)
+        return copies
+
+    fetches = [fetch(step) for step in range(STEPS // 2)]
     fetch_labels.wait()
+    fetches += [fetch(step) for step in range(STEPS // 2, STEPS)]
     cluster = labels[...]
     row = jnp.broadcast_to(cluster.astype(f32), (DOCS, DOCS))
     first, second = iota((DOCS, DOCS), 0), iota((DOCS, DOCS), 1)
@@ -73,8 +77,8 @@
     )
     live = jnp.dot(chosen, jnp.ones((2 * DOCS, 128), bf16), preferred_element_type=f32) > 0.5
     for step in range(STEPS):
-        for fetch in fetches[step]:
-            fetch.wait()
+        for copy in fetches[step]:
+            copy.wait()
         merged = jnp.dot(chosen, docs[step], preferred_element_type=f32)
         at = (step % 2) * STRIP
         if at == 0:

time: 117 us -> 117 us (level)
  no operation moved by 1% of the time
where the time goes in v7:
time: 117 us; the launch traced here: 116 us
  blocking collectives  102 us (87%)
  starting transfers between devices  6.7 us (6%)
  Pallas kernels  5.88 us (5%)
    all_to_all x1, blocking collectives, on_device(): lax.all_to_all(outgoing.reshape(SOURCES, 2 * RANKS, HALF), ('z', 'x'), 0,...  70.3 us
    all_to_all x1, blocking collectives, on_device(): lax.all_to_all(best.reshape(REPS * PLANES, 1, 128), ('rep', 'z'), 0, 0, t...  18.8 us
    all_to_all x1, blocking collectives, on_device(): products = lax.all_to_all(products, 'x', 0, 0, tiled=True)  12.8 us
    ppermute x1, starting transfers between devices, on_device(): other_rows = lax.ppermute(own_rows, 'core', [(0, 1), (1, 0)])  6.7 us
    pallas_call x1, Pallas kernels, on_device(): pl.pallas_call(dispatch_kernel, in_specs=[HBM, HBM], out_specs=[VMEM, VME...  2.7 us
  transfers between devices with their start and end apart: 1, of which 1 were waited for; matrix products, arithmetic and copies ran while one was open for 0% of the time, Pallas kernels for 1%

profile of v7, /device:TPU:1, one launch (start us, length us, event | category | flops | bytes accessed | tf_op | source)
XLA Modules:
  0.0 115.8 jit_solution(14399960594265607958)
XLA Ops:
  0.0 2.7 %dispatch.1 = (bf16[16,2,16,1024]{3,2,1,0:T(8,128)(2,1)S(1)}, s32[1,256]{1,0:T(1,128)S(1)}) custom-call(s32[1,256]{1,0:T(1,128)} %bitcast.13, bf16[256,4096]{1,0:T(8,128)(2,1)} %docs_ref.1), custom_call_target="tpu_custom_call" | custom-call | tf_op jit(solution)/shard_map/dispatch/pallas_call | solution.py:214
  2.7 70.3 %all_to_all.15 = bf16[64,8,1024]{2,1,0:T(8,128)(2,1)S(1)} all-to-all(bf16[64,8,1024]{2,1,0:T(8,128)(2,1)S(1)} %bitcast.10), channel_id=1, replica_groups=mesh['z'=16,'x'=4,'core'=2,'rep'=4] {'z','x'}, dimensions={0} | all-to-all | bytes 2097152 | tf_op jit(solution)/shard_map/all_to_all | solution.py:231
  73.1 6.7 %collective-permute-start = (bf16[512,1024]{1,0:T(8,128)(2,1)S(1)}, bf16[512,1024]{1,0:T(8,128)(2,1)S(1)}, u32[]{:S(2)}, u32[]{:S(2)}) collective-permute-start(bf16[512,1024]{1,0:T(8,128)(2,1)S(1)} %bitcast.8), channel_id=1, source_target_pairs={{0,4},{4,0},{1,5},{5,1},{2,6},{6,2},{3,7},{7,3},{8,12},{12,8},{9,1... | collective-permute-start | bytes 3145736 | tf_op jit(solution)/shard_map/ppermute | solution.py:234
  79.8 1.1 own.1
  80.9 1.1 collective-permute-done.rows_ref
  82.0 1.1 cross.1
  83.1 12.8 %all_to_all.16.parts_ref = f32[4,264,128]{2,1,0:T(8,128)S(1)} all-to-all(f32[4,264,128]{2,1,0:T(8,128)S(1)} %cross.1), channel_id=1, replica_groups=mesh['z'=16,'x'=4,'core'=2,'rep'=4] {'x'}, dimensions={0} | all-to-all | bytes 1081344 | tf_op jit(solution)/shard_map/all_to_all | solution.py:259
  96.0 0.2 best.1
  96.2 18.8 %all_to_all.17 = f32[64,1,128]{2,1,0:T(1,128)S(1)} all-to-all(f32[64,1,128]{2,1,0:T(1,128)S(1)} %bitcast.11), channel_id=1, replica_groups=mesh['z'=16,'x'=4,'core'=2,'rep'=4] {'rep','z'}, dimensions={0} | all-to-all | bytes 65536 | tf_op jit(solution)/shard_map/all_to_all | solution.py:268
  115.1 0.7 collect.1
Async XLA Ops:
  73.1 9.0 %collective-permute-start = (bf16[512,1024]{1,0:T(8,128)(2,1)S(1)}, bf16[512,1024]{1,0:T(8,128)(2,1)S(1)}, u32[]{:S(2)}, u32[]{:S(2)}) collective-permute-start(bf16[512,1024]{1,0:T(8,128)(2,1)S(1)} %bitcast.8), channel_id=1, source_target_pairs={{0,4},{4,0},{1,5},{5,1},{2,6},{6,2},{3,7},{7,3},{8,12},{12,8},{9,1... | collective-permute-start | bytes 3145736 | tf_op jit(solution)/shard_map/ppermute | solution.py:234

commit v8 on v6

--- a/solution.py
+++ b/solution.py
@@ -22,8 +22,6 @@
 CHUNK = 256
 LOCAL = SLOTS // LANES
 BLOCK = 4 * LOCAL + 8
-STRIP = HALF // 2
-STEPS = PARTS * 2
 
 epsilon = 1e-06
 f32 = jnp.float32
@@ -39,18 +37,13 @@
 ):
     fetch_labels = pltpu.make_async_copy(cluster_ref, labels, label_sem)
     fetch_labels.start()
+
     fetches = []
-    for step in range(STEPS):
-        fetches.append([])
-        for half in range(2):
-            at = (step // 2) * SHARE + half * HALF + (step % 2) * STRIP
-            fetch = pltpu.make_async_copy(
-                docs_ref.at[:, at : at + STRIP],
-                docs.at[step, half * DOCS : (half + 1) * DOCS, :],
-                sems.at[step, half],
-            )
-            fetch.start()
-            fetches[step].append(fetch)
+    for part in range(PARTS):
+        columns = slice(part * SHARE, (part + 1) * SHARE)
+        fetch = pltpu.make_async_copy(docs_ref.at[:, columns], docs.at[part], sems.at[part])
+        fetch.start()
+        fetches.append(fetch)
     fetch_labels.wait()
     cluster = labels[...]
     row = jnp.broadcast_to(cluster.astype(f32), (DOCS, DOCS))
@@ -64,23 +57,17 @@
     hit = (first >> 1) == local
     odd = (first & 1) == 1
     zero, one = f32(0.0), f32(1.0)
-    chosen = jnp.concatenate(
-        [
-            jnp.where(hit & jnp.logical_not(odd), one, zero).astype(bf16),
-            jnp.where(hit & odd, one, zero).astype(bf16),
-        ],
-        axis=1,
-    )
-    live = jnp.dot(chosen, jnp.ones((2 * DOCS, 128), bf16), preferred_element_type=f32) > 0.5
-    for step in range(STEPS):
-        for fetch in fetches[step]:
-            fetch.wait()
-        merged = jnp.dot(chosen, docs[step], preferred_element_type=f32)
-        at = (step % 2) * STRIP
-        if at == 0:
-            marked = jnp.where(live, merged[:, :128], jnp.nan)
-            merged = jnp.concatenate([marked, merged[:, 128:]], axis=1)
-        out_ref[:, step // 2, :, at : at + STRIP] = merged.astype(bf16).reshape(PLANES, 16, STRIP)
+    even = jnp.where(hit & jnp.logical_not(odd), one, zero).astype(bf16)
+    uneven = jnp.where(hit & odd, one, zero).astype(bf16)
+    ones = jnp.ones((DOCS, 128), bf16)
+    live = jnp.dot(even + uneven, ones, preferred_element_type=f32) > 0.5
+    for part in range(PARTS):
+        fetches[part].wait()
+        merged = jnp.dot(even, docs[part, :, :HALF], preferred_element_type=f32)
+        merged = merged + jnp.dot(uneven, docs[part, :, HALF:], preferred_element_type=f32)
+        marked = jnp.where(live, merged[:, :128], jnp.nan)
+        merged = jnp.concatenate([marked, merged[:, 128:]], axis=1)
+        out_ref[:, part, :, :] = merged.astype(bf16).reshape(PLANES, 16, HALF)
 
 
 def multiply(left, right):
@@ -217,9 +204,9 @@
         ],
         scratch_shapes=[
             pltpu.VMEM((1, DOCS), jnp.int32),
-            pltpu.VMEM((STEPS, 2 * DOCS, STRIP), bf16),
+            pltpu.VMEM((PARTS, DOCS, SHARE), bf16),
             pltpu.SemaphoreType.DMA,
-            pltpu.SemaphoreType.DMA((STEPS, 2)),
+            pltpu.SemaphoreType.DMA((PARTS,)),
         ],
         compiler_params=PARAMS,
         name="dispatch",

time: 117 us -> 116 us (level)
  no operation moved by 1% of the time
where the time goes in v8:
time: 116 us; the launch traced here: 115 us
  blocking collectives  102 us (88%)
  starting transfers between devices  6.7 us (6%)
  Pallas kernels  5.38 us (5%)
    all_to_all x1, blocking collectives, on_device(): lax.all_to_all(outgoing.reshape(SOURCES, 2 * RANKS, HALF), ('z', 'x'), 0,...  70.3 us
    all_to_all x1, blocking collectives, on_device(): lax.all_to_all(best.reshape(REPS * PLANES, 1, 128), ('rep', 'z'), 0, 0, t...  18.9 us
    all_to_all x1, blocking collectives, on_device(): products = lax.all_to_all(products, 'x', 0, 0, tiled=True)  12.8 us
    ppermute x1, starting transfers between devices, on_device(): other_rows = lax.ppermute(own_rows, 'core', [(0, 1), (1, 0)])  6.7 us
  transfers between devices with their start and end apart: 1, of which 1 were waited for; matrix products, arithmetic and copies ran while one was open for 0% of the time, Pallas kernels for 1%

profile of v8, /device:TPU:1, one launch (start us, length us, event | category | flops | bytes accessed | tf_op | source)
XLA Modules:
  0.0 115.3 jit_solution(11913334593902807615)
XLA Ops:
  0.0 2.2 %dispatch.1 = (bf16[16,2,16,1024]{3,2,1,0:T(8,128)(2,1)S(1)}, s32[1,256]{1,0:T(1,128)S(1)}) custom-call(s32[1,256]{1,0:T(1,128)} %bitcast.13, bf16[256,4096]{1,0:T(8,128)(2,1)} %docs_ref.1), custom_call_target="tpu_custom_call" | custom-call | tf_op jit(solution)/shard_map/dispatch/pallas_call | solution.py:197
  2.2 70.3 %all_to_all.15 = bf16[64,8,1024]{2,1,0:T(8,128)(2,1)S(1)} all-to-all(bf16[64,8,1024]{2,1,0:T(8,128)(2,1)S(1)} %bitcast.10), channel_id=1, replica_groups=mesh['z'=16,'x'=4,'core'=2,'rep'=4] {'z','x'}, dimensions={0} | all-to-all | bytes 2097152 | tf_op jit(solution)/shard_map/all_to_all | solution.py:214
  72.6 6.7 %collective-permute-start = (bf16[512,1024]{1,0:T(8,128)(2,1)S(1)}, bf16[512,1024]{1,0:T(8,128)(2,1)S(1)}, u32[]{:S(2)}, u32[]{:S(2)}) collective-permute-start(bf16[512,1024]{1,0:T(8,128)(2,1)S(1)} %bitcast.8), channel_id=1, source_target_pairs={{0,4},{4,0},{1,5},{5,1},{2,6},{6,2},{3,7},{7,3},{8,12},{12,8},{9,1... | collective-permute-start | bytes 3145736 | tf_op jit(solution)/shard_map/ppermute | solution.py:217
  79.3 1.1 own.1
  80.4 1.1 collective-permute-done.rows_ref
  81.5 1.1 cross.1
  82.6 12.8 %all_to_all.16.parts_ref = f32[4,264,128]{2,1,0:T(8,128)S(1)} all-to-all(f32[4,264,128]{2,1,0:T(8,128)S(1)} %cross.1), channel_id=1, replica_groups=mesh['z'=16,'x'=4,'core'=2,'rep'=4] {'x'}, dimensions={0} | all-to-all | bytes 1081344 | tf_op jit(solution)/shard_map/all_to_all | solution.py:242
  95.5 0.2 best.1
  95.7 18.9 %all_to_all.17 = f32[64,1,128]{2,1,0:T(1,128)S(1)} all-to-all(f32[64,1,128]{2,1,0:T(1,128)S(1)} %bitcast.11), channel_id=1, replica_groups=mesh['z'=16,'x'=4,'core'=2,'rep'=4] {'rep','z'}, dimensions={0} | all-to-all | bytes 65536 | tf_op jit(solution)/shard_map/all_to_all | solution.py:251
  114.6 0.7 collect.1
Async XLA Ops:
  72.6 9.0 %collective-permute-start = (bf16[512,1024]{1,0:T(8,128)(2,1)S(1)}, bf16[512,1024]{1,0:T(8,128)(2,1)S(1)}, u32[]{:S(2)}, u32[]{:S(2)}) collective-permute-start(bf16[512,1024]{1,0:T(8,128)(2,1)S(1)} %bitcast.8), channel_id=1, source_target_pairs={{0,4},{4,0},{1,5},{5,1},{2,6},{6,2},{3,7},{7,3},{8,12},{12,8},{9,1... | collective-permute-start | bytes 3145736 | tf_op jit(solution)/shard_map/ppermute | solution.py:217

commit v9 on v8

--- a/solution.py
+++ b/solution.py
@@ -18,10 +18,13 @@
 HALF = SHARE // 2
 SOURCES = PLANES * LANES
 SLOTS = SOURCES * RANKS
+KEPT = SLOTS // 2
 ROWS = SLOTS * 2
 CHUNK = 256
 LOCAL = SLOTS // LANES
-BLOCK = 4 * LOCAL + 8
+BLOCK = 2 * KEPT + 8
+
+RETURNS = REPS * PAIR * PLANES
 
 epsilon = 1e-06
 f32 = jnp.float32
@@ -101,74 +104,72 @@
     return flagged, jnp.sum(jnp.where(eye, flagged, f32(0.0)), axis=0, keepdims=True)
 
 
-def own_kernel(rows_ref, out_ref, slots_ref, vacant_ref):
+def split_rows(products_ref, squares, keep_ref, send_ref):
+    mine = lax.axis_index("xl")
+    for target, ref in ((mine, keep_ref), (1 - mine, send_ref)):
+        start = pl.multiple_of(target * KEPT, KEPT)
+        for t in range(2):
+            tile = products_ref[pl.ds(start, KEPT), t * 128 : (t + 1) * 128]
+            ref[t * KEPT : (t + 1) * KEPT, :] = tile
+        ref[2 * KEPT :, :] = jnp.concatenate(squares + [jnp.zeros((6, 128), f32)], axis=0)
+
+
+def own_kernel(rows_ref, keep_ref, send_ref, slots_ref, vacant_ref, products_ref):
     gather_slots(rows_ref, slots_ref, vacant_ref)
     slots = slots_ref[...]
-    products = multiply(slots, slots)
+    products_ref[...] = multiply(slots, slots)
+    squares = []
     for b in range(2):
         span = slice(b * 128, (b + 1) * 128)
-        block, squares = flagged_block(products[span, span], vacant_ref[span, :])
-        for lane in range(LANES):
-            rows = slice(lane * LOCAL, (lane + 1) * LOCAL)
-            inside = slice((lane % 2) * LOCAL, (lane % 2 + 1) * LOCAL)
-            tile = block[inside] if lane // 2 == b else products[rows, span]
-            out_ref[lane, b * LOCAL : (b + 1) * LOCAL, :] = tile
-            out_ref[lane, 4 * LOCAL + b : 4 * LOCAL + b + 1, :] = squares
-    for lane in range(LANES):
-        out_ref[lane, 4 * LOCAL + 4 :, :] = jnp.zeros((4, 128), f32)
-
-
-def cross_kernel(part_ref, own_ref, rows_ref, out_ref, other_ref, vacant_ref):
+        block, diagonal = flagged_block(products_ref[span, span], vacant_ref[span, :])
+        products_ref[span, span] = block
+        squares.append(diagonal)
+    split_rows(products_ref, squares, keep_ref, send_ref)
+
+
+def cross_kernel(own_ref, rows_ref, keep_ref, send_ref, other_ref, vacant_ref, products_ref):
     gather_slots(rows_ref, other_ref, vacant_ref)
     other = other_ref[...]
-    products = multiply(jnp.concatenate([own_ref[...], other], axis=0), other)
-    for lane in range(LANES):
-        rows = slice(lane * LOCAL, (lane + 1) * LOCAL)
-        own_rows = slice(0, 2 * LOCAL)
-        out_ref[lane, own_rows, :] = part_ref[lane, own_rows, :]
-        out_ref[lane, 2 * LOCAL : 3 * LOCAL, :] = products[rows, :128]
-        out_ref[lane, 3 * LOCAL : 4 * LOCAL, :] = products[rows, 128:]
-        out_ref[lane, 4 * LOCAL :, :] = part_ref[lane, 4 * LOCAL :, :]
+    products_ref[...] = multiply(jnp.concatenate([own_ref[...], other], axis=0), other)
+    squares = []
     for b in range(2):
         span = slice(b * 128, (b + 1) * 128)
-        below = products[SLOTS + b * 128 : SLOTS + (b + 1) * 128, span]
-        squares = flagged_block(below, vacant_ref[span, :])[1]
-        for lane in range(LANES):
-            out_ref[lane, 4 * LOCAL + 2 + b : 4 * LOCAL + 3 + b, :] = squares
-
-
-def best_kernel(parts_ref, out_ref):
-    row, column = iota((LOCAL, 128), 0), iota((LOCAL, 128), 1)
-    spot = column & 7
-    rank = (row >> 3) & 3
-    spread = jnp.zeros((LOCAL, 128), f32)
+        below = products_ref[SLOTS + b * 128 : SLOTS + (b + 1) * 128, span]
+        squares.append(flagged_block(below, vacant_ref[span, :])[1])
+    split_rows(products_ref, squares, keep_ref, send_ref)
+
+
+def best_kernel(own_keep, own_sent, cross_keep, cross_sent, out_ref):
+    row, column = iota((KEPT, 128), 0), iota((KEPT, 128), 1)
+    mine = lax.axis_index("xl")
 
     def scale(squares):
         return jnp.where(squares == squares, lax.rsqrt(squares + epsilon), f32(-1.0))
 
-    for cluster in range(PAIR):
-        total = parts_ref[cluster] + parts_ref[PAIR + cluster]
-        tiles = [total[t * LOCAL : (t + 1) * LOCAL] for t in range(4)]
-        mates = [scale(total[4 * LOCAL + t : 4 * LOCAL + t + 1]) for t in range(4)]
-        same = [column + t * 128 == row + lax.axis_index("x") * LOCAL for t in range(2)]
-        squares = jnp.where(same[0], tiles[0], f32(0.0)) + jnp.where(same[1], tiles[1], f32(0.0))
-        own = scale(jnp.sum(squares, axis=1, keepdims=True))
-        best = jnp.full((LOCAL, 128), -1.0, f32)
-        for t in range(4):
-            cosine = tiles[t] * own * mates[t]
-            allowed = (own >= 0.0) & (mates[t] >= 0.0)
-            if t < 2:
-                allowed = allowed & jnp.logical_not(same[t])
-            best = jnp.maximum(best, jnp.where(allowed, cosine, f32(-1.0)))
-        best = jnp.max(best, axis=1, keepdims=True)
-        spread = jnp.where(spot == cluster * RANKS + rank, best, spread)
-    planes = []
-    for top in range(0, LOCAL, 32):
-        tiles = [spread[top + k * 8 : top + (k + 1) * 8] for k in range(RANKS)]
-        planes.append((tiles[0] + tiles[1]) + (tiles[2] + tiles[3]))
-    turned = jnp.concatenate(planes, axis=0)
+    tiles, mates = [], []
+    for keep, sent in ((own_keep, own_sent), (cross_keep, cross_sent)):
+        total = keep[...] + sent[...]
+        tiles += [total[t * KEPT : (t + 1) * KEPT] for t in range(2)]
+        mates += [scale(total[2 * KEPT + t : 2 * KEPT + t + 1]) for t in range(2)]
+    same = [(column == row) & (mine == t) for t in range(2)]
+    squares = jnp.where(same[0], tiles[0], f32(0.0)) + jnp.where(same[1], tiles[1], f32(0.0))
+    own = scale(jnp.sum(squares, axis=1, keepdims=True))
+    best = jnp.full((KEPT, 128), -1.0, f32)
+    for t in range(4):
+        cosine = tiles[t] * own * mates[t]
+        allowed = (own >= 0.0) & (mates[t] >= 0.0)
+        if t < 2:
+            allowed = allowed & jnp.logical_not(same[t])
+        best = jnp.maximum(best, jnp.where(allowed, cosine, f32(-1.0)))
+    best = jnp.max(best, axis=1, keepdims=True)
+    spread = jnp.where((column & 3) == ((row >> 3) & 3), best, f32(0.0))
+    lines = []
+    for top in range(0, KEPT, 32):
+        parts = [spread[top + k * 8 : top + (k + 1) * 8] for k in range(RANKS)]
+        lines.append((parts[0] + parts[1]) + (parts[2] + parts[3]))
+    turned = jnp.concatenate(lines, axis=0)
     for rep in range(REPS):
-        out_ref[rep * PLANES : (rep + 1) * PLANES, :] = turned
+        out_ref[rep * PAIR * PLANES : (rep + 1) * PAIR * PLANES, :] = turned
 
 
 def collect_kernel(slot_ref, best_ref, out_ref):
@@ -177,14 +178,16 @@
     high = best.astype(bf16).astype(f32)
     middle = (best - high).astype(bf16).astype(f32)
     low = best - high - middle
-    group = iota((REPS * PLANES, 128), 1) >> 3
+    group = iota((RETURNS, 128), 1) >> 2
     pieces = jnp.where(group == 0, high, jnp.where(group == 1, middle, low))
     pieces = jnp.where(group < 3, pieces, f32(0.0)).astype(bf16)
-    chosen = (iota((128, DOCS), 0) & 7) == (slot & 7)
+    chosen = (iota((128, DOCS), 0) & 3) == (slot & 3)
     chosen = jnp.where(chosen, f32(1.0), f32(0.0)).astype(bf16)
     values = jnp.dot(pieces, chosen, preferred_element_type=f32)
-    line = iota((REPS * PLANES, DOCS), 0) == (slot >> 3)
-    out_ref[...] = jnp.sum(jnp.where(line, values, f32(0.0)), axis=0, keepdims=True)
+    cluster = slot >> 2
+    line = (cluster >> 5) * (PAIR * PLANES) + (cluster & 1) * PLANES + ((cluster & 31) >> 1)
+    hit = iota((RETURNS, DOCS), 0) == line
+    out_ref[...] = jnp.sum(jnp.where(hit, values, f32(0.0)), axis=0, keepdims=True)
 
 
 VMEM = pl.BlockSpec(memory_space=pltpu.VMEM)
@@ -212,45 +215,52 @@
         name="dispatch",
     )(labels, pltpu.with_memory_space_constraint(embeddings, pltpu.HBM))
     own_rows = lax.all_to_all(
-        outgoing.reshape(SOURCES, 2 * RANKS, HALF), ("z", "x"), 0, 0, tiled=True
+        outgoing.reshape(SOURCES, 2 * RANKS, HALF), ("z", "xl", "xh"), 0, 0, tiled=True
     ).reshape(ROWS, HALF)
-    other_rows = lax.ppermute(own_rows, "core", [(0, 1), (1, 0)])
-    part, slots = pl.pallas_call(
+    swap = [(0, 1), (1, 0)]
+    other_rows = lax.ppermute(own_rows, "core", swap)
+    half_rows = jax.ShapeDtypeStruct((BLOCK, 128), f32)
+    own_keep, own_send, slots = pl.pallas_call(
         own_kernel,
         in_specs=[VMEM],
-        out_specs=[VMEM, VMEM],
-        out_shape=[
-            jax.ShapeDtypeStruct((LANES, BLOCK, 128), f32),
-            jax.ShapeDtypeStruct((SLOTS, SHARE), bf16),
-        ],
-        scratch_shapes=[pltpu.VMEM((SLOTS, 128), f32)],
+        out_specs=[VMEM, VMEM, VMEM],
+        out_shape=[half_rows, half_rows, jax.ShapeDtypeStruct((SLOTS, SHARE), bf16)],
+        scratch_shapes=[pltpu.VMEM((SLOTS, 128), f32), pltpu.VMEM((SLOTS, SLOTS), f32)],
         compiler_params=PARAMS,
         cost_estimate=pl.CostEstimate(
             flops=2 * SLOTS * SLOTS * SHARE * 2, bytes_accessed=2**22, transcendentals=0
         ),
         name="own",
     )(own_rows)
-    products = pl.pallas_call(
+    own_sent = lax.ppermute(own_send, "xl", swap)
+    cross_keep, cross_send = pl.pallas_call(
         cross_kernel,
-        in_specs=[VMEM, VMEM, VMEM],
-        out_specs=VMEM,
-        out_shape=jax.ShapeDtypeStruct((LANES, BLOCK, 128), f32),
-        scratch_shapes=[pltpu.VMEM((SLOTS, SHARE), bf16), pltpu.VMEM((SLOTS, 128), f32)],
-        compiler_params=PARAMS,
+        in_specs=[VMEM, VMEM],
+        out_specs=[VMEM, VMEM],
+        out_shape=[half_rows, half_rows],
+        scratch_shapes=[
+            pltpu.VMEM((SLOTS, SHARE), bf16),
+            pltpu.VMEM((SLOTS, 128), f32),
+            pltpu.VMEM((2 * SLOTS, SLOTS), f32),
+        ],
+        compiler_params=PARAMS,
+        cost_estimate=pl.CostEstimate(
+            flops=2 * SLOTS * SLOTS * SHARE * 2, bytes_accessed=2**22, transcendentals=0
+        ),
         name="cross",
-    )(part, slots, other_rows)
-    products = lax.all_to_all(products, "x", 0, 0, tiled=True)
+    )(slots, other_rows)
+    cross_sent = lax.ppermute(cross_send, "xl", swap)
     best = pl.pallas_call(
         best_kernel,
-        in_specs=[VMEM],
+        in_specs=[VMEM, VMEM, VMEM, VMEM],
         out_specs=VMEM,
-        out_shape=jax.ShapeDtypeStruct((REPS * PLANES, 128), f32),
+        out_shape=jax.ShapeDtypeStruct((RETURNS, 128), f32),
         compiler_params=PARAMS,
         name="best",
-    )(products)
+    )(own_keep, own_sent, cross_keep, cross_sent)
     returned = lax.all_to_all(
-        best.reshape(REPS * PLANES, 1, 128), ("rep", "z"), 0, 0, tiled=True
-    ).reshape(REPS * PLANES, 128)
+        best.reshape(RETURNS, 1, 128), ("rep", "xh", "z"), 0, 0, tiled=True
+    ).reshape(RETURNS, 128)
     out = pl.pallas_call(
         collect_kernel,
         in_specs=[VMEM, VMEM],
@@ -263,8 +273,9 @@
 
 
 def solution(mesh):
-    fine = Mesh(mesh.devices.reshape(PLANES, LANES, 2, REPS), ("z", "x", "core", "rep"))
-    shard = ("z", "x", "core")
+    axes = ("z", "xh", "xl", "core", "rep")
+    fine = Mesh(mesh.devices.reshape(PLANES, 2, 2, 2, REPS), axes)
+    shard = axes[:4]
     return jax.shard_map(
         on_device,
         mesh=fine,

time: 116 us -> 117 us (level)
  blocking collectives: 102 us -> 94.9 us
  starting transfers between devices: 6.7 us -> 11.8 us
  waiting for transfers between devices: 1.13 us -> 4.61 us
    all_to_all x3 -> x2, blocking collectives: 102 us -> 94.9 us  [the longest x1 70.5 us: on_device(): lax.all_to_all(outgoing.reshape(SOURCES, 2 * RANKS, HALF), ('z', 'xl', 'x...]
    ppermute x1 -> x3, starting transfers between devices: 6.7 us -> 11.8 us  [the longest x1 6.55 us: on_device(): other_rows = lax.ppermute(own_rows, 'core', swap)]
    ppermute x1 -> x3, waiting for transfers between devices: 1.13 us -> 4.61 us  [the longest x1 3.98 us: on_device(): cross_sent = lax.ppermute(cross_send, 'xl', swap)]
  transfers between devices with their start and end apart: 1 -> 3, of which waited for: 1 -> 2; matrix products, arithmetic and copies ran while one was open for 0% -> 0% of each run, Pallas kernels for 1% -> 2%
where the time goes in v9:
time: 117 us
  blocking collectives  94.9 us (81%)
  starting transfers between devices  11.8 us (10%)
  Pallas kernels  5.52 us (5%)
  waiting for transfers between devices  4.61 us (4%)
    all_to_all x1, blocking collectives, on_device(): lax.all_to_all(outgoing.reshape(SOURCES, 2 * RANKS, HALF), ('z', 'xl', 'x...  70.5 us
    all_to_all x1, blocking collectives, on_device(): lax.all_to_all(best.reshape(RETURNS, 1, 128), ('rep', 'xh', 'z'), 0, 0, t...  24.4 us
    ppermute x1, starting transfers between devices, on_device(): other_rows = lax.ppermute(own_rows, 'core', swap)  6.55 us
    ppermute x1, waiting for transfers between devices, on_device(): cross_sent = lax.ppermute(cross_send, 'xl', swap)  3.98 us
    ppermute x1, starting transfers between devices, on_device(): own_sent = lax.ppermute(own_send, 'xl', swap)  3.11 us
  transfers between devices with their start and end apart: 3, of which 2 were waited for; matrix products, arithmetic and copies ran while one was open for 0% of the time, Pallas kernels for 2%

profile of v9, /device:TPU:1, one launch (start us, length us, event | category | flops | bytes accessed | tf_op | source)
XLA Modules:
  0.0 116.9 jit_solution(2115593508601939211)
XLA Ops:
  0.0 2.2 %dispatch.1 = (bf16[16,2,16,1024]{3,2,1,0:T(8,128)(2,1)S(1)}, s32[1,256]{1,0:T(1,128)S(1)}) custom-call(s32[1,256]{1,0:T(1,128)} %bitcast.13, bf16[256,4096]{1,0:T(8,128)(2,1)} %docs_ref.1), custom_call_target="tpu_custom_call" | custom-call | tf_op jit(solution)/shard_map/dispatch/pallas_call | solution.py:200
  2.2 70.5 %all_to_all.10 = bf16[64,8,1024]{2,1,0:T(8,128)(2,1)S(1)} all-to-all(bf16[64,8,1024]{2,1,0:T(8,128)(2,1)S(1)} %bitcast.10), channel_id=1, replica_groups=mesh['z'=16,'xh'=2,'xl'=2,'core'=2,'rep'=4] {'z','xl','xh'}, dimensions={0} | all-to-all | bytes 2097152 | tf_op jit(solution)/shard_map/all_to_all | solution.py:217
  72.7 6.6 %collective-permute-start.1 = (bf16[512,1024]{1,0:T(8,128)(2,1)S(1)}, bf16[512,1024]{1,0:T(8,128)(2,1)S(1)}, u32[]{:S(2)}, u32[]{:S(2)}) collective-permute-start(bf16[512,1024]{1,0:T(8,128)(2,1)S(1)} %bitcast.8), channel_id=1, source_target_pairs={{0,4},{4,0},{1,5},{5,1},{2,6},{6,2},{3,7},{7,3},{8,12},{12,8},{9,1... | collective-permute-start | bytes 3145736 | tf_op jit(solution)/shard_map/ppermute | solution.py:221
  79.3 1.2 %own.1 = (f32[264,128]{1,0:T(8,128)S(1)}, f32[264,128]{1,0:T(8,128)S(1)}, bf16[256,2048]{1,0:T(8,128)(2,1)S(1)}) custom-call(bf16[512,1024]{1,0:T(8,128)(2,1)S(1)} %bitcast.9), custom_call_target="tpu_custom_call" | custom-call | flops 536870912 | bytes 4194304 | tf_op jit(solution)/shard_map/own/pallas_call | solution.py:223
  80.5 3.1 %collective-permute-start = (f32[264,128]{1,0:T(8,128)S(1)}, f32[264,128]{1,0:T(8,128)S(1)}, u32[]{:S(2)}, u32[]{:S(2)}) collective-permute-start(f32[264,128]{1,0:T(8,128)S(1)} %get-tuple-element.15), channel_id=1, source_target_pairs={{0,8},{8,0},{1,9},{9,1},{2,10},{10,2},{3,11},{11,3},{4,12},{12,4},... | collective-permute-start | bytes 405512 | tf_op jit(solution)/shard_map/ppermute | solution.py:235
  83.6 0.0 collective-permute-done.1.rows_ref
  83.6 1.2 cross.1
  84.7 2.2 %collective-permute-start.2 = (f32[264,128]{1,0:T(8,128)S(1)}, f32[264,128]{1,0:T(8,128)S(1)}, u32[]{:S(2)}, u32[]{:S(2)}) collective-permute-start(f32[264,128]{1,0:T(8,128)S(1)} %get-tuple-element.18), channel_id=1, source_target_pairs={{0,8},{8,0},{1,9},{9,1},{2,10},{10,2},{3,11},{11,3},{4,12},{12,4},... | collective-permute-start | bytes 405512 | tf_op jit(solution)/shard_map/ppermute | solution.py:252
  86.9 0.6 collective-permute-done.own_sent
  87.6 4.0 %collective-permute-done.2.cross_sent = f32[264,128]{1,0:T(8,128)S(1)} collective-permute-done((f32[264,128]{1,0:T(8,128)S(1)}, f32[264,128]{1,0:T(8,128)S(1)}, u32[]{:S(2)}, u32[]{:S(2)}) %collective-permute-start.2) | collective-permute-done | bytes 135200 | tf_op jit(solution)/shard_map/ppermute | solution.py:252
  91.5 0.2 best.1
  91.8 24.4 %all_to_all.11 = f32[128,1,128]{2,1,0:T(1,128)S(1)} all-to-all(f32[128,1,128]{2,1,0:T(1,128)S(1)} %bitcast.11), channel_id=1, replica_groups=mesh['z'=16,'xh'=2,'xl'=2,'core'=2,'rep'=4] {'rep','xh','z'}, dimensions={0} | all-to-all | bytes 131072 | tf_op jit(solution)/shard_map/all_to_all | solution.py:261
  116.2 0.7 collect.1
Async XLA Ops:
  72.7 10.9 %collective-permute-start.1 = (bf16[512,1024]{1,0:T(8,128)(2,1)S(1)}, bf16[512,1024]{1,0:T(8,128)(2,1)S(1)}, u32[]{:S(2)}, u32[]{:S(2)}) collective-permute-start(bf16[512,1024]{1,0:T(8,128)(2,1)S(1)} %bitcast.8), channel_id=1, source_target_pairs={{0,4},{4,0},{1,5},{5,1},{2,6},{6,2},{3,7},{7,3},{8,12},{12,8},{9,1... | collective-permute-start | bytes 3145736 | tf_op jit(solution)/shard_map/ppermute | solution.py:221
  80.5 7.1 %collective-permute-start = (f32[264,128]{1,0:T(8,128)S(1)}, f32[264,128]{1,0:T(8,128)S(1)}, u32[]{:S(2)}, u32[]{:S(2)}) collective-permute-start(f32[264,128]{1,0:T(8,128)S(1)} %get-tuple-element.15), channel_id=1, source_target_pairs={{0,8},{8,0},{1,9},{9,1},{2,10},{10,2},{3,11},{11,3},{4,12},{12,4},... | collective-permute-start | bytes 405512 | tf_op jit(solution)/shard_map/ppermute | solution.py:235
  84.7 6.8 %collective-permute-start.2 = (f32[264,128]{1,0:T(8,128)S(1)}, f32[264,128]{1,0:T(8,128)S(1)}, u32[]{:S(2)}, u32[]{:S(2)}) collective-permute-start(f32[264,128]{1,0:T(8,128)S(1)} %get-tuple-element.18), channel_id=1, source_target_pairs={{0,8},{8,0},{1,9},{9,1},{2,10},{10,2},{3,11},{11,3},{4,12},{12,4},... | collective-permute-start | bytes 405512 | tf_op jit(solution)/shard_map/ppermute | solution.py:252

commit v10 on v8

--- a/solution.py
+++ b/solution.py
@@ -42,7 +42,7 @@
     for part in range(PARTS):
         columns = slice(part * SHARE, (part + 1) * SHARE)
         fetch = pltpu.make_async_copy(docs_ref.at[:, columns], docs.at[part], sems.at[part])
-        fetch.start()
+        fetch.start(priority=1)
         fetches.append(fetch)
     fetch_labels.wait()
     cluster = labels[...]

time: 116 us -> 116 us (level)
  no operation moved by 1% of the time
where the time goes in v10:
time: 116 us; the launch traced here: 115 us
  blocking collectives  102 us (88%)
  starting transfers between devices  6.7 us (6%)
  Pallas kernels  5.33 us (5%)
    all_to_all x1, blocking collectives, on_device(): lax.all_to_all(outgoing.reshape(SOURCES, 2 * RANKS, HALF), ('z', 'x'), 0,...  70.3 us
    all_to_all x1, blocking collectives, on_device(): lax.all_to_all(best.reshape(REPS * PLANES, 1, 128), ('rep', 'z'), 0, 0, t...  18.9 us
    all_to_all x1, blocking collectives, on_device(): products = lax.all_to_all(products, 'x', 0, 0, tiled=True)  12.9 us
    ppermute x1, starting transfers between devices, on_device(): other_rows = lax.ppermute(own_rows, 'core', [(0, 1), (1, 0)])  6.7 us
  transfers between devices with their start and end apart: 1, of which 1 were waited for; matrix products, arithmetic and copies ran while one was open for 0% of the time, Pallas kernels for 1%

profile of v10, /device:TPU:1, one launch (start us, length us, event | category | flops | bytes accessed | tf_op | source)
XLA Modules:
  0.0 115.2 jit_solution(12231253136448941318)
XLA Ops:
  0.0 2.2 %dispatch.1 = (bf16[16,2,16,1024]{3,2,1,0:T(8,128)(2,1)S(1)}, s32[1,256]{1,0:T(1,128)S(1)}) custom-call(s32[1,256]{1,0:T(1,128)} %bitcast.13, bf16[256,4096]{1,0:T(8,128)(2,1)} %docs_ref.1), custom_call_target="tpu_custom_call" | custom-call | tf_op jit(solution)/shard_map/dispatch/pallas_call | solution.py:197
  2.2 70.3 %all_to_all.15 = bf16[64,8,1024]{2,1,0:T(8,128)(2,1)S(1)} all-to-all(bf16[64,8,1024]{2,1,0:T(8,128)(2,1)S(1)} %bitcast.10), channel_id=1, replica_groups=mesh['z'=16,'x'=4,'core'=2,'rep'=4] {'z','x'}, dimensions={0} | all-to-all | bytes 2097152 | tf_op jit(solution)/shard_map/all_to_all | solution.py:214
  72.5 6.7 %collective-permute-start = (bf16[512,1024]{1,0:T(8,128)(2,1)S(1)}, bf16[512,1024]{1,0:T(8,128)(2,1)S(1)}, u32[]{:S(2)}, u32[]{:S(2)}) collective-permute-start(bf16[512,1024]{1,0:T(8,128)(2,1)S(1)} %bitcast.8), channel_id=1, source_target_pairs={{0,4},{4,0},{1,5},{5,1},{2,6},{6,2},{3,7},{7,3},{8,12},{12,8},{9,1... | collective-permute-start | bytes 3145736 | tf_op jit(solution)/shard_map/ppermute | solution.py:217
  79.2 1.1 own.1
  80.4 1.1 collective-permute-done.rows_ref
  81.5 1.1 cross.1
  82.6 12.9 %all_to_all.16.parts_ref = f32[4,264,128]{2,1,0:T(8,128)S(1)} all-to-all(f32[4,264,128]{2,1,0:T(8,128)S(1)} %cross.1), channel_id=1, replica_groups=mesh['z'=16,'x'=4,'core'=2,'rep'=4] {'x'}, dimensions={0} | all-to-all | bytes 1081344 | tf_op jit(solution)/shard_map/all_to_all | solution.py:242
  95.4 0.2 best.1
  95.7 18.9 %all_to_all.17 = f32[64,1,128]{2,1,0:T(1,128)S(1)} all-to-all(f32[64,1,128]{2,1,0:T(1,128)S(1)} %bitcast.11), channel_id=1, replica_groups=mesh['z'=16,'x'=4,'core'=2,'rep'=4] {'rep','z'}, dimensions={0} | all-to-all | bytes 65536 | tf_op jit(solution)/shard_map/all_to_all | solution.py:251
  114.5 0.7 collect.1
Async XLA Ops:
  72.5 9.0 %collective-permute-start = (bf16[512,1024]{1,0:T(8,128)(2,1)S(1)}, bf16[512,1024]{1,0:T(8,128)(2,1)S(1)}, u32[]{:S(2)}, u32[]{:S(2)}) collective-permute-start(bf16[512,1024]{1,0:T(8,128)(2,1)S(1)} %bitcast.8), channel_id=1, source_target_pairs={{0,4},{4,0},{1,5},{5,1},{2,6},{6,2},{3,7},{7,3},{8,12},{12,8},{9,1... | collective-permute-start | bytes 3145736 | tf_op jit(solution)/shard_map/ppermute | solution.py:217

commit v11 on v10

--- a/solution.py
+++ b/solution.py
@@ -54,7 +54,9 @@
     slot = cluster * RANKS + rank.astype(jnp.int32)
     slot_ref[...] = slot
     local = slot - lax.axis_index("rep") * (PLANES * PAIR * RANKS)
-    hit = (first >> 1) == local
+    place = ((local >> 2) & 1) * (PLANES * RANKS) + (local >> 3) * RANKS + (local & 3)
+    here = (local >= 0) & (local < PLANES * PAIR * RANKS)
+    hit = (first >> 1) == jnp.where(here, place, -1)
     odd = (first & 1) == 1
     zero, one = f32(0.0), f32(1.0)
     even = jnp.where(hit & jnp.logical_not(odd), one, zero).astype(bf16)
@@ -67,7 +69,7 @@
         merged = merged + jnp.dot(uneven, docs[part, :, HALF:], preferred_element_type=f32)
         marked = jnp.where(live, merged[:, :128], jnp.nan)
         merged = jnp.concatenate([marked, merged[:, 128:]], axis=1)
-        out_ref[:, part, :, :] = merged.astype(bf16).reshape(PLANES, 16, HALF)
+        out_ref[part] = merged.astype(bf16)
 
 
 def multiply(left, right):
@@ -76,8 +78,8 @@
 
 def gather_slots(rows_ref, slots_ref, vacant_ref):
     row = iota((CHUNK, CHUNK), 0)
-    half, lane, rank, plane = row >> 7, (row >> 5) & 3, (row >> 3) & 3, row & 7
-    source = (plane * LANES + lane) * (2 * RANKS) + rank * 2 + half
+    half, lane, rank, plane = row >> 7, (row >> 6) & 1, (row >> 4) & 3, row & 15
+    source = (lane * PLANES + plane) * (2 * RANKS) + rank * 2 + half
     pick = jnp.where(iota((CHUNK, CHUNK), 1) == source, f32(1.0), f32(0.0)).astype(bf16)
     for chunk in range(ROWS // CHUNK):
         span = slice(chunk * CHUNK, (chunk + 1) * CHUNK)
@@ -88,11 +90,10 @@
         rows = jnp.concatenate([clean, rows_ref[span, 128:], flags], axis=1)
         picked = jnp.dot(pick, rows, preferred_element_type=f32)
         slots = picked[:, :HALF].astype(bf16)
-        for lane in range(LANES):
-            top = lane * LOCAL + chunk * 32
-            slots_ref[top : top + 32, :HALF] = slots[lane * 32 : (lane + 1) * 32]
-            slots_ref[top : top + 32, HALF:] = slots[128 + lane * 32 : 128 + (lane + 1) * 32]
-            vacant_ref[top : top + 32, :] = picked[lane * 32 : (lane + 1) * 32, HALF:]
+        at = slice(chunk * 128, (chunk + 1) * 128)
+        slots_ref[at, :HALF] = slots[:128]
+        slots_ref[at, HALF:] = slots[128:]
+        vacant_ref[at, :] = picked[:128, HALF:]
 
 
 def flagged_block(block, vacant):
@@ -140,7 +141,7 @@
 def best_kernel(parts_ref, out_ref):
     row, column = iota((LOCAL, 128), 0), iota((LOCAL, 128), 1)
     spot = column & 7
-    rank = (row >> 3) & 3
+    rank = (row >> 4) & 3
     spread = jnp.zeros((LOCAL, 128), f32)
 
     def scale(squares):
@@ -162,11 +163,8 @@
             best = jnp.maximum(best, jnp.where(allowed, cosine, f32(-1.0)))
         best = jnp.max(best, axis=1, keepdims=True)
         spread = jnp.where(spot == cluster * RANKS + rank, best, spread)
-    planes = []
-    for top in range(0, LOCAL, 32):
-        tiles = [spread[top + k * 8 : top + (k + 1) * 8] for k in range(RANKS)]
-        planes.append((tiles[0] + tiles[1]) + (tiles[2] + tiles[3]))
-    turned = jnp.concatenate(planes, axis=0)
+    ranks = [spread[k * PLANES : (k + 1) * PLANES] for k in range(RANKS)]
+    turned = (ranks[0] + ranks[1]) + (ranks[2] + ranks[3])
     for rep in range(REPS):
         out_ref[rep * PLANES : (rep + 1) * PLANES, :] = turned
 
@@ -199,7 +197,7 @@
         in_specs=[HBM, HBM],
         out_specs=[VMEM, VMEM],
         out_shape=[
-            jax.ShapeDtypeStruct((PLANES, PARTS, 16, HALF), bf16),
+            jax.ShapeDtypeStruct((PARTS, PAIR * PLANES * RANKS * 2, HALF), bf16),
             jax.ShapeDtypeStruct((1, DOCS), jnp.int32),
         ],
         scratch_shapes=[
@@ -212,7 +210,7 @@
         name="dispatch",
     )(labels, pltpu.with_memory_space_constraint(embeddings, pltpu.HBM))
     own_rows = lax.all_to_all(
-        outgoing.reshape(SOURCES, 2 * RANKS, HALF), ("z", "x"), 0, 0, tiled=True
+        outgoing.reshape(SOURCES, 2 * RANKS, HALF), ("x", "z"), 0, 0, tiled=True
     ).reshape(ROWS, HALF)
     other_rows = lax.ppermute(own_rows, "core", [(0, 1), (1, 0)])
     part, slots = pl.pallas_call(

time: 116 us -> 116 us (level)
    all_to_all x1, blocking collectives: 18.9 us -> 20.8 us  [on_device(): lax.all_to_all(best.reshape(REPS * PLANES, 1, 128), ('rep', 'z'), 0, 0, t...]
where the time goes in v11:
time: 116 us
  blocking collectives  103 us (89%)
  starting transfers between devices  6.39 us (6%)
  Pallas kernels  5.3 us (5%)
    all_to_all x1, blocking collectives, on_device(): lax.all_to_all(outgoing.reshape(SOURCES, 2 * RANKS, HALF), ('x', 'z'), 0,...  69.2 us
    all_to_all x1, blocking collectives, on_device(): lax.all_to_all(best.reshape(REPS * PLANES, 1, 128), ('rep', 'z'), 0, 0, t...  20.8 us
    all_to_all x1, blocking collectives, on_device(): products = lax.all_to_all(products, 'x', 0, 0, tiled=True)  13 us
    ppermute x1, starting transfers between devices, on_device(): other_rows = lax.ppermute(own_rows, 'core', [(0, 1), (1, 0)])  6.39 us
  transfers between devices with their start and end apart: 1, of which 1 were waited for; matrix products, arithmetic and copies ran while one was open for 0% of the time, Pallas kernels for 1%

profile of v11, /device:TPU:1, one launch (start us, length us, event | category | flops | bytes accessed | tf_op | source)
XLA Modules:
  0.0 115.9 jit_solution(6646343785414555874)
XLA Ops:
  0.0 2.2 %dispatch.1 = (bf16[2,256,1024]{2,1,0:T(8,128)(2,1)S(1)}, s32[1,256]{1,0:T(1,128)S(1)}) custom-call(s32[1,256]{1,0:T(1,128)} %bitcast.13, bf16[256,4096]{1,0:T(8,128)(2,1)} %docs_ref.1), custom_call_target="tpu_custom_call" | custom-call | tf_op jit(solution)/shard_map/dispatch/pallas_call | solution.py:195
  2.2 69.2 %all_to_all.15 = bf16[64,8,1024]{2,1,0:T(8,128)(2,1)S(1)} all-to-all(bf16[64,8,1024]{2,1,0:T(8,128)(2,1)S(1)} %bitcast.10), channel_id=1, replica_groups=mesh['z'=16,'x'=4,'core'=2,'rep'=4] {'x','z'}, dimensions={0} | all-to-all | bytes 2097152 | tf_op jit(solution)/shard_map/all_to_all | solution.py:212
  71.4 6.4 %collective-permute-start = (bf16[512,1024]{1,0:T(8,128)(2,1)S(1)}, bf16[512,1024]{1,0:T(8,128)(2,1)S(1)}, u32[]{:S(2)}, u32[]{:S(2)}) collective-permute-start(bf16[512,1024]{1,0:T(8,128)(2,1)S(1)} %bitcast.8), channel_id=1, source_target_pairs={{0,4},{4,0},{1,5},{5,1},{2,6},{6,2},{3,7},{7,3},{8,12},{12,8},{9,1... | collective-permute-start | bytes 3145736 | tf_op jit(solution)/shard_map/ppermute | solution.py:215
  77.8 1.1 own.1
  78.9 1.2 collective-permute-done.rows_ref
  80.0 1.1 cross.1
  81.1 13.0 %all_to_all.16.parts_ref = f32[4,264,128]{2,1,0:T(8,128)S(1)} all-to-all(f32[4,264,128]{2,1,0:T(8,128)S(1)} %cross.1), channel_id=1, replica_groups=mesh['z'=16,'x'=4,'core'=2,'rep'=4] {'x'}, dimensions={0} | all-to-all | bytes 1081344 | tf_op jit(solution)/shard_map/all_to_all | solution.py:240
  94.1 0.2 best.1
  94.3 20.8 %all_to_all.17 = f32[64,1,128]{2,1,0:T(1,128)S(1)} all-to-all(f32[64,1,128]{2,1,0:T(1,128)S(1)} %bitcast.11), channel_id=1, replica_groups=mesh['z'=16,'x'=4,'core'=2,'rep'=4] {'rep','z'}, dimensions={0} | all-to-all | bytes 65536 | tf_op jit(solution)/shard_map/all_to_all | solution.py:249
  115.2 0.7 collect.1
Async XLA Ops:
  71.4 8.7 %collective-permute-start = (bf16[512,1024]{1,0:T(8,128)(2,1)S(1)}, bf16[512,1024]{1,0:T(8,128)(2,1)S(1)}, u32[]{:S(2)}, u32[]{:S(2)}) collective-permute-start(bf16[512,1024]{1,0:T(8,128)(2,1)S(1)} %bitcast.8), channel_id=1, source_target_pairs={{0,4},{4,0},{1,5},{5,1},{2,6},{6,2},{3,7},{7,3},{8,12},{12,8},{9,1... | collective-permute-start | bytes 3145736 | tf_op jit(solution)/shard_map/ppermute | solution.py:215

commit v12 on v10

--- a/solution.py
+++ b/solution.py
@@ -32,6 +32,10 @@
     return lax.broadcasted_iota(jnp.int32, shape, dim)
 
 
+def turn_plane(z):
+    return ((z & 7) << 1) + (z >> 3)
+
+
 def dispatch_kernel(
     cluster_ref, docs_ref, out_ref, slot_ref, labels, docs, label_sem, sems
 ):
@@ -54,7 +58,9 @@
     slot = cluster * RANKS + rank.astype(jnp.int32)
     slot_ref[...] = slot
     local = slot - lax.axis_index("rep") * (PLANES * PAIR * RANKS)
-    hit = (first >> 1) == local
+    here = (local >= 0) & (local < PLANES * PAIR * RANKS)
+    place = turn_plane(local >> 3) * (PAIR * RANKS) + (local & 7)
+    hit = (first >> 1) == jnp.where(here, place, -1)
     odd = (first & 1) == 1
     zero, one = f32(0.0), f32(1.0)
     even = jnp.where(hit & jnp.logical_not(odd), one, zero).astype(bf16)
@@ -183,7 +189,9 @@
     chosen = (iota((128, DOCS), 0) & 7) == (slot & 7)
     chosen = jnp.where(chosen, f32(1.0), f32(0.0)).astype(bf16)
     values = jnp.dot(pieces, chosen, preferred_element_type=f32)
-    line = iota((REPS * PLANES, DOCS), 0) == (slot >> 3)
+    home = slot >> 3
+    home = (home & -PLANES) + turn_plane(home & (PLANES - 1))
+    line = iota((REPS * PLANES, DOCS), 0) == home
     out_ref[...] = jnp.sum(jnp.where(line, values, f32(0.0)), axis=0, keepdims=True)
 
 
@@ -212,7 +220,7 @@
         name="dispatch",
     )(labels, pltpu.with_memory_space_constraint(embeddings, pltpu.HBM))
     own_rows = lax.all_to_all(
-        outgoing.reshape(SOURCES, 2 * RANKS, HALF), ("z", "x"), 0, 0, tiled=True
+        outgoing.reshape(SOURCES, 2 * RANKS, HALF), ("zl", "zh", "x"), 0, 0, tiled=True
     ).reshape(ROWS, HALF)
     other_rows = lax.ppermute(own_rows, "core", [(0, 1), (1, 0)])
     part, slots = pl.pallas_call(
@@ -249,7 +257,7 @@
         name="best",
     )(products)
     returned = lax.all_to_all(
-        best.reshape(REPS * PLANES, 1, 128), ("rep", "z"), 0, 0, tiled=True
+        best.reshape(REPS * PLANES, 1, 128), ("rep", "zl", "zh"), 0, 0, tiled=True
     ).reshape(REPS * PLANES, 128)
     out = pl.pallas_call(
         collect_kernel,
@@ -263,8 +271,9 @@
 
 
 def solution(mesh):
-    fine = Mesh(mesh.devices.reshape(PLANES, LANES, 2, REPS), ("z", "x", "core", "rep"))
-    shard = ("z", "x", "core")
+    axes = ("zh", "zl", "x", "core", "rep")
+    fine = Mesh(mesh.devices.reshape(2, PLANES // 2, LANES, 2, REPS), axes)
+    shard = axes[:4]
     return jax.shard_map(
         on_device,
         mesh=fine,

time: 116 us -> 117 us (level)
  blocking collectives: 102 us -> 105 us
  starting transfers between devices: 6.7 us -> 5.02 us
    all_to_all x2, blocking collectives: 89.2 us -> 92.8 us  [the longest x1 71.2 us: on_device(): lax.all_to_all(outgoing.reshape(SOURCES, 2 * RANKS, HALF), ('zl', 'zh', '...]
    ppermute x1, starting transfers between devices: 6.7 us -> 5.02 us  [on_device(): other_rows = lax.ppermute(own_rows, 'core', [(0, 1), (1, 0)])]
where the time goes in v12:
time: 117 us; the launch traced here: 116 us
  blocking collectives  105 us (90%)
  Pallas kernels  5.33 us (5%)
  starting transfers between devices  5.02 us (4%)
    all_to_all x1, blocking collectives, on_device(): lax.all_to_all(outgoing.reshape(SOURCES, 2 * RANKS, HALF), ('zl', 'zh', '...  71.2 us
    all_to_all x1, blocking collectives, on_device(): lax.all_to_all(best.reshape(REPS * PLANES, 1, 128), ('rep', 'zl', 'zh'),...  21.5 us
    all_to_all x1, blocking collectives, on_device(): products = lax.all_to_all(products, 'x', 0, 0, tiled=True)  11.8 us
    ppermute x1, starting transfers between devices, on_device(): other_rows = lax.ppermute(own_rows, 'core', [(0, 1), (1, 0)])  5.02 us
  transfers between devices with their start and end apart: 1, of which 1 were waited for; matrix products, arithmetic and copies ran while one was open for 0% of the time, Pallas kernels for 1%

profile of v12, /device:TPU:1, one launch (start us, length us, event | category | flops | bytes accessed | tf_op | source)
XLA Modules:
  0.0 116.0 jit_solution(5333198970171049360)
XLA Ops:
  0.0 2.2 %dispatch.1 = (bf16[16,2,16,1024]{3,2,1,0:T(8,128)(2,1)S(1)}, s32[1,256]{1,0:T(1,128)S(1)}) custom-call(s32[1,256]{1,0:T(1,128)} %bitcast.13, bf16[256,4096]{1,0:T(8,128)(2,1)} %docs_ref.1), custom_call_target="tpu_custom_call" | custom-call | tf_op jit(solution)/shard_map/dispatch/pallas_call | solution.py:205
  2.2 71.2 %all_to_all.15 = bf16[64,8,1024]{2,1,0:T(8,128)(2,1)S(1)} all-to-all(bf16[64,8,1024]{2,1,0:T(8,128)(2,1)S(1)} %bitcast.10), channel_id=1, replica_groups=mesh['zh'=2,'zl'=8,'x'=4,'core'=2,'rep'=4] {'zl','zh','x'}, dimensions={0} | all-to-all | bytes 2097152 | tf_op jit(solution)/shard_map/all_to_all | solution.py:222
  73.4 5.0 %collective-permute-start = (bf16[512,1024]{1,0:T(8,128)(2,1)S(1)}, bf16[512,1024]{1,0:T(8,128)(2,1)S(1)}, u32[]{:S(2)}, u32[]{:S(2)}) collective-permute-start(bf16[512,1024]{1,0:T(8,128)(2,1)S(1)} %bitcast.8), channel_id=1, source_target_pairs={{0,4},{4,0},{1,5},{5,1},{2,6},{6,2},{3,7},{7,3},{8,12},{12,8},{9,1... | collective-permute-start | bytes 3145736 | tf_op jit(solution)/shard_map/ppermute | solution.py:225
  78.4 1.1 own.1
  79.6 1.1 collective-permute-done.rows_ref
  80.7 1.1 cross.1
  81.8 11.8 %all_to_all.16.parts_ref = f32[4,264,128]{2,1,0:T(8,128)S(1)} all-to-all(f32[4,264,128]{2,1,0:T(8,128)S(1)} %cross.1), channel_id=1, replica_groups=mesh['zh'=2,'zl'=8,'x'=4,'core'=2,'rep'=4] {'x'}, dimensions={0} | all-to-all | bytes 1081344 | tf_op jit(solution)/shard_map/all_to_all | solution.py:250
  93.6 0.2 best.1
  93.8 21.5 %all_to_all.17 = f32[64,1,128]{2,1,0:T(1,128)S(1)} all-to-all(f32[64,1,128]{2,1,0:T(1,128)S(1)} %bitcast.11), channel_id=1, replica_groups=mesh['zh'=2,'zl'=8,'x'=4,'core'=2,'rep'=4] {'rep','zl','zh'}, dimensions={0} | all-to-all | bytes 65536 | tf_op jit(solution)/shard_map/all_to_all | solution.py:259
  115.3 0.7 collect.1
Async XLA Ops:
  73.4 7.3 %collective-permute-start = (bf16[512,1024]{1,0:T(8,128)(2,1)S(1)}, bf16[512,1024]{1,0:T(8,128)(2,1)S(1)}, u32[]{:S(2)}, u32[]{:S(2)}) collective-permute-start(bf16[512,1024]{1,0:T(8,128)(2,1)S(1)} %bitcast.8), channel_id=1, source_target_pairs={{0,4},{4,0},{1,5},{5,1},{2,6},{6,2},{3,7},{7,3},{8,12},{12,8},{9,1... | collective-permute-start | bytes 3145736 | tf_op jit(solution)/shard_map/ppermute | solution.py:225

commit v13 on v10

--- a/solution.py
+++ b/solution.py
@@ -168,7 +168,7 @@
         planes.append((tiles[0] + tiles[1]) + (tiles[2] + tiles[3]))
     turned = jnp.concatenate(planes, axis=0)
     for rep in range(REPS):
-        out_ref[rep * PLANES : (rep + 1) * PLANES, :] = turned
+        out_ref[:, rep, :] = turned
 
 
 def collect_kernel(slot_ref, best_ref, out_ref):
@@ -183,7 +183,9 @@
     chosen = (iota((128, DOCS), 0) & 7) == (slot & 7)
     chosen = jnp.where(chosen, f32(1.0), f32(0.0)).astype(bf16)
     values = jnp.dot(pieces, chosen, preferred_element_type=f32)
-    line = iota((REPS * PLANES, DOCS), 0) == (slot >> 3)
+    home = slot >> 3
+    home = (home & (PLANES - 1)) * REPS + home // PLANES
+    line = iota((REPS * PLANES, DOCS), 0) == home
     out_ref[...] = jnp.sum(jnp.where(line, values, f32(0.0)), axis=0, keepdims=True)
 
 
@@ -244,12 +246,12 @@
         best_kernel,
         in_specs=[VMEM],
         out_specs=VMEM,
-        out_shape=jax.ShapeDtypeStruct((REPS * PLANES, 128), f32),
+        out_shape=jax.ShapeDtypeStruct((PLANES, REPS, 128), f32),
         compiler_params=PARAMS,
         name="best",
     )(products)
     returned = lax.all_to_all(
-        best.reshape(REPS * PLANES, 1, 128), ("rep", "z"), 0, 0, tiled=True
+        best.reshape(REPS * PLANES, 1, 128), ("z", "rep"), 0, 0, tiled=True
     ).reshape(REPS * PLANES, 128)
     out = pl.pallas_call(
         collect_kernel,

time: 116 us -> 116 us (level)
  no operation moved by 1% of the time
where the time goes in v13:
time: 116 us; the launch traced here: 115 us
  blocking collectives  102 us (88%)
  starting transfers between devices  6.7 us (6%)
  Pallas kernels  5.34 us (5%)
    all_to_all x1, blocking collectives, on_device(): lax.all_to_all(outgoing.reshape(SOURCES, 2 * RANKS, HALF), ('z', 'x'), 0,...  70.3 us
    all_to_all x1, blocking collectives, on_device(): lax.all_to_all(best.reshape(REPS * PLANES, 1, 128), ('z', 'rep'), 0, 0, t...  19 us
    all_to_all x1, blocking collectives, on_device(): products = lax.all_to_all(products, 'x', 0, 0, tiled=True)  12.9 us
    ppermute x1, starting transfers between devices, on_device(): other_rows = lax.ppermute(own_rows, 'core', [(0, 1), (1, 0)])  6.7 us
  transfers between devices with their start and end apart: 1, of which 1 were waited for; matrix products, arithmetic and copies ran while one was open for 0% of the time, Pallas kernels for 1%

profile of v13, /device:TPU:1, one launch (start us, length us, event | category | flops | bytes accessed | tf_op | source)
XLA Modules:
  0.0 115.4 jit_solution(6512925352008065872)
XLA Ops:
  0.0 2.2 %dispatch.1 = (bf16[16,2,16,1024]{3,2,1,0:T(8,128)(2,1)S(1)}, s32[1,256]{1,0:T(1,128)S(1)}) custom-call(s32[1,256]{1,0:T(1,128)} %bitcast.13, bf16[256,4096]{1,0:T(8,128)(2,1)} %docs_ref.1), custom_call_target="tpu_custom_call" | custom-call | tf_op jit(solution)/shard_map/dispatch/pallas_call | solution.py:199
  2.2 70.3 %all_to_all.15 = bf16[64,8,1024]{2,1,0:T(8,128)(2,1)S(1)} all-to-all(bf16[64,8,1024]{2,1,0:T(8,128)(2,1)S(1)} %bitcast.10), channel_id=1, replica_groups=mesh['z'=16,'x'=4,'core'=2,'rep'=4] {'z','x'}, dimensions={0} | all-to-all | bytes 2097152 | tf_op jit(solution)/shard_map/all_to_all | solution.py:216
  72.5 6.7 %collective-permute-start = (bf16[512,1024]{1,0:T(8,128)(2,1)S(1)}, bf16[512,1024]{1,0:T(8,128)(2,1)S(1)}, u32[]{:S(2)}, u32[]{:S(2)}) collective-permute-start(bf16[512,1024]{1,0:T(8,128)(2,1)S(1)} %bitcast.8), channel_id=1, source_target_pairs={{0,4},{4,0},{1,5},{5,1},{2,6},{6,2},{3,7},{7,3},{8,12},{12,8},{9,1... | collective-permute-start | bytes 3145736 | tf_op jit(solution)/shard_map/ppermute | solution.py:219
  79.2 1.1 own.1
  80.4 1.1 collective-permute-done.rows_ref
  81.5 1.1 cross.1
  82.6 12.9 %all_to_all.16.parts_ref = f32[4,264,128]{2,1,0:T(8,128)S(1)} all-to-all(f32[4,264,128]{2,1,0:T(8,128)S(1)} %cross.1), channel_id=1, replica_groups=mesh['z'=16,'x'=4,'core'=2,'rep'=4] {'x'}, dimensions={0} | all-to-all | bytes 1081344 | tf_op jit(solution)/shard_map/all_to_all | solution.py:244
  95.4 0.2 best.1
  95.7 19.0 %all_to_all.17 = f32[64,1,128]{2,1,0:T(1,128)S(1)} all-to-all(f32[64,1,128]{2,1,0:T(1,128)S(1)} %bitcast.11), channel_id=1, replica_groups=mesh['z'=16,'x'=4,'core'=2,'rep'=4] {'z','rep'}, dimensions={0} | all-to-all | bytes 65536 | tf_op jit(solution)/shard_map/all_to_all | solution.py:253
  114.7 0.7 collect.1
Async XLA Ops:
  72.5 9.0 %collective-permute-start = (bf16[512,1024]{1,0:T(8,128)(2,1)S(1)}, bf16[512,1024]{1,0:T(8,128)(2,1)S(1)}, u32[]{:S(2)}, u32[]{:S(2)}) collective-permute-start(bf16[512,1024]{1,0:T(8,128)(2,1)S(1)} %bitcast.8), channel_id=1, source_target_pairs={{0,4},{4,0},{1,5},{5,1},{2,6},{6,2},{3,7},{7,3},{8,12},{12,8},{9,1... | collective-permute-start | bytes 3145736 | tf_op jit(solution)/shard_map/ppermute | solution.py:219

commit v14 on v11

--- a/solution.py
+++ b/solution.py
@@ -166,7 +166,7 @@
     ranks = [spread[k * PLANES : (k + 1) * PLANES] for k in range(RANKS)]
     turned = (ranks[0] + ranks[1]) + (ranks[2] + ranks[3])
     for rep in range(REPS):
-        out_ref[rep * PLANES : (rep + 1) * PLANES, :] = turned
+        out_ref[:, rep, :] = turned
 
 
 def collect_kernel(slot_ref, best_ref, out_ref):
@@ -181,7 +181,9 @@
     chosen = (iota((128, DOCS), 0) & 7) == (slot & 7)
     chosen = jnp.where(chosen, f32(1.0), f32(0.0)).astype(bf16)
     values = jnp.dot(pieces, chosen, preferred_element_type=f32)
-    line = iota((REPS * PLANES, DOCS), 0) == (slot >> 3)
+    home = slot >> 3
+    home = (home & (PLANES - 1)) * REPS + home // PLANES
+    line = iota((REPS * PLANES, DOCS), 0) == home
     out_ref[...] = jnp.sum(jnp.where(line, values, f32(0.0)), axis=0, keepdims=True)
 
 
@@ -242,12 +244,12 @@
         best_kernel,
         in_specs=[VMEM],
         out_specs=VMEM,
-        out_shape=jax.ShapeDtypeStruct((REPS * PLANES, 128), f32),
+        out_shape=jax.ShapeDtypeStruct((PLANES, REPS, 128), f32),
         compiler_params=PARAMS,
         name="best",
     )(products)
     returned = lax.all_to_all(
-        best.reshape(REPS * PLANES, 1, 128), ("rep", "z"), 0, 0, tiled=True
+        best.reshape(REPS * PLANES, 1, 128), ("z", "rep"), 0, 0, tiled=True
     ).reshape(REPS * PLANES, 128)
     out = pl.pallas_call(
         collect_kernel,

time: 116 us -> 117 us (level)
  no operation moved by 1% of the time
where the time goes in v14:
time: 117 us; the launch traced here: 116 us
  blocking collectives  103 us (88%)
  starting transfers between devices  6.39 us (5%)
  Pallas kernels  5.32 us (5%)
    all_to_all x1, blocking collectives, on_device(): lax.all_to_all(outgoing.reshape(SOURCES, 2 * RANKS, HALF), ('x', 'z'), 0,...  69.2 us
    all_to_all x1, blocking collectives, on_device(): lax.all_to_all(best.reshape(REPS * PLANES, 1, 128), ('z', 'rep'), 0, 0, t...  21 us
    all_to_all x1, blocking collectives, on_device(): products = lax.all_to_all(products, 'x', 0, 0, tiled=True)  13 us
    ppermute x1, starting transfers between devices, on_device(): other_rows = lax.ppermute(own_rows, 'core', [(0, 1), (1, 0)])  6.39 us
  transfers between devices with their start and end apart: 1, of which 1 were waited for; matrix products, arithmetic and copies ran while one was open for 0% of the time, Pallas kernels for 1%

profile of v14, /device:TPU:1, one launch (start us, length us, event | category | flops | bytes accessed | tf_op | source)
XLA Modules:
  0.0 116.1 jit_solution(10656620748863949808)
XLA Ops:
  0.0 2.2 %dispatch.1 = (bf16[2,256,1024]{2,1,0:T(8,128)(2,1)S(1)}, s32[1,256]{1,0:T(1,128)S(1)}) custom-call(s32[1,256]{1,0:T(1,128)} %bitcast.13, bf16[256,4096]{1,0:T(8,128)(2,1)} %docs_ref.1), custom_call_target="tpu_custom_call" | custom-call | tf_op jit(solution)/shard_map/dispatch/pallas_call | solution.py:197
  2.2 69.2 %all_to_all.15 = bf16[64,8,1024]{2,1,0:T(8,128)(2,1)S(1)} all-to-all(bf16[64,8,1024]{2,1,0:T(8,128)(2,1)S(1)} %bitcast.10), channel_id=1, replica_groups=mesh['z'=16,'x'=4,'core'=2,'rep'=4] {'x','z'}, dimensions={0} | all-to-all | bytes 2097152 | tf_op jit(solution)/shard_map/all_to_all | solution.py:214
  71.4 6.4 %collective-permute-start = (bf16[512,1024]{1,0:T(8,128)(2,1)S(1)}, bf16[512,1024]{1,0:T(8,128)(2,1)S(1)}, u32[]{:S(2)}, u32[]{:S(2)}) collective-permute-start(bf16[512,1024]{1,0:T(8,128)(2,1)S(1)} %bitcast.8), channel_id=1, source_target_pairs={{0,4},{4,0},{1,5},{5,1},{2,6},{6,2},{3,7},{7,3},{8,12},{12,8},{9,1... | collective-permute-start | bytes 3145736 | tf_op jit(solution)/shard_map/ppermute | solution.py:217
  77.8 1.1 own.1
  78.9 1.2 collective-permute-done.rows_ref
  80.0 1.1 cross.1
  81.1 13.0 %all_to_all.16.parts_ref = f32[4,264,128]{2,1,0:T(8,128)S(1)} all-to-all(f32[4,264,128]{2,1,0:T(8,128)S(1)} %cross.1), channel_id=1, replica_groups=mesh['z'=16,'x'=4,'core'=2,'rep'=4] {'x'}, dimensions={0} | all-to-all | bytes 1081344 | tf_op jit(solution)/shard_map/all_to_all | solution.py:242
  94.1 0.3 best.1
  94.4 21.0 %all_to_all.17 = f32[64,1,128]{2,1,0:T(1,128)S(1)} all-to-all(f32[64,1,128]{2,1,0:T(1,128)S(1)} %bitcast.11), channel_id=1, replica_groups=mesh['z'=16,'x'=4,'core'=2,'rep'=4] {'z','rep'}, dimensions={0} | all-to-all | bytes 65536 | tf_op jit(solution)/shard_map/all_to_all | solution.py:251
  115.3 0.7 collect.1
Async XLA Ops:
  71.4 8.7 %collective-permute-start = (bf16[512,1024]{1,0:T(8,128)(2,1)S(1)}, bf16[512,1024]{1,0:T(8,128)(2,1)S(1)}, u32[]{:S(2)}, u32[]{:S(2)}) collective-permute-start(bf16[512,1024]{1,0:T(8,128)(2,1)S(1)} %bitcast.8), channel_id=1, source_target_pairs={{0,4},{4,0},{1,5},{5,1},{2,6},{6,2},{3,7},{7,3},{8,12},{12,8},{9,1... | collective-permute-start | bytes 3145736 | tf_op jit(solution)/shard_map/ppermute | solution.py:217

commit v15 on v9

--- a/solution.py
+++ b/solution.py
@@ -45,7 +45,7 @@
     for part in range(PARTS):
         columns = slice(part * SHARE, (part + 1) * SHARE)
         fetch = pltpu.make_async_copy(docs_ref.at[:, columns], docs.at[part], sems.at[part])
-        fetch.start()
+        fetch.start(priority=1)
         fetches.append(fetch)
     fetch_labels.wait()
     cluster = labels[...]
@@ -169,7 +169,8 @@
         lines.append((parts[0] + parts[1]) + (parts[2] + parts[3]))
     turned = jnp.concatenate(lines, axis=0)
     for rep in range(REPS):
-        out_ref[rep * PAIR * PLANES : (rep + 1) * PAIR * PLANES, :] = turned
+        for xh in range(2):
+            out_ref[rep, :, xh, :] = turned[xh * PLANES : (xh + 1) * PLANES]
 
 
 def collect_kernel(slot_ref, best_ref, out_ref):
@@ -184,9 +185,7 @@
     chosen = (iota((128, DOCS), 0) & 3) == (slot & 3)
     chosen = jnp.where(chosen, f32(1.0), f32(0.0)).astype(bf16)
     values = jnp.dot(pieces, chosen, preferred_element_type=f32)
-    cluster = slot >> 2
-    line = (cluster >> 5) * (PAIR * PLANES) + (cluster & 1) * PLANES + ((cluster & 31) >> 1)
-    hit = iota((RETURNS, DOCS), 0) == line
+    hit = iota((RETURNS, DOCS), 0) == (slot >> 2)
     out_ref[...] = jnp.sum(jnp.where(hit, values, f32(0.0)), axis=0, keepdims=True)
 
 
@@ -254,12 +253,12 @@
         best_kernel,
         in_specs=[VMEM, VMEM, VMEM, VMEM],
         out_specs=VMEM,
-        out_shape=jax.ShapeDtypeStruct((RETURNS, 128), f32),
+        out_shape=jax.ShapeDtypeStruct((REPS, PLANES, 2, 128), f32),
         compiler_params=PARAMS,
         name="best",
     )(own_keep, own_sent, cross_keep, cross_sent)
     returned = lax.all_to_all(
-        best.reshape(RETURNS, 1, 128), ("rep", "xh", "z"), 0, 0, tiled=True
+        best.reshape(RETURNS, 1, 128), ("rep", "z", "xh"), 0, 0, tiled=True
     ).reshape(RETURNS, 128)
     out = pl.pallas_call(
         collect_kernel,

time: 117 us -> 117 us (level)
  no operation moved by 1% of the time
where the time goes in v15:
time: 117 us
  blocking collectives  94.8 us (81%)
  starting transfers between devices  11.8 us (10%)
  Pallas kernels  5.47 us (5%)
  waiting for transfers between devices  4.6 us (4%)
    all_to_all x1, blocking collectives, on_device(): lax.all_to_all(outgoing.reshape(SOURCES, 2 * RANKS, HALF), ('z', 'xl', 'x...  70.5 us
    all_to_all x1, blocking collectives, on_device(): lax.all_to_all(best.reshape(RETURNS, 1, 128), ('rep', 'z', 'xh'), 0, 0, t...  24.3 us
    ppermute x1, starting transfers between devices, on_device(): other_rows = lax.ppermute(own_rows, 'core', swap)  6.55 us
    ppermute x1, waiting for transfers between devices, on_device(): cross_sent = lax.ppermute(cross_send, 'xl', swap)  3.97 us
    ppermute x1, starting transfers between devices, on_device(): own_sent = lax.ppermute(own_send, 'xl', swap)  3.1 us
  transfers between devices with their start and end apart: 3, of which 2 were waited for; matrix products, arithmetic and copies ran while one was open for 0% of the time, Pallas kernels for 2%

profile of v15, /device:TPU:1, one launch (start us, length us, event | category | flops | bytes accessed | tf_op | source)
XLA Modules:
  0.0 116.7 jit_solution(15962706914689218236)
XLA Ops:
  0.0 2.2 %dispatch.1 = (bf16[16,2,16,1024]{3,2,1,0:T(8,128)(2,1)S(1)}, s32[1,256]{1,0:T(1,128)S(1)}) custom-call(s32[1,256]{1,0:T(1,128)} %bitcast.13, bf16[256,4096]{1,0:T(8,128)(2,1)} %docs_ref.1), custom_call_target="tpu_custom_call" | custom-call | tf_op jit(solution)/shard_map/dispatch/pallas_call | solution.py:199
  2.2 70.5 %all_to_all.10 = bf16[64,8,1024]{2,1,0:T(8,128)(2,1)S(1)} all-to-all(bf16[64,8,1024]{2,1,0:T(8,128)(2,1)S(1)} %bitcast.10), channel_id=1, replica_groups=mesh['z'=16,'xh'=2,'xl'=2,'core'=2,'rep'=4] {'z','xl','xh'}, dimensions={0} | all-to-all | bytes 2097152 | tf_op jit(solution)/shard_map/all_to_all | solution.py:216
  72.7 6.6 %collective-permute-start.1 = (bf16[512,1024]{1,0:T(8,128)(2,1)S(1)}, bf16[512,1024]{1,0:T(8,128)(2,1)S(1)}, u32[]{:S(2)}, u32[]{:S(2)}) collective-permute-start(bf16[512,1024]{1,0:T(8,128)(2,1)S(1)} %bitcast.8), channel_id=1, source_target_pairs={{0,4},{4,0},{1,5},{5,1},{2,6},{6,2},{3,7},{7,3},{8,12},{12,8},{9,1... | collective-permute-start | bytes 3145736 | tf_op jit(solution)/shard_map/ppermute | solution.py:220
  79.2 1.2 %own.1 = (f32[264,128]{1,0:T(8,128)S(1)}, f32[264,128]{1,0:T(8,128)S(1)}, bf16[256,2048]{1,0:T(8,128)(2,1)S(1)}) custom-call(bf16[512,1024]{1,0:T(8,128)(2,1)S(1)} %bitcast.9), custom_call_target="tpu_custom_call" | custom-call | flops 536870912 | bytes 4194304 | tf_op jit(solution)/shard_map/own/pallas_call | solution.py:222
  80.4 3.1 %collective-permute-start = (f32[264,128]{1,0:T(8,128)S(1)}, f32[264,128]{1,0:T(8,128)S(1)}, u32[]{:S(2)}, u32[]{:S(2)}) collective-permute-start(f32[264,128]{1,0:T(8,128)S(1)} %get-tuple-element.15), channel_id=1, source_target_pairs={{0,8},{8,0},{1,9},{9,1},{2,10},{10,2},{3,11},{11,3},{4,12},{12,4},... | collective-permute-start | bytes 405512 | tf_op jit(solution)/shard_map/ppermute | solution.py:234
  83.5 0.0 collective-permute-done.1.rows_ref
  83.5 1.2 cross.1
  84.7 2.2 %collective-permute-start.2 = (f32[264,128]{1,0:T(8,128)S(1)}, f32[264,128]{1,0:T(8,128)S(1)}, u32[]{:S(2)}, u32[]{:S(2)}) collective-permute-start(f32[264,128]{1,0:T(8,128)S(1)} %get-tuple-element.18), channel_id=1, source_target_pairs={{0,8},{8,0},{1,9},{9,1},{2,10},{10,2},{3,11},{11,3},{4,12},{12,4},... | collective-permute-start | bytes 405512 | tf_op jit(solution)/shard_map/ppermute | solution.py:251
  86.9 0.6 collective-permute-done.own_sent
  87.5 4.0 %collective-permute-done.2.cross_sent = f32[264,128]{1,0:T(8,128)S(1)} collective-permute-done((f32[264,128]{1,0:T(8,128)S(1)}, f32[264,128]{1,0:T(8,128)S(1)}, u32[]{:S(2)}, u32[]{:S(2)}) %collective-permute-start.2) | collective-permute-done | bytes 135200 | tf_op jit(solution)/shard_map/ppermute | solution.py:251
  91.5 0.2 best.1
  91.7 24.3 %all_to_all.11 = f32[128,1,128]{2,1,0:T(1,128)S(1)} all-to-all(f32[128,1,128]{2,1,0:T(1,128)S(1)} %bitcast.11), channel_id=1, replica_groups=mesh['z'=16,'xh'=2,'xl'=2,'core'=2,'rep'=4] {'rep','z','xh'}, dimensions={0} | all-to-all | bytes 131072 | tf_op jit(solution)/shard_map/all_to_all | solution.py:260
  116.0 0.7 collect.1
Async XLA Ops:
  72.7 10.9 %collective-permute-start.1 = (bf16[512,1024]{1,0:T(8,128)(2,1)S(1)}, bf16[512,1024]{1,0:T(8,128)(2,1)S(1)}, u32[]{:S(2)}, u32[]{:S(2)}) collective-permute-start(bf16[512,1024]{1,0:T(8,128)(2,1)S(1)} %bitcast.8), channel_id=1, source_target_pairs={{0,4},{4,0},{1,5},{5,1},{2,6},{6,2},{3,7},{7,3},{8,12},{12,8},{9,1... | collective-permute-start | bytes 3145736 | tf_op jit(solution)/shard_map/ppermute | solution.py:220
  80.4 7.1 %collective-permute-start = (f32[264,128]{1,0:T(8,128)S(1)}, f32[264,128]{1,0:T(8,128)S(1)}, u32[]{:S(2)}, u32[]{:S(2)}) collective-permute-start(f32[264,128]{1,0:T(8,128)S(1)} %get-tuple-element.15), channel_id=1, source_target_pairs={{0,8},{8,0},{1,9},{9,1},{2,10},{10,2},{3,11},{11,3},{4,12},{12,4},... | collective-permute-start | bytes 405512 | tf_op jit(solution)/shard_map/ppermute | solution.py:234
  84.7 6.8 %collective-permute-start.2 = (f32[264,128]{1,0:T(8,128)S(1)}, f32[264,128]{1,0:T(8,128)S(1)}, u32[]{:S(2)}, u32[]{:S(2)}) collective-permute-start(f32[264,128]{1,0:T(8,128)S(1)} %get-tuple-element.18), channel_id=1, source_target_pairs={{0,8},{8,0},{1,9},{9,1},{2,10},{10,2},{3,11},{11,3},{4,12},{12,4},... | collective-permute-start | bytes 405512 | tf_op jit(solution)/shard_map/ppermute | solution.py:251

commit v16 on v13

--- a/solution.py
+++ b/solution.py
@@ -139,6 +139,7 @@
 
 def best_kernel(parts_ref, out_ref):
     row, column = iota((LOCAL, 128), 0), iota((LOCAL, 128), 1)
+    lane = lax.axis_index("xl") * 2 + lax.axis_index("xh")
     spot = column & 7
     rank = (row >> 3) & 3
     spread = jnp.zeros((LOCAL, 128), f32)
@@ -150,7 +151,7 @@
         total = parts_ref[cluster] + parts_ref[PAIR + cluster]
         tiles = [total[t * LOCAL : (t + 1) * LOCAL] for t in range(4)]
         mates = [scale(total[4 * LOCAL + t : 4 * LOCAL + t + 1]) for t in range(4)]
-        same = [column + t * 128 == row + lax.axis_index("x") * LOCAL for t in range(2)]
+        same = [column + t * 128 == row + lane * LOCAL for t in range(2)]
         squares = jnp.where(same[0], tiles[0], f32(0.0)) + jnp.where(same[1], tiles[1], f32(0.0))
         own = scale(jnp.sum(squares, axis=1, keepdims=True))
         best = jnp.full((LOCAL, 128), -1.0, f32)
@@ -214,7 +215,7 @@
         name="dispatch",
     )(labels, pltpu.with_memory_space_constraint(embeddings, pltpu.HBM))
     own_rows = lax.all_to_all(
-        outgoing.reshape(SOURCES, 2 * RANKS, HALF), ("z", "x"), 0, 0, tiled=True
+        outgoing.reshape(SOURCES, 2 * RANKS, HALF), ("z", "xl", "xh"), 0, 0, tiled=True
     ).reshape(ROWS, HALF)
     other_rows = lax.ppermute(own_rows, "core", [(0, 1), (1, 0)])
     part, slots = pl.pallas_call(
@@ -241,7 +242,7 @@
         compiler_params=PARAMS,
         name="cross",
     )(part, slots, other_rows)
-    products = lax.all_to_all(products, "x", 0, 0, tiled=True)
+    products = lax.all_to_all(products, ("xl", "xh"), 0, 0, tiled=True)
     best = pl.pallas_call(
         best_kernel,
         in_specs=[VMEM],
@@ -265,8 +266,9 @@
 
 
 def solution(mesh):
-    fine = Mesh(mesh.devices.reshape(PLANES, LANES, 2, REPS), ("z", "x", "core", "rep"))
-    shard = ("z", "x", "core")
+    axes = ("z", "xh", "xl", "core", "rep")
+    fine = Mesh(mesh.devices.reshape(PLANES, 2, 2, 2, REPS), axes)
+    shard = axes[:4]
     return jax.shard_map(
         on_device,
         mesh=fine,

time: 116 us -> 116 us (level)
  no operation moved by 1% of the time
where the time goes in v16:
time: 116 us
  blocking collectives  103 us (89%)
  starting transfers between devices  6.55 us (6%)
  Pallas kernels  5.34 us (5%)
    all_to_all x1, blocking collectives, on_device(): lax.all_to_all(outgoing.reshape(SOURCES, 2 * RANKS, HALF), ('z', 'xl', 'x...  70.5 us
    all_to_all x1, blocking collectives, on_device(): lax.all_to_all(best.reshape(REPS * PLANES, 1, 128), ('z', 'rep'), 0, 0, t...  19.3 us
    all_to_all x1, blocking collectives, on_device(): products = lax.all_to_all(products, ('xl', 'xh'), 0, 0, tiled=True)  12.7 us
    ppermute x1, starting transfers between devices, on_device(): other_rows = lax.ppermute(own_rows, 'core', [(0, 1), (1, 0)])  6.55 us
  transfers between devices with their start and end apart: 1, of which 1 were waited for; matrix products, arithmetic and copies ran while one was open for 0% of the time, Pallas kernels for 1%

profile of v16, /device:TPU:1, one launch (start us, length us, event | category | flops | bytes accessed | tf_op | source)
XLA Modules:
  0.0 115.6 jit_solution(5053813819375234317)
XLA Ops:
  0.0 2.2 %dispatch.1 = (bf16[16,2,16,1024]{3,2,1,0:T(8,128)(2,1)S(1)}, s32[1,256]{1,0:T(1,128)S(1)}) custom-call(s32[1,256]{1,0:T(1,128)} %bitcast.13, bf16[256,4096]{1,0:T(8,128)(2,1)} %docs_ref.1), custom_call_target="tpu_custom_call" | custom-call | tf_op jit(solution)/shard_map/dispatch/pallas_call | solution.py:200
  2.2 70.5 %all_to_all.15 = bf16[64,8,1024]{2,1,0:T(8,128)(2,1)S(1)} all-to-all(bf16[64,8,1024]{2,1,0:T(8,128)(2,1)S(1)} %bitcast.10), channel_id=1, replica_groups=mesh['z'=16,'xh'=2,'xl'=2,'core'=2,'rep'=4] {'z','xl','xh'}, dimensions={0} | all-to-all | bytes 2097152 | tf_op jit(solution)/shard_map/all_to_all | solution.py:217
  72.7 6.6 %collective-permute-start = (bf16[512,1024]{1,0:T(8,128)(2,1)S(1)}, bf16[512,1024]{1,0:T(8,128)(2,1)S(1)}, u32[]{:S(2)}, u32[]{:S(2)}) collective-permute-start(bf16[512,1024]{1,0:T(8,128)(2,1)S(1)} %bitcast.8), channel_id=1, source_target_pairs={{0,4},{4,0},{1,5},{5,1},{2,6},{6,2},{3,7},{7,3},{8,12},{12,8},{9,1... | collective-permute-start | bytes 3145736 | tf_op jit(solution)/shard_map/ppermute | solution.py:220
  79.2 1.1 own.1
  80.4 1.1 collective-permute-done.rows_ref
  81.5 1.1 cross.1
  82.6 12.7 %all_to_all.16.parts_ref = f32[4,264,128]{2,1,0:T(8,128)S(1)} all-to-all(f32[4,264,128]{2,1,0:T(8,128)S(1)} %cross.1), channel_id=1, replica_groups=mesh['z'=16,'xh'=2,'xl'=2,'core'=2,'rep'=4] {'xl','xh'}, dimensions={0} | all-to-all | bytes 1081344 | tf_op jit(solution)/shard_map/all_to_all | solution.py:245
  95.3 0.2 best.1
  95.6 19.3 %all_to_all.17 = f32[64,1,128]{2,1,0:T(1,128)S(1)} all-to-all(f32[64,1,128]{2,1,0:T(1,128)S(1)} %bitcast.11), channel_id=1, replica_groups=mesh['z'=16,'xh'=2,'xl'=2,'core'=2,'rep'=4] {'z','rep'}, dimensions={0} | all-to-all | bytes 65536 | tf_op jit(solution)/shard_map/all_to_all | solution.py:254
  114.9 0.7 collect.1
Async XLA Ops:
  72.7 8.8 %collective-permute-start = (bf16[512,1024]{1,0:T(8,128)(2,1)S(1)}, bf16[512,1024]{1,0:T(8,128)(2,1)S(1)}, u32[]{:S(2)}, u32[]{:S(2)}) collective-permute-start(bf16[512,1024]{1,0:T(8,128)(2,1)S(1)} %bitcast.8), channel_id=1, source_target_pairs={{0,4},{4,0},{1,5},{5,1},{2,6},{6,2},{3,7},{7,3},{8,12},{12,8},{9,1... | collective-permute-start | bytes 3145736 | tf_op jit(solution)/shard_map/ppermute | solution.py:220
